TPU v7x, 32 devices: a whole 2x2x4 slice. The times are simulated.
32 devices in a mesh: ctx: 16 (over z, y, x), fsdp: 2 (over core).
Axes of the slice: x: 2, y: 2, z: 4, core: 2. Of those that a mesh axis runs over, the one named last changes fastest.
Arguments:
- tokens_in: bfloat16 [2, 2048, 1536], P('fsdp', 'ctx'), may hold values from -6 to 6
- deal_table: int32 [2, 32], P('fsdp'), may hold values from 0 to 31, as said below
- cont_id: int32 [2, 2048], P('fsdp', 'ctx'), may hold values from 0 to 1, as said below
- position: int32 [2, 2048], P('fsdp', 'ctx'), may hold values from 0 to 2047, as said below
- qkv_weight: bfloat16 [1536, 2048], P(('ctx', 'fsdp')), may hold values from -0.15625 to 0.15625
- qkv_bias: bfloat16 [2048], P(('ctx', 'fsdp')), may hold values from -3 to 3
- out_weight: bfloat16 [1536, 1536], P(('ctx', 'fsdp')), may hold values from -1.75 to 1.75
- attn_gain: bfloat16 [1536], P(('ctx', 'fsdp')), may hold values from 0.5 to 1.5
- mlp_gain: bfloat16 [1536], P(('ctx', 'fsdp')), may hold values from 0.5 to 1.5
- gate_weight: bfloat16 [1536, 8960], P(('ctx', 'fsdp')), may hold values from -0.15625 to 0.15625
- up_weight: bfloat16 [1536, 8960], P(('ctx', 'fsdp')), may hold values from -0.15625 to 0.15625
- down_weight: bfloat16 [8960, 1536], P(('ctx', 'fsdp')), may hold values from -0.0625 to 0.0625
- cotangent: bfloat16 [2, 2048, 1536], P('fsdp', 'ctx'), may hold values from -6 to 6
Outputs:
- layer_out: bfloat16 [2, 2048, 1536], P('fsdp', 'ctx')
- input_grad: float32 [2, 2048, 1536], P('fsdp', 'ctx')
- qkv_weight_grad: float32 [1536, 2048], P(('ctx', 'fsdp'))
- qkv_bias_grad: float32 [1792], P(('ctx', 'fsdp'))
- value_bias_grad: float32 [256], P(('ctx', 'fsdp'))
- out_weight_grad: float32 [1536, 1536], P(('ctx', 'fsdp'))
- attn_gain_grad: float32 [1536], P(('ctx', 'fsdp'))
- mlp_gain_grad: float32 [1536], P(('ctx', 'fsdp'))
- gate_weight_grad: float32 [1536, 8960], P(('ctx', 'fsdp'))
- up_weight_grad: float32 [1536, 8960], P(('ctx', 'fsdp'))
- down_weight_grad: float32 [8960, 1536], P(('ctx', 'fsdp'))
Inputs may be any that keep to these rules, and one draw needn't show every extreme that they name: `deal_table`: each set's row is a permutation of 0 to 31: entry c * 2 + b names the block of 64 consecutive tokens of the set's order (the prompt's 1024 tokens, then 1 continuations of 1024) that ctx index c holds as its block b. `cont_id`: for the token at place t of the set's order that deal_table puts at this row: 0 if t < 1024, else 1 + (t - 1024) // 1024. `position`: for the same token: t if t < 1024, else 1024 + (t - 1024) % 1024.
All inputs are finite; a program needn't handle non-finite values.
Results may differ from a plain program's by a relative error of at most 0.018.
Values may be sent and summed in bfloat16 or wider, within the bound.
No kernel may reach another device: no remote copies, remote signals or barrier semaphores. Data moves between devices by JAX's collectives and lax.ppermute only.
A program may use at most 512 MiB of HBM per device.

v0:
```python
import jax
import jax.numpy as jnp
from jax import lax
from jax.sharding import PartitionSpec as P

H = 12
KV = 2
HD = 128
BLOCKS_DEV = 2
CONT_LEN = 1024


epsilon = 1e-06
rope_base = 1000000.0
neg_large = -1e30


def rms_scale(values):
    return values * lax.rsqrt(jnp.mean(values * values, axis=-1, keepdims=True) + epsilon)


def norm_back(values, gain, incoming):
    inverse = lax.rsqrt(jnp.mean(values * values, axis=-1, keepdims=True) + epsilon)
    normal = values * inverse
    gain_grad = jnp.sum(incoming * normal, axis=0)
    scaled = incoming * gain
    return (
        inverse * (scaled - normal * jnp.mean(scaled * normal, axis=-1, keepdims=True)),
        gain_grad,
    )


def rope_tables(position):
    half_dim = HD // 2
    frequency = jnp.exp(-jnp.log(rope_base) * (2.0 * jnp.arange(half_dim, dtype=jnp.float32) / HD))
    angles = position.astype(jnp.float32)[:, None] * frequency[None, :]
    return (
        jnp.concatenate([jnp.cos(angles)] * 2, axis=-1),
        jnp.concatenate([jnp.sin(angles)] * 2, axis=-1),
    )


def rotate_half(values):
    half_dim = values.shape[-1] // 2
    return jnp.concatenate([-values[..., half_dim:], values[..., :half_dim]], axis=-1)


def apply_rope(values, cosine, sine_table):
    return values * cosine[:, None, :] + rotate_half(values) * sine_table[:, None, :]


def rope_back(incoming, cosine, sine_table):
    return incoming * cosine[:, None, :] - rotate_half(incoming * sine_table[:, None, :])


def visible_pairs(query_seq, query_pos, key_seq, key_pos):
    same_seq = key_seq[None, :] == query_seq[:, None]
    seen = (key_seq[None, :] == 0) | same_seq
    return seen & (~same_seq | (key_pos[None, :] <= query_pos[:, None]))


def key_meta(deal_row, offset, count, block_len, prompt_len):
    row_ids = offset + jnp.arange(count, dtype=jnp.int32)
    slots = row_ids // block_len
    matches = slots[:, None] == jnp.arange(deal_row.shape[0], dtype=jnp.int32)[None, :]
    picked = jnp.sum(jnp.where(matches, deal_row[None, :], 0), axis=1)
    place = picked * block_len + row_ids % block_len
    key_seq = jnp.where(place < prompt_len, 0, 1 + (place - prompt_len) // CONT_LEN)
    key_pos = jnp.where(place < prompt_len, place, prompt_len + (place - prompt_len) % CONT_LEN)
    return (key_seq, key_pos)


def keep_state(state_in):
    return state_in


def shards(
    tokens_in,
    deal_table,
    cont_id,
    position,
    qkv_weight,
    qkv_bias,
    out_weight,
    attn_gain,
    mlp_gain,
    gate_weight,
    up_weight,
    down_weight,
    cotangent,
):
    ctx_size = lax.axis_size("ctx")
    tok_dev = tokens_in.shape[1]
    block_len = tok_dev // BLOCKS_DEV
    prompt_len = tok_dev * ctx_size // 2
    group_size = H // KV
    score_scale = HD ** (-0.5)
    width_q = H * HD
    width_kv = KV * HD
    deal_row = deal_table[0]
    query_seq = cont_id[0]
    query_pos = position[0]
    hidden_in = tokens_in[0].astype(jnp.float32)
    full_qkv, full_bias, full_out, full_attn_gain, full_mlp_gain = (
        lax.all_gather(qkv_weight, ("ctx", "fsdp"), axis=0, tiled=True),
        lax.all_gather(qkv_bias, ("ctx", "fsdp"), axis=0, tiled=True),
        lax.all_gather(out_weight, ("ctx", "fsdp"), axis=0, tiled=True),
        lax.all_gather(attn_gain, ("ctx", "fsdp"), axis=0, tiled=True),
        lax.all_gather(mlp_gain, ("ctx", "fsdp"), axis=0, tiled=True),
    )
    normed = (rms_scale(hidden_in) * full_attn_gain.astype(jnp.float32)).astype(jnp.bfloat16)
    projected = jnp.dot(normed, full_qkv, preferred_element_type=jnp.float32) + full_bias.astype(
        jnp.float32
    )
    cosine, sine_table = rope_tables(query_pos)
    query_low = apply_rope(
        projected[:, :width_q].reshape(tok_dev, H, HD), cosine, sine_table
    ).astype(jnp.bfloat16)
    key_low = apply_rope(
        projected[:, width_q : width_q + width_kv].reshape(tok_dev, KV, HD), cosine, sine_table
    ).astype(jnp.bfloat16)
    value_low = projected[:, width_q + width_kv :].reshape(tok_dev, KV, HD).astype(jnp.bfloat16)
    query_group = query_low.reshape(tok_dev, KV, group_size, HD)

    def visible_for(offset, count):
        key_seq, key_pos = key_meta(deal_row, offset, count, block_len, prompt_len)
        return visible_pairs(query_seq, query_pos, key_seq, key_pos)

    start_state = (
        jnp.full((tok_dev, KV, group_size), neg_large, jnp.float32),
        jnp.zeros((tok_dev, KV, group_size), jnp.float32),
        jnp.zeros((tok_dev, KV, group_size, HD), jnp.float32),
    )
    key_part = lax.all_gather(key_low, "ctx", axis=0, tiled=True)
    value_part = lax.all_gather(value_low, "ctx", axis=0, tiled=True)
    visible = visible_for(jnp.int32(0), key_part.shape[0])

    def attend_compute(state_in):
        run_max, run_total, accum = state_in
        allowed = visible[:, None, None, :]
        scores = (
            jnp.einsum("tkgd,nkd->tkgn", query_group, key_part, preferred_element_type=jnp.float32)
            * score_scale
        )
        block_top = jnp.max(jnp.where(allowed, scores, neg_large), axis=-1)
        new_max = jnp.maximum(run_max, block_top)
        weights = jnp.exp(jnp.where(allowed, scores - new_max[..., None], neg_large))
        new_total = jnp.sum(weights, axis=-1)
        new_accum = jnp.einsum(
            "tkgn,nkd->tkgd",
            weights.astype(jnp.bfloat16),
            value_part,
            preferred_element_type=jnp.float32,
        )
        return (new_max, new_total, new_accum)

    run_max, run_total, accum = lax.cond(jnp.any(visible), attend_compute, keep_state, start_state)
    mixed = accum / run_total[..., None]
    log_total = run_max + jnp.log(run_total)
    attended = mixed.reshape(tok_dev, width_q).astype(jnp.bfloat16)
    resid = hidden_in + jnp.dot(attended, full_out, preferred_element_type=jnp.float32)
    normed_mlp = (rms_scale(resid) * full_mlp_gain.astype(jnp.float32)).astype(jnp.bfloat16)
    full_gate, full_up, full_down = (
        lax.all_gather(gate_weight, ("ctx", "fsdp"), axis=0, tiled=True),
        lax.all_gather(up_weight, ("ctx", "fsdp"), axis=0, tiled=True),
        lax.all_gather(down_weight, ("ctx", "fsdp"), axis=0, tiled=True),
    )
    gate_pre = jnp.dot(normed_mlp, full_gate, preferred_element_type=jnp.float32)
    up_pre = jnp.dot(normed_mlp, full_up, preferred_element_type=jnp.float32)
    sigmoid_gate = jax.nn.sigmoid(gate_pre)
    gate_act = gate_pre * sigmoid_gate
    hidden_low = (gate_act * up_pre).astype(jnp.bfloat16)
    layer_out = resid + jnp.dot(hidden_low, full_down, preferred_element_type=jnp.float32)
    back_qkv, back_out, back_attn_gain, back_mlp_gain = (
        lax.all_gather(qkv_weight, ("ctx", "fsdp"), axis=0, tiled=True),
        lax.all_gather(out_weight, ("ctx", "fsdp"), axis=0, tiled=True),
        lax.all_gather(attn_gain, ("ctx", "fsdp"), axis=0, tiled=True),
        lax.all_gather(mlp_gain, ("ctx", "fsdp"), axis=0, tiled=True),
    )
    back_gate, back_up, back_down = (
        lax.all_gather(gate_weight, ("ctx", "fsdp"), axis=0, tiled=True),
        lax.all_gather(up_weight, ("ctx", "fsdp"), axis=0, tiled=True),
        lax.all_gather(down_weight, ("ctx", "fsdp"), axis=0, tiled=True),
    )
    out_low = cotangent[0]
    out_grad = out_low.astype(jnp.float32)
    hidden_grad = jnp.einsum("td,fd->tf", out_low, back_down, preferred_element_type=jnp.float32)
    gate_grad = (
        hidden_grad * up_pre * sigmoid_gate * (1.0 + gate_pre * (1.0 - sigmoid_gate))
    ).astype(jnp.bfloat16)
    up_grad = (hidden_grad * gate_act).astype(jnp.bfloat16)
    mlp_normed_grad = jnp.einsum(
        "tf,df->td", gate_grad, back_gate, preferred_element_type=jnp.float32
    ) + jnp.einsum("tf,df->td", up_grad, back_up, preferred_element_type=jnp.float32)
    both_grads = jnp.concatenate([gate_grad, up_grad], axis=1)
    ff_width = gate_grad.shape[1]
    columns = normed_mlp
    gate_up_share = lax.psum_scatter(
        jnp.einsum("td,tf->df", columns, both_grads, preferred_element_type=jnp.float32),
        ("ctx", "fsdp"),
        scatter_dimension=0,
        tiled=True,
    )
    columns = hidden_low
    down_share = lax.psum_scatter(
        jnp.einsum("tf,td->fd", columns, out_low, preferred_element_type=jnp.float32),
        ("ctx", "fsdp"),
        scatter_dimension=0,
        tiled=True,
    )
    gate_share = gate_up_share[:, :ff_width]
    up_share = gate_up_share[:, ff_width:]
    resid_part, mlp_gain_grad = norm_back(resid, back_mlp_gain.astype(jnp.float32), mlp_normed_grad)
    resid_grad = out_grad + resid_part
    resid_low = resid_grad.astype(jnp.bfloat16)
    out_w_grad = jnp.einsum("tq,td->qd", attended, resid_low, preferred_element_type=jnp.float32)
    mixed_grad = (
        jnp.einsum("td,qd->tq", resid_low, back_out, preferred_element_type=jnp.float32)
        .astype(jnp.bfloat16)
        .reshape(tok_dev, KV, group_size, HD)
    )
    row_dot = jnp.sum(mixed_grad.astype(jnp.float32) * mixed, axis=-1)
    key_all, value_all = (
        lax.all_gather(key_low, "ctx", axis=0, tiled=True),
        lax.all_gather(value_low, "ctx", axis=0, tiled=True),
    )
    total_keys = key_all.shape[0]
    key_block = min(total_keys, max(tok_dev * max(1, 1024 // tok_dev), total_keys // 16))
    count_blocks = total_keys // key_block

    def back_step(query_acc, block_in):
        key_part, value_part, block_index = block_in
        visible = visible_for(block_index * key_block, key_block)

        def back_compute(acc_in):
            allowed = visible[:, None, None, :]
            scores = (
                jnp.einsum(
                    "tkgd,nkd->tkgn", query_group, key_part, preferred_element_type=jnp.float32
                )
                * score_scale
            )
            probs = jnp.exp(jnp.where(allowed, scores - log_total[..., None], neg_large))
            prob_grad = jnp.einsum(
                "tkgd,nkd->tkgn", mixed_grad, value_part, preferred_element_type=jnp.float32
            )
            score_grad = (probs * (prob_grad - row_dot[..., None])).astype(jnp.bfloat16)
            acc_out = (
                acc_in
                + jnp.einsum(
                    "tkgn,nkd->tkgd", score_grad, key_part, preferred_element_type=jnp.float32
                )
                * score_scale
            )
            key_grad = (
                jnp.einsum(
                    "tkgn,tkgd->nkd", score_grad, query_group, preferred_element_type=jnp.float32
                )
                * score_scale
            )
            value_grad = jnp.einsum(
                "tkgn,tkgd->nkd",
                probs.astype(jnp.bfloat16),
                mixed_grad,
                preferred_element_type=jnp.float32,
            )
            return (acc_out, key_grad, value_grad)

        def skip_block(acc_in):
            blank = jnp.zeros((key_block, KV, HD), jnp.float32)
            return (acc_in, blank, blank)

        acc_out, key_grad, value_grad = lax.cond(
            jnp.any(visible), back_compute, skip_block, query_acc
        )
        return (acc_out, (key_grad, value_grad))

    block_inputs = (
        key_all.reshape(count_blocks, key_block, KV, HD),
        value_all.reshape(count_blocks, key_block, KV, HD),
        jnp.arange(count_blocks, dtype=jnp.int32),
    )
    query_acc, (key_grads, value_grads) = lax.scan(
        back_step, jnp.zeros((tok_dev, KV, group_size, HD), jnp.float32), block_inputs
    )
    key_share, value_share = (
        lax.psum_scatter(
            key_grads.reshape(total_keys, KV, HD), "ctx", scatter_dimension=0, tiled=True
        ),
        lax.psum_scatter(
            value_grads.reshape(total_keys, KV, HD), "ctx", scatter_dimension=0, tiled=True
        ),
    )
    query_grad = rope_back(query_acc.reshape(tok_dev, H, HD), cosine, sine_table)
    key_grad_own = rope_back(key_share, cosine, sine_table)
    proj_grad = jnp.concatenate(
        [
            query_grad.reshape(tok_dev, width_q),
            key_grad_own.reshape(tok_dev, width_kv),
            value_share.reshape(tok_dev, width_kv),
        ],
        axis=1,
    )
    bias_grad = jnp.sum(proj_grad, axis=0)
    front_bias = bias_grad[: width_q + width_kv]
    value_bias = bias_grad[width_q + width_kv :]
    proj_low = proj_grad.astype(jnp.bfloat16)
    qkv_w_grad = jnp.einsum("td,tc->dc", normed, proj_low, preferred_element_type=jnp.float32)
    normed_grad = jnp.einsum("tc,dc->td", proj_low, back_qkv, preferred_element_type=jnp.float32)
    input_part, attn_gain_grad = norm_back(
        hidden_in, back_attn_gain.astype(jnp.float32), normed_grad
    )
    input_grad = resid_grad + input_part
    qkv_share, front_share, value_bias_share, out_share, attn_gain_share, mlp_gain_share = (
        lax.psum_scatter(qkv_w_grad, ("ctx", "fsdp"), scatter_dimension=0, tiled=True),
        lax.psum_scatter(front_bias, ("ctx", "fsdp"), scatter_dimension=0, tiled=True),
        lax.psum_scatter(value_bias, ("ctx", "fsdp"), scatter_dimension=0, tiled=True),
        lax.psum_scatter(out_w_grad, ("ctx", "fsdp"), scatter_dimension=0, tiled=True),
        lax.psum_scatter(attn_gain_grad, ("ctx", "fsdp"), scatter_dimension=0, tiled=True),
        lax.psum_scatter(mlp_gain_grad, ("ctx", "fsdp"), scatter_dimension=0, tiled=True),
    )
    return (
        layer_out.astype(jnp.bfloat16)[None],
        input_grad[None],
        qkv_share,
        front_share,
        value_bias_share,
        out_share,
        attn_gain_share,
        mlp_gain_share,
        gate_share,
        up_share,
        down_share,
    )


def solution(mesh):
    return jax.shard_map(
        shards,
        mesh=mesh,
        in_specs=(
            P("fsdp", "ctx", None),
            P("fsdp", None),
            P("fsdp", "ctx"),
            P("fsdp", "ctx"),
            P(("ctx", "fsdp"), None),
            P(("ctx", "fsdp")),
            P(("ctx", "fsdp"), None),
            P(("ctx", "fsdp")),
            P(("ctx", "fsdp")),
            P(("ctx", "fsdp"), None),
            P(("ctx", "fsdp"), None),
            P(("ctx", "fsdp"), None),
            P("fsdp", "ctx", None),
        ),
        out_specs=(
            P("fsdp", "ctx", None),
            P("fsdp", "ctx", None),
            P(("ctx", "fsdp"), None),
            P(("ctx", "fsdp")),
            P(("ctx", "fsdp")),
            P(("ctx", "fsdp"), None),
            P(("ctx", "fsdp")),
            P(("ctx", "fsdp")),
            P(("ctx", "fsdp"), None),
            P(("ctx", "fsdp"), None),
            P(("ctx", "fsdp"), None),
        ),
        check_vma=False,
    )
```

profile of v0, /device:TPU:0, one launch (start us, length us, event | category | flops | bytes accessed | tf_op | source)
XLA Modules:
  0.0 2679.5 jit_solution(648798799434912077)
XLA Ops:
  10.5 43.0 %all-reduce.9 = (bf16[2048]{0:T(1024)(128)(2,1)S(1)}, bf16[1536]{0:T(1024)(128)(2,1)S(1)}, bf16[1536]{0:T(1024)(128)(2,1)S(1)}) all-reduce(bf16[2048]{0:T(1024)(128)(2,1)S(1)} %dynamic-update-slice.1, bf16[1536]{0:T(1024)(128)(2,1)S(1)} %dynamic-update-slice, ...), channel_id=1, replica_groups=mesh['ctx'=16,'fsdp'=2] {'ctx','fsdp'}, use_global_device_ids=true, to_apply=%add.1 | all-reduce | flops 5120 | bytes 20480
  55.9 27.3 %all-gather.8.cloned.1.call-done = bf16[1536,2048]{1,0:T(8,128)(2,1)} async-done(((bf16[48,2048]{1,0:T(8,128)(2,1)}), bf16[1536,2048]{1,0:T(8,128)(2,1)}) %all-gather.8.cloned.1.call-update) | async-done | bytes 6291472 | tf_op jit(solution)/shard_map/all_gather | solution.py:105
  83.2 4.0 convolution_add_fusion.3
  91.6 2.3 fusion.112
  95.3 46.8 %all-gather.10.cloned.1.call-done = bf16[2048,2,128]{2,0,1:T(8,128)(2,1)} async-done(((bf16[128,2,128]{2,0,1:T(8,128)(2,1)}), bf16[2048,2,128]{2,0,1:T(8,128)(2,1)}) %all-gather.10.cloned.1.call-update) | async-done | bytes 1048592 | tf_op jit(solution)/shard_map/all_gather | solution.py:134
  142.1 2.3 copy.98
  144.4 55.4 %all-gather.12.cloned.1.call-done = bf16[2048,2,128]{2,0,1:T(8,128)(2,1)} async-done(((bf16[128,2,128]{2,0,1:T(8,128)(2,1)}), bf16[2048,2,128]{2,0,1:T(8,128)(2,1)}) %all-gather.12.cloned.1.call-update) | async-done | bytes 1048592 | tf_op jit(solution)/shard_map/all_gather | solution.py:135
  199.9 2.3 copy.100
  202.1 16.7 conditional.2
  203.0 3.2 fusion
  206.8 3.8 fusion.4
  211.3 5.9 fusion.8
  220.9 44.3 %all-gather.14.cloned.1.call-done = bf16[1536,1536]{1,0:T(8,128)(2,1)} async-done(((bf16[48,1536]{1,0:T(8,128)(2,1)}), bf16[1536,1536]{1,0:T(8,128)(2,1)}) %all-gather.14.cloned.1.call-update) | async-done | bytes 4718608 | tf_op jit(solution)/shard_map/all_gather | solution.py:107
  265.3 3.2 multiply_reduce_fusion.3
  268.7 164.1 %all-gather.16.cloned.1.call-done = bf16[1536,8960]{1,0:T(8,128)(2,1)} async-done(((bf16[48,8960]{1,0:T(8,128)(2,1)}), bf16[1536,8960]{1,0:T(8,128)(2,1)}) %all-gather.16.cloned.1.call-update) | async-done | bytes 27525136 | tf_op jit(solution)/shard_map/all_gather | solution.py:164
  432.8 14.8 fusion.115
  447.6 152.1 %all-gather.18.cloned.1.call-done = bf16[1536,8960]{1,0:T(8,128)(2,1)} async-done(((bf16[48,8960]{1,0:T(8,128)(2,1)}), bf16[1536,8960]{1,0:T(8,128)(2,1)}) %all-gather.18.cloned.1.call-update) | async-done | bytes 27525136 | tf_op jit(solution)/shard_map/all_gather | solution.py:165
  599.7 14.8 fusion.116
  614.5 152.3 %all-gather.20.cloned.1.call-done = bf16[8960,1536]{1,0:T(8,128)(2,1)} async-done(((bf16[280,1536]{1,0:T(8,128)(2,1)}), bf16[8960,1536]{1,0:T(8,128)(2,1)}) %all-gather.20.cloned.1.call-update) | async-done | bytes 27525136 | tf_op jit(solution)/shard_map/all_gather | solution.py:166
  766.8 18.9 multiply_convert_fusion
  785.6 14.5 fusion.117
  800.2 16.0 multiply_reduce_fusion
  817.6 4.3 convolution_convert_fusion
  824.5 26.5 while.20
  828.2 8.1 conditional.4
  828.3 2.1 fusion.33
  830.5 2.0 fusion.17
  832.5 1.5 fusion.30
  836.4 1.5 bitcast_dynamic-update-slice_fusion.3
  841.4 8.1 conditional.4
  841.4 2.1 fusion.33
  843.6 2.0 fusion.17
  845.6 1.5 fusion.30
  852.7 39.9 %fusion.55 = f32[1536,17920]{1,0:T(8,128)} fusion(bf16[128,1536]{1,0:T(8,128)(2,1)} %copy-done.12, bf16[128,8960]{1,0:T(8,128)(2,1)} %get-tuple-element.474, bf16[128,8960]{1,0:T(8,128)(2,1)S(1)} %copy-done.5), kind=kOutput, calls=%fused_computation.79 | convolution fusion | flops 7055605760 | bytes 115081216 | tf_op jit(solution)/shard_map/td,tf->df/dot_general | solution.py:199
  893.8 5.1 fusion.85
  900.1 29.6 %reduce-scatter.9.cloned.1.call-done = f32[128,2,128]{2,0,1:T(8,128)} async-done(((f32[2048,2,128]{2,0,1:T(8,128)}), f32[128,2,128]{2,0,1:T(8,128)}) %reduce-scatter.9.cloned.1.call-update) | async-done | bytes 131088 | tf_op jit(solution)/shard_map/reduce_scatter | solution.py:287
  931.9 78.1 %reduce-scatter.11.cloned.1.call-done = f32[128,2,128]{2,0,1:T(8,128)} async-done(((f32[2048,2,128]{2,0,1:T(8,128)}), f32[128,2,128]{2,0,1:T(8,128)}) %reduce-scatter.11.cloned.1.call-update) | async-done | bytes 131088 | tf_op jit(solution)/shard_map/reduce_scatter | solution.py:290
  1011.0 6.4 fusion.90
  1017.5 1.8 copy-done.6
  1019.4 34.7 %fusion.80 = f32[8960,1536]{1,0:T(8,128)} fusion(bf16[128,8960]{1,0:T(8,128)(2,1)S(1)} %copy-done.6, bf16[1,128,1536]{2,1,0:T(8,128)(2,1)S(1)} %copy-done.21), kind=kOutput, calls=%fused_computation.131 | convolution fusion | flops 3523215360 | bytes 57737216 | tf_op jit(solution)/shard_map/tf,td->fd/dot_general | solution.py:206
  1055.4 18.0 fusion.61
  1073.8 6.5 fusion.74
  1080.3 37.3 %all-reduce.8 = (f32[1792]{0:T(1024)S(1)}, f32[256]{0:T(256)S(1)}, f32[1536]{0:T(1024)S(1)}, f32[1536]{0:T(1024)S(1)}) all-reduce(f32[1792]{0:T(1024)S(1)} %bitcast.209, f32[256]{0:T(256)S(1)} %slice.73, f32[1536]{0:T(1024)S(1)} %get-tuple-element.425, f32[1536]{0:T(1024)S(1)} %copy-done.34), channel_id=5, replica_groups=mesh['ctx'=16,'fsdp'=2] {'ctx','fsdp'}, use_global_device_ids=true, to_apply=%region_21.22.clone | all-reduce | flops 5120 | bytes 40960
  1121.2 779.0 %reduce-scatter.17.cloned.1.call-done = f32[48,17920]{1,0:T(8,128)} async-done(((f32[1536,17920]{1,0:T(8,128)}), f32[48,17920]{1,0:T(8,128)}) %reduce-scatter.17.cloned.1.call-update) | async-done | bytes 3440656 | tf_op jit(solution)/shard_map/reduce_scatter | solution.py:198
  1900.2 4.0 fusion.114
  1904.1 138.2 %reduce-scatter.15.cloned.1.call-done = f32[48,1536]{1,0:T(8,128)} async-done(((f32[1536,1536]{1,0:T(8,128)}), f32[48,1536]{1,0:T(8,128)}) %reduce-scatter.15.cloned.1.call-update) | async-done | bytes 294928 | tf_op jit(solution)/shard_map/reduce_scatter | solution.py:318
  2042.3 161.0 %reduce-scatter.13.cloned.1.call-done = f32[48,2048]{1,0:T(8,128)} async-done(((f32[1536,2048]{1,0:T(8,128)}), f32[48,2048]{1,0:T(8,128)}) %reduce-scatter.13.cloned.1.call-update) | async-done | bytes 393232 | tf_op jit(solution)/shard_map/reduce_scatter | solution.py:315
  2203.3 469.5 %reduce-scatter.19.cloned.1.call-done = f32[280,1536]{1,0:T(8,128)} async-done(((f32[8960,1536]{1,0:T(8,128)}), f32[280,1536]{1,0:T(8,128)}) %reduce-scatter.19.cloned.1.call-update) | async-done | bytes 1720336
  (202 shorter events, 43.3 us)
Async XLA Ops:
  7.2 76.0 %all-gather.8.cloned.1.call-start = ((), (), s32[]{:S(2)}) async-start(), calls=%async_computation.6 | async-start | bytes 6488064 | tf_op jit(solution)/shard_map/all_gather | solution.py:105
  7.9 134.2 %all-gather.10.cloned.1.call-start = ((), (), s32[]{:S(2)}) async-start(), calls=%async_computation.7 | async-start | bytes 1114112 | tf_op jit(solution)/shard_map/all_gather | solution.py:134
  53.6 33.6 %copy-start.32 = (f32[1536]{0:T(1024)}, f32[1536]{0:T(1024)S(1)}, u32[]{:S(2)}) copy-start(f32[1536]{0:T(1024)S(1)} %convert_element_type.100) | copy-start | bytes 18436
  54.5 40.5 %copy-start.22 = (f32[128,128]{0,1:T(8,128)}, f32[128,128]{0,1:T(8,128)S(1)}, u32[]{:S(2)}) copy-start(f32[128,128]{0,1:T(8,128)S(1)} %get-tuple-element.493) | copy-start | bytes 196612
  54.5 40.5 %copy-start.24 = (f32[128,128]{0,1:T(8,128)}, f32[128,128]{0,1:T(8,128)S(1)}, u32[]{:S(2)}) copy-start(f32[128,128]{0,1:T(8,128)S(1)} %get-tuple-element.494) | copy-start | bytes 196612
  54.6 33.5 %copy-start.29 = (f32[128,128]{1,0:T(8,128)}, f32[128,128]{1,0:T(8,128)S(1)}, u32[]{:S(2)}) copy-start(f32[128,128]{1,0:T(8,128)S(1)} %copy.91) | copy-start | bytes 196612
  54.7 33.4 %copy-start.27 = (f32[128,128]{1,0:T(8,128)}, f32[128,128]{1,0:T(8,128)S(1)}, u32[]{:S(2)}) copy-start(f32[128,128]{1,0:T(8,128)S(1)} %copy.87) | copy-start | bytes 196612
  55.9 31.3 %copy-start.39 = (f32[128]{0:T(128)}, f32[128]{0:T(128)S(1)}, u32[]{:S(2)}) copy-start(f32[128]{0:T(128)S(1)} %add_rsqrt_fusion.1) | copy-start | bytes 1540
  55.9 35.5 %copy-start.37 = (s32[1,32]{1,0:T(1,128)S(1)}, s32[1,32]{1,0:T(1,128)}, u32[]{:S(2)}) copy-start(s32[1,32]{1,0:T(1,128)} %param.20) | copy-start | bytes 388
  55.9 35.7 %copy-start.35 = (s32[1,128]{1,0:T(1,128)S(1)}, s32[1,128]{1,0:T(1,128)}, u32[]{:S(2)}) copy-start(s32[1,128]{1,0:T(1,128)} %param.22) | copy-start | bytes 1540
  55.9 35.7 %copy-start.36 = (s32[1,128]{1,0:T(1,128)S(1)}, s32[1,128]{1,0:T(1,128)}, u32[]{:S(2)}) copy-start(s32[1,128]{1,0:T(1,128)} %param.21) | copy-start | bytes 1540
  88.1 111.8 %all-gather.12.cloned.1.call-start = ((), (), s32[]{:S(2)}) async-start(), calls=%async_computation.8 | async-start | bytes 1114112 | tf_op jit(solution)/shard_map/all_gather | solution.py:135
  88.8 176.4 %all-gather.14.cloned.1.call-start = ((), (), s32[]{:S(2)}) async-start(), calls=%async_computation.9 | async-start | bytes 4866048 | tf_op jit(solution)/shard_map/all_gather | solution.py:107
  89.4 343.4 %all-gather.16.cloned.1.call-start = ((), (), s32[]{:S(2)}) async-start(), calls=%async_computation.10 | async-start | bytes 28385280 | tf_op jit(solution)/shard_map/all_gather | solution.py:164
  90.0 509.7 %all-gather.18.cloned.1.call-start = ((), (), s32[]{:S(2)}) async-start(), calls=%async_computation.11 | async-start | bytes 28385280 | tf_op jit(solution)/shard_map/all_gather | solution.py:165
  90.6 676.2 %all-gather.20.cloned.1.call-start = ((), (), s32[]{:S(2)}) async-start(), calls=%async_computation.12 | async-start | bytes 28385280 | tf_op jit(solution)/shard_map/all_gather | solution.py:166
  91.3 838.4 %reduce-scatter.9.cloned.1.call-start = ((), (), s32[]{:S(2)}) async-start(), calls=%async_computation.13 | async-start | bytes 2228224 | tf_op jit(solution)/shard_map/reduce_scatter | solution.py:287
  202.1 63.1 %copy-start.3 = (bf16[1,128,1536]{2,1,0:T(8,128)(2,1)S(1)}, bf16[1,128,1536]{2,1,0:T(8,128)(2,1)}, u32[]{:S(2)}) copy-start(bf16[1,128,1536]{2,1,0:T(8,128)(2,1)} %param.19) | copy-start | bytes 1179652
  220.9 47.6 %copy-start.14 = (bf16[128,2,6,128]{0,3,2,1:T(8,128)(2,1)}, bf16[128,2,6,128]{0,3,2,1:T(8,128)(2,1)S(1)}, u32[]{:S(2)}) copy-start(bf16[128,2,6,128]{0,3,2,1:T(8,128)(2,1)S(1)} %fusion.84) | copy-start | bytes 1179652
  268.5 547.7 %copy-start.1 = (f32[128,1536]{1,0:T(8,128)}, f32[128,1536]{1,0:T(8,128)S(1)}, u32[]{:S(2)}) copy-start(f32[128,1536]{1,0:T(8,128)S(1)} %get-tuple-element.490) | copy-start | bytes 2359300
  268.7 331.0 %copy-start.12 = (bf16[128,1536]{1,0:T(8,128)(2,1)}, bf16[128,1536]{1,0:T(8,128)(2,1)S(1)}, u32[]{:S(2)}) copy-start(bf16[128,1536]{1,0:T(8,128)(2,1)S(1)} %multiply_convert_fusion.3) | copy-start | bytes 1179652
  447.6 319.2 %copy-start.20 = (bf16[1,128,1536]{2,1,0:T(8,128)(2,1)S(1)}, bf16[1,128,1536]{2,1,0:T(8,128)(2,1)}, u32[]{:S(2)}) copy-start(bf16[1,128,1536]{2,1,0:T(8,128)(2,1)} %param.31) | copy-start | bytes 1179652
  817.6 6.9 copy-start.9
  817.6 6.9 copy-start.38
  828.2 2.2 copy-start.26
  828.2 2.2 copy-start.31
  841.4 2.2 copy-start.26
  841.4 2.2 copy-start.31
  841.4 2.2 copy-start.41
  841.4 2.2 copy-start.42
  851.0 158.9 %reduce-scatter.11.cloned.1.call-start = ((), (), s32[]{:S(2)}) async-start(), calls=%async_computation.14 | async-start | bytes 2228224 | tf_op jit(solution)/shard_map/reduce_scatter | solution.py:290
  851.8 1048.4 %reduce-scatter.17.cloned.1.call-start = ((), (), s32[]{:S(2)}) async-start(), calls=%async_computation.17 | async-start | bytes 113541120 | tf_op jit(solution)/shard_map/reduce_scatter | solution.py:198
  892.6 1149.7 %reduce-scatter.15.cloned.1.call-start = ((), (), s32[]{:S(2)}) async-start(), calls=%async_computation.16 | async-start | bytes 9732096 | tf_op jit(solution)/shard_map/reduce_scatter | solution.py:318
  899.0 30.7 %copy-start.30 = (f32[128,128]{1,0:T(8,128)S(1)}, f32[128,128]{1,0:T(8,128)}, u32[]{:S(2)}) copy-start(f32[128,128]{1,0:T(8,128)} %copy-done.29) | copy-start | bytes 196612
  899.0 1304.3 %reduce-scatter.13.cloned.1.call-start = ((), (), s32[]{:S(2)}) async-start(), calls=%async_computation.15 | async-start | bytes 12976128 | tf_op jit(solution)/shard_map/reduce_scatter | solution.py:315
  899.0 31.7 %copy-start.28 = (f32[128,128]{1,0:T(8,128)S(1)}, f32[128,128]{1,0:T(8,128)}, u32[]{:S(2)}) copy-start(f32[128,128]{1,0:T(8,128)} %copy-done.27) | copy-start | bytes 196612
  899.8 111.2 %copy-start.4 = (bf16[1,128,1536]{2,1,0:T(8,128)(2,1)S(1)}, bf16[1,128,1536]{2,1,0:T(8,128)(2,1)}, u32[]{:S(2)}) copy-start(bf16[1,128,1536]{2,1,0:T(8,128)(2,1)} %param.19) | copy-start | bytes 1179652
  899.8 111.2 %copy-start.33 = (f32[1536]{0:T(1024)S(1)}, f32[1536]{0:T(1024)}, u32[]{:S(2)}) copy-start(f32[1536]{0:T(1024)} %copy-done.32) | copy-start | bytes 18436
  899.8 111.2 %copy-start.40 = (f32[128]{0:T(128)S(1)}, f32[128]{0:T(128)}, u32[]{:S(2)}) copy-start(f32[128]{0:T(128)} %copy-done.39) | copy-start | bytes 1540
  900.1 117.3 %copy-start.7 = (f32[128,1536]{0,1:T(8,128)}, f32[128,1536]{0,1:T(8,128)S(1)}, u32[]{:S(2)}) copy-start(f32[128,1536]{0,1:T(8,128)S(1)} %bitcast_subtract_fusion.3) | copy-start | bytes 2359300
  931.9 85.6 %copy-start.16 = (f32[128,2,128]{0,2,1:T(8,128)}, f32[128,2,128]{0,2,1:T(8,128)S(1)}, u32[]{:S(2)}) copy-start(f32[128,2,128]{0,2,1:T(8,128)S(1)} %copy.105) | copy-start | bytes 393220
  1011.0 6.5 copy-start.18
  1017.5 1655.3 %reduce-scatter.19.cloned.1.call-start = ((), (), s32[]{:S(2)}) async-start(), calls=%async_computation.18 | async-start | bytes 56770560
  1055.4 18.0 copy-start.8
  1055.4 18.0 copy-start.17
  1055.4 18.0 copy-start.19
  1073.4 6.9 copy-start.34
  1073.4 46.5 %copy-start.11 = (f32[128,1536]{1,0:T(8,128)S(1)}, f32[128,1536]{1,0:T(8,128)}, u32[]{:S(2)}) copy-start(f32[128,1536]{1,0:T(8,128)} %copy-done.9) | copy-start | bytes 2359300
  (13 other events, 20.2 us)
Sparse Core Ops, SparseCore 0:
  10.9 72.2 all-gather.7
  88.2 53.8 all-gather.9
  145.5 54.3 all-gather.11
  202.6 62.5 all-gather.13
  268.0 164.7 all-gather.15
  435.6 164.0 all-gather.17
  602.6 164.0 all-gather.19
  851.2 78.4 reduce-scatter.8
  932.0 77.9 reduce-scatter.10
  1016.2 883.8 reduce-scatter.16
  1907.6 134.6 reduce-scatter.14
  2048.7 154.4 reduce-scatter.12
  2211.4 461.3 reduce-scatter.18
where the time goes:
time: 2680 us
  waiting for transfers between devices  2300 us (86%)
  matrix products  226 us (8%)
  blocking collectives  80.3 us (3%)
  local copies, waits for them, and re-layouts  29.9 us (1%)
    reduce_scatter x1, waiting for transfers between devices, shards(): lax.psum_scatter(jnp.einsum('td,tf->df', columns, both_grads, preferred_e...  779 us
    unnamed x14, waiting for transfers between devices  473 us
    all_gather x1, waiting for transfers between devices, shards(): lax.all_gather(gate_weight, ('ctx', 'fsdp'), axis=0, tiled=True)  164 us
    reduce_scatter x1, waiting for transfers between devices, shards(): lax.psum_scatter(qkv_w_grad, ('ctx', 'fsdp'), scatter_dimension=0, tiled=...  161 us
    all_gather x1, waiting for transfers between devices, shards(): lax.all_gather(down_weight, ('ctx', 'fsdp'), axis=0, tiled=True)  152 us
    all_gather x1, waiting for transfers between devices, shards(): lax.all_gather(up_weight, ('ctx', 'fsdp'), axis=0, tiled=True)  152 us
    reduce_scatter x1, waiting for transfers between devices, shards(): lax.psum_scatter(out_w_grad, ('ctx', 'fsdp'), scatter_dimension=0, tiled=...  138 us
    unnamed x2, blocking collectives  80.3 us
  transfers between devices with their start and end apart: 13, of which 13 were waited for; matrix products, arithmetic and copies ran while one was open for 7% of the time, Pallas kernels for 0%

commit v1 on v0

v1 whole, which is shorter than its diff:
```python
import jax
import jax.numpy as jnp
from jax import lax
from jax.sharding import PartitionSpec as P

H = 12
KV = 2
HD = 128
BLOCKS_DEV = 2
CONT_LEN = 1024


epsilon = 1e-06
rope_base = 1000000.0
neg_large = -1e30
low = jnp.bfloat16


def rms_scale(values):
    return values * lax.rsqrt(jnp.mean(values * values, axis=-1, keepdims=True) + epsilon)


def norm_back(values, gain, incoming):
    inverse = lax.rsqrt(jnp.mean(values * values, axis=-1, keepdims=True) + epsilon)
    normal = values * inverse
    gain_grad = jnp.sum(incoming * normal, axis=0)
    scaled = incoming * gain
    return (
        inverse * (scaled - normal * jnp.mean(scaled * normal, axis=-1, keepdims=True)),
        gain_grad,
    )


def rope_tables(position):
    half_dim = HD // 2
    frequency = jnp.exp(-jnp.log(rope_base) * (2.0 * jnp.arange(half_dim, dtype=jnp.float32) / HD))
    angles = position.astype(jnp.float32)[:, None] * frequency[None, :]
    return (
        jnp.concatenate([jnp.cos(angles)] * 2, axis=-1),
        jnp.concatenate([jnp.sin(angles)] * 2, axis=-1),
    )


def rotate_half(values):
    half_dim = values.shape[-1] // 2
    return jnp.concatenate([-values[..., half_dim:], values[..., :half_dim]], axis=-1)


def apply_rope(values, cosine, sine_table):
    return values * cosine[:, None, :] + rotate_half(values) * sine_table[:, None, :]


def rope_back(incoming, cosine, sine_table):
    return incoming * cosine[:, None, :] - rotate_half(incoming * sine_table[:, None, :])


def visible_pairs(query_seq, query_pos, key_seq, key_pos):
    same_seq = key_seq[None, :] == query_seq[:, None]
    seen = (key_seq[None, :] == 0) | same_seq
    return seen & (~same_seq | (key_pos[None, :] <= query_pos[:, None]))


def key_meta(deal_row, row_ids, block_len, prompt_len):
    slots = row_ids // block_len
    matches = slots[:, None] == jnp.arange(deal_row.shape[0], dtype=jnp.int32)[None, :]
    picked = jnp.sum(jnp.where(matches, deal_row[None, :], 0), axis=1)
    place = picked * block_len + row_ids % block_len
    key_seq = jnp.where(place < prompt_len, 0, 1 + (place - prompt_len) // CONT_LEN)
    key_pos = jnp.where(place < prompt_len, place, prompt_len + (place - prompt_len) % CONT_LEN)
    return (key_seq, key_pos)


def axes_of(size):
    return {16: (4, 2, 2), 64: (2, 4, 4, 2)}.get(size, (size,))


class Grid:
    def __init__(self, size):
        self.size = size
        self.axes = axes_of(size)
        self.rank = len(self.axes)
        self.strides = []
        step = size
        for extent in self.axes:
            step //= extent
            self.strides.append(step)
        index = lax.axis_index("ctx")
        self.place = [(index // s) % e for s, e in zip(self.strides, self.axes)]

    def shift(self, values, axis, by):
        stride, extent = self.strides[axis], self.axes[axis]
        pairs = []
        for i in range(self.size):
            digit = (i // stride) % extent
            pairs.append((i, i + (((digit + by) % extent) - digit) * stride))
        return lax.ppermute(values, "ctx", pairs)

    def gather_axis(self, values, axis, absolute):
        extent = self.axes[axis]
        pieces = [values]
        for _ in range(extent - 1):
            pieces.append(self.shift(pieces[-1], axis, 1))
        if not absolute:
            return jnp.concatenate(pieces, axis=axis)
        wheel = jnp.concatenate(pieces[::-1] + pieces[:0:-1], axis=axis)
        return lax.dynamic_slice_in_dim(wheel, extent - 1 - self.place[axis], extent, axis=axis)

    def scatter_axis(self, values, axis, absolute):
        extent = self.axes[axis]

        def take(back):
            if absolute:
                spot = (self.place[axis] - back + extent) % extent
                return lax.dynamic_slice_in_dim(values, spot, 1, axis=axis)
            return lax.slice_in_dim(values, back, back + 1, axis=axis)

        total = take(extent - 1)
        for back in range(extent - 2, -1, -1):
            total = take(back) + self.shift(total, axis, -1)
        return total

    def gather(self, parts, orders, absolute):
        parts = [p.reshape((1,) * self.rank + p.shape) for p in parts]
        for stage in range(max(len(o) for o in orders)):
            parts = [
                self.gather_axis(p, o[stage], absolute) if stage < len(o) else p
                for p, o in zip(parts, orders)
            ]
        return parts

    def scatter(self, parts, orders, absolute):
        for stage in range(max(len(o) for o in orders)):
            parts = [
                self.scatter_axis(p, o[::-1][stage], absolute) if stage < len(o) else p
                for p, o in zip(parts, orders)
            ]
        return [p.reshape(p.shape[self.rank :]) for p in parts]

    def source_rows(self, first, count, over):
        index = jnp.int32(0)
        for axis in range(self.rank):
            if axis in over:
                back = jnp.arange(self.axes[axis], dtype=jnp.int32)
            else:
                back = jnp.zeros((1,), jnp.int32)
            digit = (self.place[axis] - back + self.axes[axis]) % self.axes[axis]
            shape = [1] * self.rank
            shape[axis] = digit.shape[0]
            index = index + digit.reshape(shape) * self.strides[axis]
        return index[..., None], first + jnp.arange(count, dtype=jnp.int32)


def rotations(axes):
    axes = list(axes)
    return [tuple(axes[i:] + axes[:i]) for i in range(len(axes))]


def other_core(values):
    return lax.ppermute(values, "fsdp", [(0, 1), (1, 0)])


def both_cores(values, core, axis):
    other = other_core(values)
    first = jnp.where(core == 0, values, other)
    second = jnp.where(core == 0, other, values)
    return jnp.concatenate([first, second], axis=axis)


def own_core_sum(values, core, axis):
    mine = lax.dynamic_slice_in_dim(values, core, 1, axis=axis)
    theirs = lax.dynamic_slice_in_dim(values, 1 - core, 1, axis=axis)
    return mine + other_core(theirs)


def split_rows(total, shares):
    bounds = [0]
    run = 0.0
    for share in shares[:-1]:
        run += share
        bounds.append(max(bounds[-1], int(round(total * run / 16)) * 16))
    bounds.append(total)
    return bounds


def shards(
    tokens_in,
    deal_table,
    cont_id,
    position,
    qkv_weight,
    qkv_bias,
    out_weight,
    attn_gain,
    mlp_gain,
    gate_weight,
    up_weight,
    down_weight,
    cotangent,
):
    ctx_size = lax.axis_size("ctx")
    devices = 2 * ctx_size
    core = lax.axis_index("fsdp")
    grid = Grid(ctx_size)
    all_axes = tuple(range(grid.rank))
    tok_dev, width = tokens_in.shape[1], tokens_in.shape[2]
    block_len = tok_dev // BLOCKS_DEV
    prompt_len = tok_dev * ctx_size // 2
    group_size = H // KV
    score_scale = HD ** (-0.5)
    width_q = H * HD
    width_kv = KV * HD
    deal_row = deal_table[0]
    query_seq = cont_id[0]
    query_pos = position[0]
    hidden_in = tokens_in[0].astype(jnp.float32)
    rows_w = qkv_weight.shape[0]

    ff_axes = (0, 1) if grid.rank == 3 else all_axes
    far_axes = tuple(a for a in all_axes if a not in ff_axes)
    ff_size = 1
    for a in ff_axes:
        ff_size *= grid.axes[a]
    far_size = ctx_size // ff_size
    ff_total = gate_weight.shape[1]
    ff_cols = ff_total // ff_size
    members = {}
    for i in range(ctx_size):
        key = tuple((i // grid.strides[a]) % grid.axes[a] for a in far_axes)
        members.setdefault(key, []).append(i)
    groups = [members[k] for k in sorted(members)]

    orders3 = rotations(all_axes)
    if grid.rank == 3:
        orders3 = [(2, 1, 0), (1, 0, 2), (0, 2, 1)]
        token_bounds = split_rows(tok_dev, (0.25, 0.375, 0.375))
    else:
        token_bounds = split_rows(tok_dev, (1.0 / grid.rank,) * grid.rank)
    if grid.rank == 3:
        ff_orders = [(0, 1), (1, 0)]
        ff_bounds = split_rows(tok_dev, (0.625, 0.375))
    else:
        ff_orders, ff_bounds = orders3, token_bounds

    def gather_columns(weight, pieces):
        bounds = [weight.shape[1] * i // (128 * pieces) * 128 for i in range(pieces)]
        bounds.append(weight.shape[1])
        parts = [weight[:, a:b] for a, b in zip(bounds[:-1], bounds[1:])]
        orders = (orders3 * pieces)[:pieces]
        parts = grid.gather([p[None] for p in parts], orders, True)
        parts = [both_cores(p, core, grid.rank) for p in parts]
        return [p.reshape(devices * rows_w, p.shape[-1]) for p in parts]

    def scatter_columns(grad):
        pieces = grid.rank
        lead = grid.axes + (2, rows_w)
        bounds = [grad.shape[1] * i // (128 * pieces) * 128 for i in range(pieces)]
        bounds.append(grad.shape[1])
        parts = [
            own_core_sum(
                grad[:, a:b].astype(low).reshape(lead + (b - a,)), core, grid.rank
            )
            for a, b in zip(bounds[:-1], bounds[1:])
        ]
        parts = grid.scatter(parts, orders3, True)
        return jnp.concatenate([p[0] for p in parts], axis=1).astype(jnp.float32)

    def gather_tokens(values, bounds, orders):
        parts = [values[a:b] for a, b in zip(bounds[:-1], bounds[1:])]
        parts = grid.gather(parts, orders, False)
        return jnp.concatenate([p.reshape(-1, p.shape[-1]) for p in parts], axis=0)

    def scatter_tokens(values, bounds, orders, over):
        parts = []
        start = 0
        lead = tuple(grid.axes[a] if a in over else 1 for a in all_axes)
        count = 1
        for e in lead:
            count *= e
        for a, b in zip(bounds[:-1], bounds[1:]):
            rows = count * (b - a)
            parts.append(values[start : start + rows].reshape(lead + (b - a, values.shape[-1])))
            start += rows
        return jnp.concatenate(grid.scatter(parts, orders, False), axis=0)

    side_rows = jnp.zeros((rows_w, 128), low)
    bias_len = qkv_bias.shape[0]
    side_rows = side_rows.at[0, :rows_w].set(attn_gain)
    side_rows = side_rows.at[1, :rows_w].set(mlp_gain)
    side_rows = side_rows.at[2, :bias_len].set(qkv_bias)
    kv_cols, q_front, q_back = gather_columns(
        jnp.concatenate(
            [qkv_weight[:, width_q:], side_rows, qkv_weight[:, :width_q]], axis=1
        ),
        3,
    )
    full_kv_q = jnp.concatenate([kv_cols, q_front, q_back], axis=1)
    side = full_kv_q[:, 2 * width_kv : 2 * width_kv + 128].reshape(devices, rows_w, 128)
    full_attn_gain = side[:, 0, :rows_w].reshape(-1).astype(jnp.float32)
    full_mlp_gain = side[:, 1, :rows_w].reshape(-1).astype(jnp.float32)
    full_bias = side[:, 2, :bias_len].reshape(-1).astype(jnp.float32)
    full_qkv = jnp.concatenate(
        [full_kv_q[:, 2 * width_kv + 128 :], full_kv_q[:, : 2 * width_kv]], axis=1
    )
    full_out = jnp.concatenate(gather_columns(out_weight, grid.rank), axis=1)

    normed = (rms_scale(hidden_in) * full_attn_gain).astype(low)
    projected = jnp.dot(normed, full_qkv, preferred_element_type=jnp.float32) + full_bias
    cosine, sine_table = rope_tables(query_pos)
    query_low = apply_rope(
        projected[:, :width_q].reshape(tok_dev, H, HD), cosine, sine_table
    ).astype(low)
    key_low = apply_rope(
        projected[:, width_q : width_q + width_kv].reshape(tok_dev, KV, HD), cosine, sine_table
    ).astype(low)
    value_low = projected[:, width_q + width_kv :].astype(low)
    query_group = query_low.reshape(tok_dev, KV, group_size, HD)

    kv_all = gather_tokens(
        jnp.concatenate([key_low.reshape(tok_dev, width_kv), value_low], axis=1),
        token_bounds,
        orders3,
    )
    total_keys = kv_all.shape[0]
    key_all = kv_all[:, :width_kv].reshape(total_keys, KV, HD)
    value_all = kv_all[:, width_kv:].reshape(total_keys, KV, HD)
    row_ids = []
    for a, b in zip(token_bounds[:-1], token_bounds[1:]):
        chips, rows = grid.source_rows(a, b - a, all_axes)
        row_ids.append((chips * tok_dev + rows).reshape(-1))
    row_ids = jnp.concatenate(row_ids)
    key_seq, key_pos = key_meta(deal_row, row_ids, block_len, prompt_len)
    allowed = visible_pairs(query_seq, query_pos, key_seq, key_pos)[:, None, None, :]

    scores = (
        jnp.einsum("tkgd,nkd->tkgn", query_group, key_all, preferred_element_type=jnp.float32)
        * score_scale
    )
    scores = jnp.where(allowed, scores, neg_large)
    top = jnp.max(scores, axis=-1)
    weights = jnp.exp(scores - top[..., None])
    weight_sum = jnp.sum(weights, axis=-1)
    mixed = (
        jnp.einsum(
            "tkgn,nkd->tkgd", weights.astype(low), value_all, preferred_element_type=jnp.float32
        )
        / weight_sum[..., None]
    )
    log_total = top + jnp.log(weight_sum)
    attended = mixed.reshape(tok_dev, width_q).astype(low)
    resid = hidden_in + jnp.dot(attended, full_out, preferred_element_type=jnp.float32)
    normed_mlp = (rms_scale(resid) * full_mlp_gain).astype(low)

    def to_columns(weight):
        return jnp.swapaxes(weight.reshape(rows_w, ff_size, ff_cols), 0, 1)

    gate_up = jnp.concatenate([to_columns(gate_weight), to_columns(up_weight)], axis=2)
    gate_up = lax.all_to_all(
        gate_up, "ctx", split_axis=0, concat_axis=0, tiled=True, axis_index_groups=groups
    )
    lead = tuple(grid.axes[a] if a in ff_axes else 1 for a in all_axes)
    gate_up = gate_up.reshape(lead + (1, rows_w, 2 * ff_cols))
    for a in far_axes:
        gate_up = grid.gather_axis(gate_up, a, True)
    gate_up = both_cores(gate_up, core, grid.rank).reshape(width, 2 * ff_cols)
    rows_d = down_weight.shape[0]
    down = down_weight.reshape((1,) * (grid.rank + 1) + down_weight.shape)
    for a in far_axes:
        down = grid.gather_axis(down, a, True)
    down = both_cores(down, core, grid.rank).reshape(ff_cols, width)

    out_low = cotangent[0]
    out_grad = out_low.astype(jnp.float32)
    cot_all = gather_tokens(out_low, ff_bounds, ff_orders)
    mlp_all = gather_tokens(normed_mlp, ff_bounds, ff_orders)

    hidden_grad = jnp.einsum("td,fd->tf", cot_all, down, preferred_element_type=jnp.float32)
    gate_up_pre = jnp.dot(mlp_all, gate_up, preferred_element_type=jnp.float32)
    gate_pre, up_pre = gate_up_pre[:, :ff_cols], gate_up_pre[:, ff_cols:]
    sigmoid_gate = jax.nn.sigmoid(gate_pre)
    gate_act = gate_pre * sigmoid_gate
    hidden_low = (gate_act * up_pre).astype(low)
    gate_grad = (
        hidden_grad * up_pre * sigmoid_gate * (1.0 + gate_pre * (1.0 - sigmoid_gate))
    ).astype(low)
    up_grad = (hidden_grad * gate_act).astype(low)
    both_grads = jnp.concatenate([gate_grad, up_grad], axis=1)
    mlp_partial = jnp.einsum(
        "tf,df->td", both_grads, gate_up, preferred_element_type=jnp.float32
    ).astype(low)
    mlp_normed_grad = scatter_tokens(mlp_partial, ff_bounds, ff_orders, ff_axes).astype(
        jnp.float32
    )
    out_partial = jnp.dot(hidden_low, down, preferred_element_type=jnp.float32).astype(low)
    layer_out = resid + scatter_tokens(out_partial, ff_bounds, ff_orders, ff_axes).astype(
        jnp.float32
    )

    gate_up_grad = jnp.einsum("td,tf->df", mlp_all, both_grads, preferred_element_type=jnp.float32)
    gate_up_grad = gate_up_grad.astype(low).reshape(grid.axes + (2, rows_w, 2 * ff_cols))
    gate_up_grad = own_core_sum(gate_up_grad, core, grid.rank)
    for a in far_axes:
        gate_up_grad = grid.scatter_axis(gate_up_grad, a, True)
    gate_up_grad = gate_up_grad.reshape(ff_size, rows_w, 2 * ff_cols)
    gate_up_grad = lax.all_to_all(
        gate_up_grad, "ctx", split_axis=0, concat_axis=0, tiled=True, axis_index_groups=groups
    ).astype(jnp.float32)

    def to_rows(grad):
        return jnp.swapaxes(grad, 0, 1).reshape(rows_w, ff_total)

    gate_share = to_rows(gate_up_grad[:, :, :ff_cols])
    up_share = to_rows(gate_up_grad[:, :, ff_cols:])
    down_grad = jnp.einsum("tf,td->fd", hidden_low, cot_all, preferred_element_type=jnp.float32)
    far_lead = tuple(grid.axes[a] if a in far_axes else 1 for a in all_axes)
    down_grad = down_grad.astype(low).reshape(far_lead + (2, rows_d, width))
    down_grad = own_core_sum(down_grad, core, grid.rank)
    for a in far_axes:
        down_grad = grid.scatter_axis(down_grad, a, True)
    down_share = down_grad.reshape(rows_d, width).astype(jnp.float32)

    resid_part, mlp_gain_grad = norm_back(resid, full_mlp_gain, mlp_normed_grad)
    resid_grad = out_grad + resid_part
    resid_low = resid_grad.astype(low)
    out_w_grad = jnp.einsum("tq,td->qd", attended, resid_low, preferred_element_type=jnp.float32)
    out_share = scatter_columns(out_w_grad)
    mixed_grad = (
        jnp.einsum("td,qd->tq", resid_low, full_out, preferred_element_type=jnp.float32)
        .astype(low)
        .reshape(tok_dev, KV, group_size, HD)
    )
    row_dot = jnp.sum(mixed_grad.astype(jnp.float32) * mixed, axis=-1)
    scores = (
        jnp.einsum("tkgd,nkd->tkgn", query_group, key_all, preferred_element_type=jnp.float32)
        * score_scale
    )
    probs = jnp.exp(jnp.where(allowed, scores - log_total[..., None], neg_large))
    prob_grad = jnp.einsum(
        "tkgd,nkd->tkgn", mixed_grad, value_all, preferred_element_type=jnp.float32
    )
    score_grad = (probs * (prob_grad - row_dot[..., None])).astype(low)
    query_rot = (
        jnp.einsum("tkgn,nkd->tkgd", score_grad, key_all, preferred_element_type=jnp.float32)
        * score_scale
    )
    key_rot = (
        jnp.einsum("tkgn,tkgd->nkd", score_grad, query_group, preferred_element_type=jnp.float32)
        * score_scale
    )
    value_rot = jnp.einsum(
        "tkgn,tkgd->nkd", probs.astype(low), mixed_grad, preferred_element_type=jnp.float32
    )
    kv_partial = jnp.concatenate(
        [key_rot.reshape(total_keys, width_kv), value_rot.reshape(total_keys, width_kv)], axis=1
    ).astype(low)
    kv_share = scatter_tokens(kv_partial, token_bounds, orders3, all_axes).astype(jnp.float32)
    query_grad = rope_back(query_rot.reshape(tok_dev, H, HD), cosine, sine_table)
    key_grad_own = rope_back(
        kv_share[:, :width_kv].reshape(tok_dev, KV, HD), cosine, sine_table
    )
    proj_grad = jnp.concatenate(
        [
            query_grad.reshape(tok_dev, width_q),
            key_grad_own.reshape(tok_dev, width_kv),
            kv_share[:, width_kv:],
        ],
        axis=1,
    )
    bias_grad = jnp.sum(proj_grad, axis=0)
    proj_low = proj_grad.astype(low)
    qkv_w_grad = jnp.einsum("td,tc->dc", normed, proj_low, preferred_element_type=jnp.float32)
    qkv_share = scatter_columns(qkv_w_grad)
    normed_grad = jnp.einsum("tc,dc->td", proj_low, full_qkv, preferred_element_type=jnp.float32)
    input_part, attn_gain_grad = norm_back(hidden_in, full_attn_gain, normed_grad)
    input_grad = resid_grad + input_part

    small = [
        bias_grad[: width_q + width_kv],
        bias_grad[width_q + width_kv :],
        attn_gain_grad,
        mlp_gain_grad,
    ]
    small = jnp.concatenate([s.reshape(devices, -1) for s in small], axis=1)
    sizes = ((width_q + width_kv) // devices, width_kv // devices, rows_w, rows_w)
    small = jnp.pad(small, ((0, 0), (0, -small.shape[1] % 128)))
    small = jnp.sum(
        lax.all_to_all(small, ("ctx", "fsdp"), split_axis=0, concat_axis=0, tiled=True), axis=0
    )
    vectors = []
    start = 0
    for count in sizes:
        vectors.append(small[start : start + count])
        start += count
    front_share, value_bias_share, attn_gain_share, mlp_gain_share = vectors
    return (
        layer_out.astype(low)[None],
        input_grad[None],
        qkv_share,
        front_share,
        value_bias_share,
        out_share,
        attn_gain_share,
        mlp_gain_share,
        gate_share,
        up_share,
        down_share,
    )


def solution(mesh):
    return jax.shard_map(
        shards,
        mesh=mesh,
        in_specs=(
            P("fsdp", "ctx", None),
            P("fsdp", None),
            P("fsdp", "ctx"),
            P("fsdp", "ctx"),
            P(("ctx", "fsdp"), None),
            P(("ctx", "fsdp")),
            P(("ctx", "fsdp"), None),
            P(("ctx", "fsdp")),
            P(("ctx", "fsdp")),
            P(("ctx", "fsdp"), None),
            P(("ctx", "fsdp"), None),
            P(("ctx", "fsdp"), None),
            P("fsdp", "ctx", None),
        ),
        out_specs=(
            P("fsdp", "ctx", None),
            P("fsdp", "ctx", None),
            P(("ctx", "fsdp"), None),
            P(("ctx", "fsdp")),
            P(("ctx", "fsdp")),
            P(("ctx", "fsdp"), None),
            P(("ctx", "fsdp")),
            P(("ctx", "fsdp")),
            P(("ctx", "fsdp"), None),
            P(("ctx", "fsdp"), None),
            P(("ctx", "fsdp"), None),
        ),
        check_vma=False,
    )
```

time: 2680 us -> 845 us (0.32)
  waiting for transfers between devices: 2300 us -> 320 us
  starting transfers between devices: 0.73 us -> 223 us
  matrix products: 226 us -> 91.8 us
  other arithmetic: 22 us -> 106 us
  blocking collectives: 80.3 us -> 0 us
  local copies, waits for them, and re-layouts: 29.9 us -> 88.6 us
    reduce_scatter x5 -> x0, waiting for transfers between devices: 1190 us -> none  [the longest x1 779 us: shards(): lax.psum_scatter(jnp.einsum('td,tf->df', columns, both_grads, preferred_e...]
    all_gather x7 -> x0, waiting for transfers between devices: 642 us -> none  [the longest x1 164 us: shards(): lax.all_gather(gate_weight, ('ctx', 'fsdp'), axis=0, tiled=True)]
    unnamed x14 -> x0, waiting for transfers between devices: 473 us -> none
    ppermute x0 -> x142, waiting for transfers between devices: none -> 320 us  [the longest x126 320 us: shift(): return lax.ppermute(values, 'ctx', pairs)]
    ppermute x0 -> x142, starting transfers between devices: none -> 210 us  [the longest x126 207 us: shift(): return lax.ppermute(values, 'ctx', pairs)]
    dot_general x23 -> x15, matrix products: 211 us -> 87.6 us  [the longest x1 12 us: shards(): gate_up_pre = jnp.dot(mlp_all, gate_up, preferred_element_type=jnp.float32)]
    unnamed x2 -> x0, blocking collectives: 80.3 us -> none
    concatenate x0 -> x42, other arithmetic: none -> 43.1 us  [the longest x17 17.7 us: gather_axis(): return jnp.concatenate(pieces, axis=axis)]
  transfers between devices with their start and end apart: 13 -> 145, of which waited for: 13 -> 73; matrix products, arithmetic and copies ran while one was open for 7% -> 26% of each run, Pallas kernels for 0% -> 0%
where the time goes in v1:
time: 845 us; the launch traced here: 834 us
  waiting for transfers between devices  320 us (38%)
  starting transfers between devices  223 us (26%)
  other arithmetic  106 us (13%)
  matrix products  91.8 us (11%)
  local copies, waits for them, and re-layouts  88.6 us (10%)
    ppermute x126, waiting for transfers between devices, shift(): return lax.ppermute(values, 'ctx', pairs)  320 us
    ppermute x126, starting transfers between devices, shift(): return lax.ppermute(values, 'ctx', pairs)  207 us
    concatenate x17, other arithmetic, gather_axis(): return jnp.concatenate(pieces, axis=axis)  17.7 us
  transfers between devices with their start and end apart: 145, of which 73 were waited for; matrix products, arithmetic and copies ran while one was open for 26% of the time, Pallas kernels for 0%

profile of v1, /device:TPU:0, one launch (start us, length us, event | category | flops | bytes accessed | tf_op | source)
XLA Modules:
  0.0 834.3 jit_solution(4986478285935550936)
XLA Ops:
  37.8 4.5 collective-permute-done.6
  43.8 19.1 %collective-permute-done.46 = bf16[1,1,1,1,48,512]{5,4,3,2,1,0:T(8,128)(2,1)S(1)} collective-permute-done((bf16[1,1,1,1,48,512]{5,4,3,2,1,0:T(8,128)(2,1)S(1)}, bf16[1,1,1,1,48,512]{5,4,3,2,1,0:T(8,128)(2,1)S(1)}, u32[]{:S(2)}, u32[]{:S(2)}) %collective-permute-start.46) | collective-permute-done | bytes 49184 | tf_op jit(solution)/shard_map/ppermute | solution.py:96
  62.9 6.9 collective-permute-start.47
  87.2 6.2 collective-permute-done.14
  94.4 5.6 collective-permute-done.41
  101.6 5.9 collective-permute-done.42
  107.7 8.3 collective-permute-done.8
  117.9 5.1 collective-permute-done.9
  123.1 9.4 %collective-permute-done.36 = bf16[1,2,2,1,48,512]{5,4,3,2,1,0:T(8,128)(2,1)S(1)} collective-permute-done((bf16[1,2,2,1,48,512]{5,4,3,2,1,0:T(8,128)(2,1)S(1)}, bf16[1,2,2,1,48,512]{5,4,3,2,1,0:T(8,128)(2,1)S(1)}, u32[]{:S(2)}, u32[]{:S(2)}) %collective-permute-start.36) | collective-permute-done | bytes 196640 | tf_op jit(solution)/shard_map/ppermute | solution.py:96
  133.0 9.1 %collective-permute-done.37 = bf16[1,2,2,1,48,512]{5,4,3,2,1,0:T(8,128)(2,1)S(1)} collective-permute-done((bf16[1,2,2,1,48,512]{5,4,3,2,1,0:T(8,128)(2,1)S(1)}, bf16[1,2,2,1,48,512]{5,4,3,2,1,0:T(8,128)(2,1)S(1)}, u32[]{:S(2)}, u32[]{:S(2)}) %collective-permute-start.37) | collective-permute-done | bytes 196640 | tf_op jit(solution)/shard_map/ppermute | solution.py:96
  147.6 8.0 collective-permute-done.72
  160.3 6.5 collective-permute-done.73
  243.1 5.8 collective-permute-done.22
  269.3 5.4 fusion.137
  275.9 16.0 %collective-permute-done.59 = bf16[4,2,1,1,48,2240]{5,4,3,2,1,0:T(8,128)(2,1)} collective-permute-done((bf16[4,2,1,1,48,2240]{5,4,3,2,1,0:T(8,128)(2,1)S(1)}, bf16[4,2,1,1,48,2240]{5,4,3,2,1,0:T(8,128)(2,1)}, u32[]{:S(2)}, u32[]{:S(2)}) %collective-permute-start.59) | collective-permute-done | bytes 1720352 | tf_op jit(solution)/shard_map/ppermute | solution.py:96
  296.6 8.9 %collective-permute-done.51 = bf16[1,1,1,80,1536]{4,3,2,1,0:T(8,128)(2,1)S(1)} collective-permute-done((bf16[1,1,1,80,1536]{4,3,2,1,0:T(8,128)(2,1)S(1)}, bf16[1,1,1,80,1536]{4,3,2,1,0:T(8,128)(2,1)S(1)}, u32[]{:S(2)}, u32[]{:S(2)}) %collective-permute-start.51) | collective-permute-done | bytes 245792 | tf_op jit(solution)/shard_map/ppermute | solution.py:96
  307.9 8.3 collective-permute-done.52
  322.5 5.3 collective-permute-done.53
  334.9 7.3 collective-permute-done.58
  343.4 5.8 collective-permute-done.54
  357.6 12.0 %fusion.29 = f32[1024,2240]{0,1:T(8,128)} fusion(bf16[1536,2240]{1,0:T(8,128)(2,1)} %bitcast.285, bf16[384,1536]{1,0:T(8,128)(2,1)S(1)} %bitcast.338, bf16[640,1536]{1,0:T(8,128)(2,1)S(1)} %bitcast.317), kind=kOutput, calls=%fused_computation.59 | convolution fusion | flops 7052722176 | bytes 19202048 | tf_op jit(solution)/shard_map/dot_general | solution.py:377
  369.6 10.4 %multiply_convert_fusion.1 = (bf16[1024,1120]{0,1:T(8,128)(2,1)}, bf16[1024,1120]{0,1:T(8,128)(2,1)}, bf16[1024,1120]{0,1:T(8,128)(2,1)S(1)}) fusion(f32[1024,2240]{0,1:T(8,128)} %fusion.29, bf16[1120,1536]{1,0:T(8,128)(2,1)S(1)} %bitcast.302, bf16[384,1536]{1,0:T(8,128)(2,1)S(1)} %bitcast.336, bf16[640,1536]{1,0:T(8,128)(2,1)S(1)} %bitcast.315), kind=kOutput, calls=%fused_computation.28 | convolution fusion | flops 3546710016 | bytes 22642688 | tf_op jit(solution)/shard_map/td,fd->tf/dot_general | solution.py:376
  380.0 4.6 convolution_convert_fusion.5
  384.7 9.8 %convolution_convert_fusion.4 = bf16[1024,1536]{1,0:T(8,128)(2,1)S(1)} fusion(bf16[1536,2240]{1,0:T(8,128)(2,1)S(1)} %bitcast.288, bf16[1024,1120]{0,1:T(8,128)(2,1)} %get-tuple-element.56, bf16[1024,1120]{0,1:T(8,128)(2,1)} %get-tuple-element.55), kind=kOutput, calls=%fused_computation.32 | convolution fusion | flops 7057178624 | bytes 14614528 | tf_op jit(solution)/shard_map/tf,df->td/dot_general | solution.py:387
  397.0 10.9 %convolution_convert_fusion = bf16[1536,2240]{0,1:T(8,128)(2,1)} fusion(bf16[1024,1120]{0,1:T(8,128)(2,1)} %get-tuple-element.56, bf16[1024,1120]{0,1:T(8,128)(2,1)S(1)} %copy-done.125, bf16[384,1536]{1,0:T(8,128)(2,1)S(1)} %bitcast.339, bf16[640,1536]{1,0:T(8,128)(2,1)S(1)} %bitcast.318), kind=kOutput, calls=%fused_computation.9 | convolution fusion | flops 7065337856 | bytes 14614528 | tf_op jit(solution)/shard_map/td,tf->df/dot_general | solution.py:398
  417.4 5.2 convolution_convert_fusion.1
  423.9 9.8 %copy.164 = bf16[1536,2240]{1,0:T(8,128)(2,1)} copy(bf16[1536,2240]{0,1:T(8,128)(2,1)} %convolution_convert_fusion) | data formatting | bytes 13762560 | tf_op jit(solution)/shard_map/convert_element_type | solution.py:399
  442.8 5.9 collective-permute-done.85
  448.8 5.8 collective-permute-done.69
  483.0 4.4 collective-permute-start.66
  496.7 8.8 %fusion.22 = bf16[2,128,2048]{2,1,0:T(8,128)(2,1)} fusion(bf16[128,2,6,128]{0,3,2,1:T(8,128)(2,1)S(1)} %bitcast.328, f32[2,2048,128,6]{2,1,3,0:T(8,128)} %copy-done, f32[128,2,6]{0,2,1:T(8,128)S(1)} %log_add_fusion, pred[128,2048]{0,1:T(8,128)(4,1)S(1)} %fusion.43), kind=kOutput, calls=%fused_computation.46 | convolution fusion | flops 818413568 | bytes 14292992 | tf_op jit(solution)/shard_map/tkgn,tkgd->nkd/dot_general | solution.py:449
  505.5 6.8 fusion.1
  562.4 4.6 collective-permute-done.98
  573.6 4.3 collective-permute-start.99
  602.8 5.5 fusion.64
  615.0 5.8 all-to-all-start.1
  647.4 7.2 collective-permute-done.133
  654.7 4.3 collective-permute-start.122
  662.2 4.3 collective-permute-start.128
  675.7 5.1 collective-permute-done.134
  688.2 4.3 collective-permute-start.135
  731.9 4.4 collective-permute-start.103
  740.1 4.3 collective-permute-start.104
  744.4 21.1 %collective-permute-done.109 = bf16[4,2,1,1,48,640]{5,4,3,2,1,0:T(8,128)(2,1)S(1)} collective-permute-done((bf16[4,2,1,1,48,640]{5,4,3,2,1,0:T(8,128)(2,1)S(1)}, bf16[4,2,1,1,48,640]{5,4,3,2,1,0:T(8,128)(2,1)S(1)}, u32[]{:S(2)}, u32[]{:S(2)}) %collective-permute-start.109) | collective-permute-done | bytes 491552 | tf_op jit(solution)/shard_map/ppermute | solution.py:96
  773.1 4.4 collective-permute-start.111
  797.3 4.9 collective-permute-done.106
  809.4 4.4 collective-permute-start.118
  813.8 9.3 %collective-permute-done.118 = bf16[1,1,1,1,48,768]{5,4,3,2,1,0:T(8,128)(2,1)S(1)} collective-permute-done((bf16[1,1,1,1,48,768]{5,4,3,2,1,0:T(8,128)(2,1)S(1)}, bf16[1,1,1,1,48,768]{5,4,3,2,1,0:T(8,128)(2,1)S(1)}, u32[]{:S(2)}, u32[]{:S(2)}) %collective-permute-start.118) | collective-permute-done | bytes 73760 | tf_op jit(solution)/shard_map/ppermute | solution.py:96
  (853 shorter events, 479.9 us)
Async XLA Ops:
  3.8 31.6 %collective-permute-start = (bf16[1,1,1,1,48,640]{5,4,3,2,1,0:T(8,128)(2,1)S(1)}, bf16[1,1,1,1,48,640]{5,4,3,2,1,0:T(8,128)(2,1)}, u32[]{:S(2)}, u32[]{:S(2)}) collective-permute-start(bf16[1,1,1,1,48,640]{5,4,3,2,1,0:T(8,128)(2,1)S(1)} %maximum_bitcast_fusion), channel_id=1, source_target_pairs={{0,2},{2,0},{4,6},{6,4},{8,10},{10,8},{12,14},{14,12},{16,18},{18,... | collective-permute-start | bytes 184328 | tf_op jit(solution)/shard_map/ppermute | solution.py:96
  8.3 25.2 %collective-permute-start.45 = (bf16[1,1,1,1,48,512]{5,4,3,2,1,0:T(8,128)(2,1)}, bf16[1,1,1,1,48,512]{5,4,3,2,1,0:T(8,128)(2,1)S(1)}, u32[]{:S(2)}, u32[]{:S(2)}) collective-permute-start(bf16[1,1,1,1,48,512]{5,4,3,2,1,0:T(8,128)(2,1)} %get-tuple-element.108), channel_id=1, source_target_pairs={{0,8},{2,10},{4,12},{6,14},{8,16},{10,18},{12,20},{14,22},{16,24},... | collective-permute-start | bytes 147464 | tf_op jit(solution)/shard_map/ppermute | solution.py:96
  9.8 20.6 %collective-permute-start.33 = (bf16[1,1,1,1,48,512]{5,4,3,2,1,0:T(8,128)(2,1)S(1)}, bf16[1,1,1,1,48,512]{5,4,3,2,1,0:T(8,128)(2,1)}, u32[]{:S(2)}, u32[]{:S(2)}) collective-permute-start(bf16[1,1,1,1,48,512]{5,4,3,2,1,0:T(8,128)(2,1)S(1)} %get-tuple-element.107), channel_id=1, source_target_pairs={{0,2},{2,0},{4,6},{6,4},{8,10},{10,8},{12,14},{14,12},{16,18},{18,... | collective-permute-start | bytes 147464 | tf_op jit(solution)/shard_map/ppermute | solution.py:96
  10.4 22.8 %collective-permute-start.39 = (bf16[1,1,1,1,48,512]{5,4,3,2,1,0:T(8,128)(2,1)S(1)}, bf16[1,1,1,1,48,512]{5,4,3,2,1,0:T(8,128)(2,1)S(1)}, u32[]{:S(2)}, u32[]{:S(2)}) collective-permute-start(bf16[1,1,1,1,48,512]{5,4,3,2,1,0:T(8,128)(2,1)S(1)} %get-tuple-element.109), channel_id=1, source_target_pairs={{0,4},{2,6},{4,0},{6,2},{8,12},{10,14},{12,8},{14,10},{16,20},{18,... | collective-permute-start | bytes 147464 | tf_op jit(solution)/shard_map/ppermute | solution.py:96
  13.5 61.3 %collective-permute-start.12 = (bf16[1,1,1,1,48,768]{5,4,3,2,1,0:T(8,128)(2,1)}, bf16[1,1,1,1,48,768]{5,4,3,2,1,0:T(8,128)(2,1)S(1)}, u32[]{:S(2)}, u32[]{:S(2)}) collective-permute-start(bf16[1,1,1,1,48,768]{5,4,3,2,1,0:T(8,128)(2,1)} %get-tuple-element.106), channel_id=1, source_target_pairs={{0,8},{2,10},{4,12},{6,14},{8,16},{10,18},{12,20},{14,22},{16,24},... | collective-permute-start | bytes 221192 | tf_op jit(solution)/shard_map/ppermute | solution.py:96
  21.3 229.4 %all-to-all-start = ((bf16[8,48,2240]{2,1,0:T(8,128)(2,1)}), bf16[8,48,2240]{2,1,0:T(8,128)(2,1)S(1)}, u32[]{:S(2)}, u32[]{:S(2)}) async-start(bf16[8,48,2240]{2,1,0:T(8,128)(2,1)} %copy.151), calls=%async_computation | async-start | bytes 3538944 | tf_op jit(solution)/shard_map/all_to_all | solution.py:357
  33.2 40.9 %collective-permute-start.75 = (bf16[1,1,1,48,1536]{4,3,2,1,0:T(8,128)(2,1)S(1)}, bf16[1,1,1,48,1536]{4,3,2,1,0:T(8,128)(2,1)S(1)}, u32[]{:S(2)}, u32[]{:S(2)}) collective-permute-start(bf16[1,1,1,48,1536]{4,3,2,1,0:T(8,128)(2,1)S(1)} %slice_bitcast_fusion.5), channel_id=1, source_target_pairs={{0,4},{2,6},{4,0},{6,2},{8,12},{10,14},{12,8},{14,10},{16,20},{18,... | collective-permute-start | bytes 442376 | tf_op jit(solution)/shard_map/ppermute | solution.py:96
  33.4 110.4 %collective-permute-start.71 = (bf16[1,1,1,80,1536]{4,3,2,1,0:T(8,128)(2,1)S(1)}, bf16[1,1,1,80,1536]{4,3,2,1,0:T(8,128)(2,1)S(1)}, u32[]{:S(2)}, u32[]{:S(2)}) collective-permute-start(bf16[1,1,1,80,1536]{4,3,2,1,0:T(8,128)(2,1)S(1)} %slice_bitcast_fusion.3), channel_id=1, source_target_pairs={{0,8},{2,10},{4,12},{6,14},{8,16},{10,18},{12,20},{14,22},{16,24},... | collective-permute-start | bytes 737288 | tf_op jit(solution)/shard_map/ppermute | solution.py:96
  35.4 27.5 %collective-permute-start.46 = (bf16[1,1,1,1,48,512]{5,4,3,2,1,0:T(8,128)(2,1)S(1)}, bf16[1,1,1,1,48,512]{5,4,3,2,1,0:T(8,128)(2,1)S(1)}, u32[]{:S(2)}, u32[]{:S(2)}) collective-permute-start(bf16[1,1,1,1,48,512]{5,4,3,2,1,0:T(8,128)(2,1)S(1)} %collective-permute-done.45), channel_id=1, source_target_pairs={{0,8},{2,10},{4,12},{6,14},{8,16},{10,18},{12,20},{14,22},{16,24},... | collective-permute-start | bytes 147464 | tf_op jit(solution)/shard_map/ppermute | solution.py:96
  42.3 125.6 %collective-permute-start.61 = (bf16[1,1,1,1,280,1536]{5,4,3,2,1,0:T(8,128)(2,1)}, bf16[1,1,1,1,280,1536]{5,4,3,2,1,0:T(8,128)(2,1)S(1)}, u32[]{:S(2)}, u32[]{:S(2)}) collective-permute-start(bf16[1,1,1,1,280,1536]{5,4,3,2,1,0:T(8,128)(2,1)} %bitcast.49), channel_id=1, source_target_pairs={{0,2},{2,0},{4,6},{6,4},{8,10},{10,8},{12,14},{14,12},{16,18},{18,... | collective-permute-start | bytes 2580488 | tf_op jit(solution)/shard_map/ppermute | solution.py:96
  83.4 16.6 %collective-permute-start.7 = (bf16[1,2,1,1,48,768]{5,4,3,2,1,0:T(8,128)(2,1)S(1)}, bf16[1,2,1,1,48,768]{5,4,3,2,1,0:T(8,128)(2,1)S(1)}, u32[]{:S(2)}, u32[]{:S(2)}) collective-permute-start(bf16[1,2,1,1,48,768]{5,4,3,2,1,0:T(8,128)(2,1)S(1)} %fusion.85), channel_id=1, source_target_pairs={{0,8},{2,10},{4,12},{6,14},{8,16},{10,18},{12,20},{14,22},{16,24},... | collective-permute-start | bytes 442376 | tf_op jit(solution)/shard_map/ppermute | solution.py:96
  87.1 29.2 %collective-permute-start.35 = (bf16[1,2,2,1,48,512]{5,4,3,2,1,0:T(8,128)(2,1)S(1)}, bf16[1,2,2,1,48,512]{5,4,3,2,1,0:T(8,128)(2,1)S(1)}, u32[]{:S(2)}, u32[]{:S(2)}) collective-permute-start(bf16[1,2,2,1,48,512]{5,4,3,2,1,0:T(8,128)(2,1)S(1)} %fusion.81), channel_id=1, source_target_pairs={{0,8},{2,10},{4,12},{6,14},{8,16},{10,18},{12,20},{14,22},{16,24},... | collective-permute-start | bytes 589832 | tf_op jit(solution)/shard_map/ppermute | solution.py:96
  116.0 31.5 %collective-permute-start.76 = (bf16[1,2,1,48,1536]{4,3,2,1,0:T(8,128)(2,1)S(1)}, bf16[1,2,1,48,1536]{4,3,2,1,0:T(8,128)(2,1)S(1)}, u32[]{:S(2)}, u32[]{:S(2)}) collective-permute-start(bf16[1,2,1,48,1536]{4,3,2,1,0:T(8,128)(2,1)S(1)} %pad_maximum_fusion.44), channel_id=1, source_target_pairs={{0,8},{2,10},{4,12},{6,14},{8,16},{10,18},{12,20},{14,22},{16,24},... | collective-permute-start | bytes 884744 | tf_op jit(solution)/shard_map/ppermute | solution.py:96
  116.3 16.3 %collective-permute-start.15 = (bf16[4,1,1,1,48,768]{5,4,3,2,1,0:T(8,128)(2,1)S(1)}, bf16[4,1,1,1,48,768]{5,4,3,2,1,0:T(8,128)(2,1)S(1)}, u32[]{:S(2)}, u32[]{:S(2)}) collective-permute-start(bf16[4,1,1,1,48,768]{5,4,3,2,1,0:T(8,128)(2,1)S(1)} %constant_dynamic-slice_fusion.31), channel_id=1, source_target_pairs={{0,2},{2,0},{4,6},{6,4},{8,10},{10,8},{12,14},{14,12},{16,18},{18,... | collective-permute-start | bytes 884744 | tf_op jit(solution)/shard_map/ppermute | solution.py:96
  155.6 21.8 %collective-permute-start.77 = (bf16[1,2,1,48,1536]{4,3,2,1,0:T(8,128)(2,1)S(1)}, bf16[1,2,1,48,1536]{4,3,2,1,0:T(8,128)(2,1)}, u32[]{:S(2)}, u32[]{:S(2)}) collective-permute-start(bf16[1,2,1,48,1536]{4,3,2,1,0:T(8,128)(2,1)S(1)} %collective-permute-done.76), channel_id=1, source_target_pairs={{0,8},{2,10},{4,12},{6,14},{8,16},{10,18},{12,20},{14,22},{16,24},... | collective-permute-start | bytes 884744 | tf_op jit(solution)/shard_map/ppermute | solution.py:96
  156.3 22.2 %collective-permute-start.16 = (bf16[4,1,2,1,48,768]{5,4,3,2,1,0:T(8,128)(2,1)S(1)}, bf16[4,1,2,1,48,768]{5,4,3,2,1,0:T(8,128)(2,1)S(1)}, u32[]{:S(2)}, u32[]{:S(2)}) collective-permute-start(bf16[4,1,2,1,48,768]{5,4,3,2,1,0:T(8,128)(2,1)S(1)} %fusion.72), channel_id=1, source_target_pairs={{0,4},{2,6},{4,0},{6,2},{8,12},{10,14},{12,8},{14,10},{16,20},{18,... | collective-permute-start | bytes 1769480 | tf_op jit(solution)/shard_map/ppermute | solution.py:96
  158.8 16.4 %collective-permute-start.10 = (bf16[4,2,1,1,48,768]{5,4,3,2,1,0:T(8,128)(2,1)S(1)}, bf16[4,2,1,1,48,768]{5,4,3,2,1,0:T(8,128)(2,1)S(1)}, u32[]{:S(2)}, u32[]{:S(2)}) collective-permute-start(bf16[4,2,1,1,48,768]{5,4,3,2,1,0:T(8,128)(2,1)S(1)} %constant_dynamic-slice_fusion.32), channel_id=1, source_target_pairs={{0,2},{2,0},{4,6},{6,4},{8,10},{10,8},{12,14},{14,12},{16,18},{18,... | collective-permute-start | bytes 1769480 | tf_op jit(solution)/shard_map/ppermute | solution.py:96
  177.4 138.8 %collective-permute-start.74 = (bf16[4,1,1,80,1536]{4,3,2,1,0:T(8,128)(2,1)}, bf16[4,1,1,80,1536]{4,3,2,1,0:T(8,128)(2,1)}, u32[]{:S(2)}, u32[]{:S(2)}) collective-permute-start(bf16[4,1,1,80,1536]{4,3,2,1,0:T(8,128)(2,1)} %pad_maximum_fusion.33), channel_id=1, source_target_pairs={{0,4},{2,6},{4,0},{6,2},{8,12},{10,14},{12,8},{14,10},{16,20},{18,... | collective-permute-start | bytes 2949128 | tf_op jit(solution)/shard_map/ppermute | solution.py:96
  178.5 116.9 %collective-permute-start.78 = (bf16[1,2,1,48,1536]{4,3,2,1,0:T(8,128)(2,1)}, bf16[1,2,1,48,1536]{4,3,2,1,0:T(8,128)(2,1)}, u32[]{:S(2)}, u32[]{:S(2)}) collective-permute-start(bf16[1,2,1,48,1536]{4,3,2,1,0:T(8,128)(2,1)} %collective-permute-done.77), channel_id=1, source_target_pairs={{0,8},{2,10},{4,12},{6,14},{8,16},{10,18},{12,20},{14,22},{16,24},... | collective-permute-start | bytes 884744 | tf_op jit(solution)/shard_map/ppermute | solution.py:96
  248.9 80.2 %collective-permute-start.62 = (bf16[1,1,2,1,280,1536]{5,4,3,2,1,0:T(8,128)(2,1)}, bf16[1,1,2,1,280,1536]{5,4,3,2,1,0:T(8,128)(2,1)}, u32[]{:S(2)}, u32[]{:S(2)}) collective-permute-start(bf16[1,1,2,1,280,1536]{5,4,3,2,1,0:T(8,128)(2,1)} %fusion.31), channel_id=1, source_target_pairs={{0,1},{1,0},{2,3},{3,2},{4,5},{5,4},{6,7},{7,6},{8,9},{9,8},{10,11... | collective-permute-start | bytes 5160968 | tf_op jit(solution)/shard_map/ppermute | solution.py:159
  250.8 41.1 %collective-permute-start.59 = (bf16[4,2,1,1,48,2240]{5,4,3,2,1,0:T(8,128)(2,1)S(1)}, bf16[4,2,1,1,48,2240]{5,4,3,2,1,0:T(8,128)(2,1)}, u32[]{:S(2)}, u32[]{:S(2)}) collective-permute-start(bf16[4,2,1,1,48,2240]{5,4,3,2,1,0:T(8,128)(2,1)S(1)} %bitcast.268), channel_id=1, source_target_pairs={{0,2},{2,0},{4,6},{6,4},{8,10},{10,8},{12,14},{14,12},{16,18},{18,... | collective-permute-start | bytes 5160968 | tf_op jit(solution)/shard_map/ppermute | solution.py:96
  295.1 55.6 %collective-permute-start.60 = (bf16[4,2,2,1,48,2240]{5,4,3,2,1,0:T(8,128)(2,1)S(1)}, bf16[4,2,2,1,48,2240]{5,4,3,2,1,0:T(8,128)(2,1)S(1)}, u32[]{:S(2)}, u32[]{:S(2)}) collective-permute-start(bf16[4,2,2,1,48,2240]{5,4,3,2,1,0:T(8,128)(2,1)S(1)} %fusion.16), channel_id=1, source_target_pairs={{0,1},{1,0},{2,3},{3,2},{4,5},{5,4},{6,7},{7,6},{8,9},{9,8},{10,11... | collective-permute-start | bytes 10321928 | tf_op jit(solution)/shard_map/ppermute | solution.py:159
  327.9 21.3 %collective-permute-start.54 = (bf16[4,1,1,80,1536]{4,3,2,1,0:T(8,128)(2,1)S(1)}, bf16[4,1,1,80,1536]{4,3,2,1,0:T(8,128)(2,1)S(1)}, u32[]{:S(2)}, u32[]{:S(2)}) collective-permute-start(bf16[4,1,1,80,1536]{4,3,2,1,0:T(8,128)(2,1)S(1)} %pad_maximum_fusion.32), channel_id=1, source_target_pairs={{0,4},{2,6},{4,0},{6,2},{8,12},{10,14},{12,8},{14,10},{16,20},{18,... | collective-permute-start | bytes 2949128 | tf_op jit(solution)/shard_map/ppermute | solution.py:96
  395.4 16.0 %collective-permute-start.83 = (bf16[1,2,1,48,1536]{4,3,2,1,0:T(8,128)(2,1)S(1)}, bf16[1,2,1,48,1536]{4,3,2,1,0:T(8,128)(2,1)S(1)}, u32[]{:S(2)}, u32[]{:S(2)}) collective-permute-start(bf16[1,2,1,48,1536]{4,3,2,1,0:T(8,128)(2,1)S(1)} %bitcast.355), channel_id=1, source_target_pairs={{0,24},{2,26},{4,28},{6,30},{8,0},{10,2},{12,4},{14,6},{16,8},{18,... | collective-permute-start | bytes 884744 | tf_op jit(solution)/shard_map/ppermute | solution.py:96
  396.3 17.0 %collective-permute-start.67 = (bf16[1,2,1,48,1536]{4,3,2,1,0:T(8,128)(2,1)S(1)}, bf16[1,2,1,48,1536]{4,3,2,1,0:T(8,128)(2,1)S(1)}, u32[]{:S(2)}, u32[]{:S(2)}) collective-permute-start(bf16[1,2,1,48,1536]{4,3,2,1,0:T(8,128)(2,1)S(1)} %bitcast.354), channel_id=1, source_target_pairs={{0,24},{2,26},{4,28},{6,30},{8,0},{10,2},{12,4},{14,6},{16,8},{18,... | collective-permute-start | bytes 884744 | tf_op jit(solution)/shard_map/ppermute | solution.py:96
  410.3 45.5 %collective-permute-start.79 = (bf16[4,1,1,80,1536]{4,3,2,1,0:T(8,128)(2,1)}, bf16[4,1,1,80,1536]{4,3,2,1,0:T(8,128)(2,1)}, u32[]{:S(2)}, u32[]{:S(2)}) collective-permute-start(bf16[4,1,1,80,1536]{4,3,2,1,0:T(8,128)(2,1)} %slice.577), channel_id=1, source_target_pairs={{0,4},{2,6},{4,0},{6,2},{8,12},{10,14},{12,8},{14,10},{16,20},{18,... | collective-permute-start | bytes 2949128 | tf_op jit(solution)/shard_map/ppermute | solution.py:96
  412.2 25.6 %collective-permute-start.84 = (bf16[1,2,1,48,1536]{4,3,2,1,0:T(8,128)(2,1)}, bf16[1,2,1,48,1536]{4,3,2,1,0:T(8,128)(2,1)}, u32[]{:S(2)}, u32[]{:S(2)}) collective-permute-start(bf16[1,2,1,48,1536]{4,3,2,1,0:T(8,128)(2,1)} %add.929), channel_id=1, source_target_pairs={{0,24},{2,26},{4,28},{6,30},{8,0},{10,2},{12,4},{14,6},{16,8},{18,... | collective-permute-start | bytes 884744 | tf_op jit(solution)/shard_map/ppermute | solution.py:96
  414.1 24.8 %collective-permute-start.68 = (bf16[1,2,1,48,1536]{4,3,2,1,0:T(8,128)(2,1)}, bf16[1,2,1,48,1536]{4,3,2,1,0:T(8,128)(2,1)}, u32[]{:S(2)}, u32[]{:S(2)}) collective-permute-start(bf16[1,2,1,48,1536]{4,3,2,1,0:T(8,128)(2,1)} %add.919), channel_id=1, source_target_pairs={{0,24},{2,26},{4,28},{6,30},{8,0},{10,2},{12,4},{14,6},{16,8},{18,... | collective-permute-start | bytes 884744 | tf_op jit(solution)/shard_map/ppermute | solution.py:96
  435.2 23.0 %collective-permute-start.63 = (bf16[4,1,1,80,1536]{4,3,2,1,0:T(8,128)(2,1)S(1)}, bf16[4,1,1,80,1536]{4,3,2,1,0:T(8,128)(2,1)S(1)}, u32[]{:S(2)}, u32[]{:S(2)}) collective-permute-start(bf16[4,1,1,80,1536]{4,3,2,1,0:T(8,128)(2,1)S(1)} %slice.564), channel_id=1, source_target_pairs={{0,4},{2,6},{4,0},{6,2},{8,12},{10,14},{12,8},{14,10},{16,20},{18,... | collective-permute-start | bytes 2949128 | tf_op jit(solution)/shard_map/ppermute | solution.py:96
  437.7 49.6 %collective-permute-start.140 = (bf16[1,1,2,1,280,1536]{5,4,3,2,1,0:T(8,128)(2,1)S(1)}, bf16[1,1,2,1,280,1536]{5,4,3,2,1,0:T(8,128)(2,1)S(1)}, u32[]{:S(2)}, u32[]{:S(2)}) collective-permute-start(bf16[1,1,2,1,280,1536]{5,4,3,2,1,0:T(8,128)(2,1)S(1)} %constant_dynamic-slice_fusion), channel_id=1, source_target_pairs={{0,1},{1,0},{2,3},{3,2},{4,5},{5,4},{6,7},{7,6},{8,9},{9,8},{10,11... | collective-permute-start | bytes 5160968 | tf_op jit(solution)/shard_map/ppermute | solution.py:159
  448.7 277.8 %collective-permute-start.138 = (bf16[4,2,2,1,48,2240]{5,4,3,2,1,0:T(8,128)(2,1)}, bf16[4,2,2,1,48,2240]{5,4,3,2,1,0:T(8,128)(2,1)}, u32[]{:S(2)}, u32[]{:S(2)}) collective-permute-start(bf16[4,2,2,1,48,2240]{5,4,3,2,1,0:T(8,128)(2,1)} %constant_dynamic-slice_fusion.2), channel_id=1, source_target_pairs={{0,1},{1,0},{2,3},{3,2},{4,5},{5,4},{6,7},{7,6},{8,9},{9,8},{10,11... | collective-permute-start | bytes 10321928 | tf_op jit(solution)/shard_map/ppermute | solution.py:159
  488.6 148.3 %collective-permute-start.141 = (bf16[1,1,1,1,280,1536]{5,4,3,2,1,0:T(8,128)(2,1)}, bf16[1,1,1,1,280,1536]{5,4,3,2,1,0:T(8,128)(2,1)}, u32[]{:S(2)}, u32[]{:S(2)}) collective-permute-start(bf16[1,1,1,1,280,1536]{5,4,3,2,1,0:T(8,128)(2,1)} %constant_dynamic-slice_fusion.30), channel_id=1, source_target_pairs={{0,2},{2,0},{4,6},{6,4},{8,10},{10,8},{12,14},{14,12},{16,18},{18,... | collective-permute-start | bytes 2580488 | tf_op jit(solution)/shard_map/ppermute | solution.py:96
  525.8 19.7 %collective-permute-start.92 = (bf16[4,2,1,48,512]{4,3,2,1,0:T(8,128)(2,1)}, bf16[4,2,1,48,512]{4,3,2,1,0:T(8,128)(2,1)}, u32[]{:S(2)}, u32[]{:S(2)}) collective-permute-start(bf16[4,2,1,48,512]{4,3,2,1,0:T(8,128)(2,1)} %slice.595), channel_id=1, source_target_pairs={{0,2},{2,0},{4,6},{6,4},{8,10},{10,8},{12,14},{14,12},{16,18},{18,... | collective-permute-start | bytes 1179656 | tf_op jit(solution)/shard_map/ppermute | solution.py:96
  528.9 18.2 %collective-permute-start.97 = (bf16[4,1,2,48,512]{4,3,2,1,0:T(8,128)(2,1)}, bf16[4,1,2,48,512]{4,3,2,1,0:T(8,128)(2,1)}, u32[]{:S(2)}, u32[]{:S(2)}) collective-permute-start(bf16[4,1,2,48,512]{4,3,2,1,0:T(8,128)(2,1)} %slice.603), channel_id=1, source_target_pairs={{0,4},{2,6},{4,0},{6,2},{8,12},{10,14},{12,8},{14,10},{16,20},{18,... | collective-permute-start | bytes 1179656 | tf_op jit(solution)/shard_map/ppermute | solution.py:96
  545.4 80.7 %collective-permute-start.126 = (bf16[4,2,2,1,48,512]{5,4,3,2,1,0:T(8,128)(2,1)}, bf16[4,2,2,1,48,512]{5,4,3,2,1,0:T(8,128)(2,1)}, u32[]{:S(2)}, u32[]{:S(2)}) collective-permute-start(bf16[4,2,2,1,48,512]{5,4,3,2,1,0:T(8,128)(2,1)} %constant_dynamic-slice_fusion.10), channel_id=1, source_target_pairs={{0,1},{1,0},{2,3},{3,2},{4,5},{5,4},{6,7},{7,6},{8,9},{9,8},{10,11... | collective-permute-start | bytes 2359304 | tf_op jit(solution)/shard_map/ppermute | solution.py:159
  545.5 84.9 %collective-permute-start.120 = (bf16[4,2,2,1,48,512]{5,4,3,2,1,0:T(8,128)(2,1)}, bf16[4,2,2,1,48,512]{5,4,3,2,1,0:T(8,128)(2,1)}, u32[]{:S(2)}, u32[]{:S(2)}) collective-permute-start(bf16[4,2,2,1,48,512]{5,4,3,2,1,0:T(8,128)(2,1)} %constant_dynamic-slice_fusion.14), channel_id=1, source_target_pairs={{0,1},{1,0},{2,3},{3,2},{4,5},{5,4},{6,7},{7,6},{8,9},{9,8},{10,11... | collective-permute-start | bytes 2359304 | tf_op jit(solution)/shard_map/ppermute | solution.py:159
  601.9 25.6 %collective-permute-start.132 = (bf16[4,2,2,1,48,512]{5,4,3,2,1,0:T(8,128)(2,1)}, bf16[4,2,2,1,48,512]{5,4,3,2,1,0:T(8,128)(2,1)}, u32[]{:S(2)}, u32[]{:S(2)}) collective-permute-start(bf16[4,2,2,1,48,512]{5,4,3,2,1,0:T(8,128)(2,1)} %constant_dynamic-slice_fusion.6), channel_id=1, source_target_pairs={{0,1},{1,0},{2,3},{3,2},{4,5},{5,4},{6,7},{7,6},{8,9},{9,8},{10,11... | collective-permute-start | bytes 2359304 | tf_op jit(solution)/shard_map/ppermute | solution.py:159
  615.0 19.4 %all-to-all-start.1 = ((f32[32,1,256]{2,1,0:T(1,128)}), f32[32,1,256]{2,1,0:T(1,128)}, u32[]{:S(2)}, u32[]{:S(2)}) async-start(f32[32,1,256]{2,1,0:T(1,128)} %all_to_all.13), calls=%async_computation.1 | async-start | bytes 65536 | tf_op jit(solution)/shard_map/all_to_all | solution.py:486
  626.1 103.6 %collective-permute-start.102 = (bf16[4,2,2,1,48,640]{5,4,3,2,1,0:T(8,128)(2,1)}, bf16[4,2,2,1,48,640]{5,4,3,2,1,0:T(8,128)(2,1)}, u32[]{:S(2)}, u32[]{:S(2)}) collective-permute-start(bf16[4,2,2,1,48,640]{5,4,3,2,1,0:T(8,128)(2,1)} %constant_dynamic-slice_fusion.26), channel_id=1, source_target_pairs={{0,1},{1,0},{2,3},{3,2},{4,5},{5,4},{6,7},{7,6},{8,9},{9,8},{10,11... | collective-permute-start | bytes 2949128 | tf_op jit(solution)/shard_map/ppermute | solution.py:159
  627.5 108.8 %collective-permute-start.108 = (bf16[4,2,2,1,48,640]{5,4,3,2,1,0:T(8,128)(2,1)}, bf16[4,2,2,1,48,640]{5,4,3,2,1,0:T(8,128)(2,1)}, u32[]{:S(2)}, u32[]{:S(2)}) collective-permute-start(bf16[4,2,2,1,48,640]{5,4,3,2,1,0:T(8,128)(2,1)} %constant_dynamic-slice_fusion.22), channel_id=1, source_target_pairs={{0,1},{1,0},{2,3},{3,2},{4,5},{5,4},{6,7},{7,6},{8,9},{9,8},{10,11... | collective-permute-start | bytes 2949128 | tf_op jit(solution)/shard_map/ppermute | solution.py:159
  646.1 92.4 %collective-permute-start.114 = (bf16[4,2,2,1,48,768]{5,4,3,2,1,0:T(8,128)(2,1)S(1)}, bf16[4,2,2,1,48,768]{5,4,3,2,1,0:T(8,128)(2,1)S(1)}, u32[]{:S(2)}, u32[]{:S(2)}) collective-permute-start(bf16[4,2,2,1,48,768]{5,4,3,2,1,0:T(8,128)(2,1)S(1)} %copy-done.67), channel_id=1, source_target_pairs={{0,1},{1,0},{2,3},{3,2},{4,5},{5,4},{6,7},{7,6},{8,9},{9,8},{10,11... | collective-permute-start | bytes 3538952 | tf_op jit(solution)/shard_map/ppermute | solution.py:159
  729.1 57.1 %collective-permute-start.139 = (bf16[4,2,1,1,48,2240]{5,4,3,2,1,0:T(8,128)(2,1)S(1)}, bf16[4,2,1,1,48,2240]{5,4,3,2,1,0:T(8,128)(2,1)S(1)}, u32[]{:S(2)}, u32[]{:S(2)}) collective-permute-start(bf16[4,2,1,1,48,2240]{5,4,3,2,1,0:T(8,128)(2,1)S(1)} %constant_dynamic-slice_fusion.1), channel_id=1, source_target_pairs={{0,2},{2,0},{4,6},{6,4},{8,10},{10,8},{12,14},{14,12},{16,18},{18,... | collective-permute-start | bytes 5160968 | tf_op jit(solution)/shard_map/ppermute | solution.py:96
  737.7 27.8 %collective-permute-start.109 = (bf16[4,2,1,1,48,640]{5,4,3,2,1,0:T(8,128)(2,1)S(1)}, bf16[4,2,1,1,48,640]{5,4,3,2,1,0:T(8,128)(2,1)S(1)}, u32[]{:S(2)}, u32[]{:S(2)}) collective-permute-start(bf16[4,2,1,1,48,640]{5,4,3,2,1,0:T(8,128)(2,1)S(1)} %constant_dynamic-slice_fusion.21), channel_id=1, source_target_pairs={{0,2},{2,0},{4,6},{6,4},{8,10},{10,8},{12,14},{14,12},{16,18},{18,... | collective-permute-start | bytes 1474568 | tf_op jit(solution)/shard_map/ppermute | solution.py:96
  740.1 37.4 %collective-permute-start.104 = (bf16[1,2,2,1,48,640]{5,4,3,2,1,0:T(8,128)(2,1)S(1)}, bf16[1,2,2,1,48,640]{5,4,3,2,1,0:T(8,128)(2,1)S(1)}, u32[]{:S(2)}, u32[]{:S(2)}) collective-permute-start(bf16[1,2,2,1,48,640]{5,4,3,2,1,0:T(8,128)(2,1)S(1)} %dynamic-slice_add_fusion.14), channel_id=1, source_target_pairs={{0,24},{2,26},{4,28},{6,30},{8,0},{10,2},{12,4},{14,6},{16,8},{18,... | collective-permute-start | bytes 737288 | tf_op jit(solution)/shard_map/ppermute | solution.py:96
  770.4 24.1 %collective-permute-start.115 = (bf16[4,1,2,1,48,768]{5,4,3,2,1,0:T(8,128)(2,1)}, bf16[4,1,2,1,48,768]{5,4,3,2,1,0:T(8,128)(2,1)}, u32[]{:S(2)}, u32[]{:S(2)}) collective-permute-start(bf16[4,1,2,1,48,768]{5,4,3,2,1,0:T(8,128)(2,1)} %constant_dynamic-slice_fusion.17), channel_id=1, source_target_pairs={{0,4},{2,6},{4,0},{6,2},{8,12},{10,14},{12,8},{14,10},{16,20},{18,... | collective-permute-start | bytes 1769480 | tf_op jit(solution)/shard_map/ppermute | solution.py:96
  787.7 40.6 %all-to-all-start.2 = ((bf16[8,48,2240]{2,1,0:T(8,128)(2,1)}), bf16[8,48,2240]{2,1,0:T(8,128)(2,1)S(1)}, u32[]{:S(2)}, u32[]{:S(2)}) async-start(bf16[8,48,2240]{2,1,0:T(8,128)(2,1)} %bitcast.112), calls=%async_computation.2 | async-start | bytes 3538944 | tf_op jit(solution)/shard_map/all_to_all | solution.py:404
  797.1 16.7 %collective-permute-start.113 = (bf16[1,1,1,1,48,640]{5,4,3,2,1,0:T(8,128)(2,1)S(1)}, bf16[1,1,1,1,48,640]{5,4,3,2,1,0:T(8,128)(2,1)S(1)}, u32[]{:S(2)}, u32[]{:S(2)}) collective-permute-start(bf16[1,1,1,1,48,640]{5,4,3,2,1,0:T(8,128)(2,1)S(1)} %constant_dynamic-slice_fusion.19), channel_id=1, source_target_pairs={{0,4},{2,6},{4,0},{6,2},{8,12},{10,14},{12,8},{14,10},{16,20},{18,... | collective-permute-start | bytes 184328 | tf_op jit(solution)/shard_map/ppermute | solution.py:96
  806.0 17.3 %collective-permute-start.107 = (bf16[1,1,1,1,48,640]{5,4,3,2,1,0:T(8,128)(2,1)S(1)}, bf16[1,1,1,1,48,640]{5,4,3,2,1,0:T(8,128)(2,1)S(1)}, u32[]{:S(2)}, u32[]{:S(2)}) collective-permute-start(bf16[1,1,1,1,48,640]{5,4,3,2,1,0:T(8,128)(2,1)S(1)} %constant_dynamic-slice_fusion.23), channel_id=1, source_target_pairs={{0,2},{2,0},{4,6},{6,4},{8,10},{10,8},{12,14},{14,12},{16,18},{18,... | collective-permute-start | bytes 184328 | tf_op jit(solution)/shard_map/ppermute | solution.py:96
  (227 other events, 2568.2 us)

commit v2 on v1

v2 whole, which is shorter than its diff:
```python
import itertools

import jax
import jax.numpy as jnp
from jax import lax
from jax.experimental import pallas as pl
from jax.experimental.pallas import tpu as pltpu
from jax.sharding import PartitionSpec as P

H = 12
KV = 2
HD = 128
BLOCKS_DEV = 2
CONT_LEN = 1024


epsilon = 1e-06
rope_base = 1000000.0
neg_large = -1e30
low = jnp.bfloat16


def rms_scale(values):
    return values * lax.rsqrt(jnp.mean(values * values, axis=-1, keepdims=True) + epsilon)


def norm_back(values, gain, incoming):
    inverse = lax.rsqrt(jnp.mean(values * values, axis=-1, keepdims=True) + epsilon)
    normal = values * inverse
    gain_grad = jnp.sum(incoming * normal, axis=0)
    scaled = incoming * gain
    return (
        inverse * (scaled - normal * jnp.mean(scaled * normal, axis=-1, keepdims=True)),
        gain_grad,
    )


def rope_tables(position):
    half_dim = HD // 2
    frequency = jnp.exp(-jnp.log(rope_base) * (2.0 * jnp.arange(half_dim, dtype=jnp.float32) / HD))
    angles = position.astype(jnp.float32)[:, None] * frequency[None, :]
    return (
        jnp.concatenate([jnp.cos(angles)] * 2, axis=-1),
        jnp.concatenate([jnp.sin(angles)] * 2, axis=-1),
    )


def rotate_half(values):
    half_dim = values.shape[-1] // 2
    return jnp.concatenate([-values[..., half_dim:], values[..., :half_dim]], axis=-1)


def apply_rope(values, cosine, sine_table):
    return values * cosine[:, None, :] + rotate_half(values) * sine_table[:, None, :]


def rope_back(incoming, cosine, sine_table):
    return incoming * cosine[:, None, :] - rotate_half(incoming * sine_table[:, None, :])


def visible_pairs(query_seq, query_pos, key_seq, key_pos):
    same_seq = key_seq[None, :] == query_seq[:, None]
    seen = (key_seq[None, :] == 0) | same_seq
    return seen & (~same_seq | (key_pos[None, :] <= query_pos[:, None]))


def key_meta(deal_row, row_ids, block_len, prompt_len):
    slots = row_ids // block_len
    matches = slots[:, None] == jnp.arange(deal_row.shape[0], dtype=jnp.int32)[None, :]
    picked = jnp.sum(jnp.where(matches, deal_row[None, :], 0), axis=1)
    place = picked * block_len + row_ids % block_len
    key_seq = jnp.where(place < prompt_len, 0, 1 + (place - prompt_len) // CONT_LEN)
    key_pos = jnp.where(place < prompt_len, place, prompt_len + (place - prompt_len) % CONT_LEN)
    return (key_seq, key_pos)


def axes_of(size):
    return {16: (4, 2, 2), 64: (2, 4, 4, 2)}.get(size, (size,))


def dot_nn(a, b):
    return lax.dot_general(a, b, (((1,), (0,)), ((), ())), preferred_element_type=jnp.float32)


def dot_nt(a, b):
    return lax.dot_general(a, b, (((1,), (1,)), ((), ())), preferred_element_type=jnp.float32)


def dot_tn(a, b):
    return lax.dot_general(a, b, (((0,), (0,)), ((), ())), preferred_element_type=jnp.float32)


def ff_tile(tokens, cots, gate, up, down):
    gate_pre = dot_nn(tokens, gate)
    up_pre = dot_nn(tokens, up)
    hidden_grad = dot_nt(cots, down)
    sigmoid_gate = jax.nn.sigmoid(gate_pre)
    gate_act = gate_pre * sigmoid_gate
    hidden = (gate_act * up_pre).astype(low)
    gate_grad = hidden_grad * up_pre * sigmoid_gate * (1.0 + gate_pre * (1.0 - sigmoid_gate))
    return hidden, gate_grad.astype(low), (hidden_grad * gate_act).astype(low)


def of_matrix(parts, which):
    return jnp.concatenate([p[:, which].reshape(-1, p.shape[-1]) for p in parts], axis=0)


def ff_kernel(tokens, cots, w0, w1, w2, w3, down, token_grad, out, d0, d1, d2, d3, down_grad, token_total, out_total):
    step = pl.program_id(0)
    weights = [w[...] for w in (w0, w1, w2, w3)]
    gate, up = of_matrix(weights, 0), of_matrix(weights, 1)
    hidden, gate_grad, up_grad = ff_tile(tokens[...], cots[...], gate, up, down[...])

    @pl.when(step == 0)
    def _():
        token_total[...] = jnp.zeros_like(token_total)
        out_total[...] = jnp.zeros_like(out_total)

    token_total[...] += dot_nt(gate_grad, gate) + dot_nt(up_grad, up)
    out_total[...] += dot_nn(hidden, down[...])
    for which, grad in ((0, gate_grad), (1, up_grad)):
        full = dot_tn(tokens[...], grad).astype(low)
        start = 0
        for d in (d0, d1, d2, d3):
            rows = d.shape[0] * d.shape[2]
            d[:, which] = full[start : start + rows].reshape(d.shape[0], d.shape[2], d.shape[3])
            start += rows
    down_grad[...] = dot_tn(hidden, cots[...]).astype(low)

    @pl.when(step == pl.num_programs(0) - 1)
    def _():
        token_grad[...] = token_total[...].astype(low)
        out[...] = out_total[...].astype(low)


def feed_forward(tokens, cots, weights, down):
    count, width = tokens.shape
    columns = down.shape[0]
    tile = 256
    if count > 1024 or columns % tile:
        gate, up = of_matrix(weights, 0), of_matrix(weights, 1)
        hidden, gate_grad, up_grad = ff_tile(tokens, cots, gate, up, down)
        grads = [dot_tn(tokens, g).astype(low) for g in (gate_grad, up_grad)]
        parts = []
        start = 0
        for w in weights:
            rows = w.shape[0] * w.shape[2]
            pair = [g[start : start + rows].reshape(w.shape[0], 1, *w.shape[2:]) for g in grads]
            parts.append(jnp.concatenate(pair, axis=1))
            start += rows
        return (
            (dot_nt(gate_grad, gate) + dot_nt(up_grad, up)).astype(low),
            dot_nn(hidden, down).astype(low),
            *parts,
            dot_tn(hidden, cots).astype(low),
        )
    whole = pl.BlockSpec((count, width), lambda i: (0, 0))
    pieces, _, rows, _ = weights[0].shape
    by_columns = pl.BlockSpec((pieces, 2, rows, tile), lambda i: (0, 0, 0, i))
    by_rows = pl.BlockSpec((tile, width), lambda i: (i, 0))
    wide = jax.ShapeDtypeStruct((count, width), low)
    long = jax.ShapeDtypeStruct(weights[0].shape, low)
    return pl.pallas_call(
        ff_kernel,
        grid=(columns // tile,),
        in_specs=[whole, whole] + [by_columns] * 4 + [by_rows],
        out_specs=[whole, whole] + [by_columns] * 4 + [by_rows],
        out_shape=[wide, wide] + [long] * 4 + [jax.ShapeDtypeStruct((columns, width), low)],
        scratch_shapes=[pltpu.VMEM((count, width), jnp.float32)] * 2,
        compiler_params=pltpu.CompilerParams(
            dimension_semantics=("arbitrary",), vmem_limit_bytes=50 * 1024 * 1024
        ),
        cost_estimate=pl.CostEstimate(
            flops=18 * count * width * columns,
            bytes_accessed=12 * width * columns + 12 * count * width,
            transcendentals=count * columns,
        ),
    )(tokens, cots, *weights, down)


class Grid:
    def __init__(self, size):
        self.size = size
        self.axes = axes_of(size)
        self.rank = len(self.axes)
        self.strides = []
        step = size
        for extent in self.axes:
            step //= extent
            self.strides.append(step)
        index = lax.axis_index("ctx")
        self.place = [(index // s) % e for s, e in zip(self.strides, self.axes)]

    def hop(self, values, moves):
        pairs = []
        for i in range(self.size):
            to = i
            for axis, by in moves.items():
                digit = (i // self.strides[axis]) % self.axes[axis]
                to += (((digit + by) % self.axes[axis]) - digit) * self.strides[axis]
            pairs.append((i, to))
        return lax.ppermute(values, "ctx", pairs)

    def offsets(self, axes):
        return list(itertools.product(*[range(self.axes[a]) for a in axes]))

    def gather_stage(self, values, axes):
        pieces = {}
        for offs in self.offsets(axes):
            pieces[offs] = self.hop(values, dict(zip(axes, offs))) if any(offs) else values

        def join(prefix):
            depth = len(prefix)
            if depth == len(axes):
                return pieces[prefix]
            return jnp.concatenate(
                [join(prefix + (j,)) for j in range(self.axes[axes[depth]])], axis=axes[depth]
            )

        return join(())

    def scatter_stage(self, values, axes, absolute):
        def take(offs):
            part = values
            for axis, back in zip(axes, offs):
                if absolute:
                    spot = (self.place[axis] - back + self.axes[axis]) % self.axes[axis]
                    part = lax.dynamic_slice_in_dim(part, spot, 1, axis=axis)
                else:
                    part = lax.slice_in_dim(part, back, back + 1, axis=axis)
            return part

        total = None
        arrived = []
        for offs in self.offsets(axes):
            part = take(offs)
            if any(offs):
                part = self.hop(part, {a: -o for a, o in zip(axes, offs)})
            arrived.append(part)
        total = arrived[0].astype(jnp.float32)
        for part in arrived[1:]:
            total = total + part.astype(jnp.float32)
        return total.astype(values.dtype)

    def gather(self, parts, orders):
        for stage in range(len(orders[0])):
            (parts,) = together(parts)
            parts = [self.gather_stage(p, o[stage]) for p, o in zip(parts, orders)]
        return parts

    def scatter_round(self, parts, orders, stage, absolute):
        return [
            self.scatter_stage(p, o[len(o) - 1 - stage], absolute) for p, o in zip(parts, orders)
        ]

    def ordered(self, values, axis):
        extent = self.axes[axis]
        wheel = [lax.slice_in_dim(values, j, j + 1, axis=axis) for j in range(extent)]
        wheel = jnp.concatenate(wheel[::-1] + wheel[:0:-1], axis=axis)
        return lax.dynamic_slice_in_dim(wheel, extent - 1 - self.place[axis], extent, axis=axis)

    def source_rows(self, first, count, over):
        index = jnp.int32(0)
        for axis in range(self.rank):
            if axis in over:
                back = jnp.arange(self.axes[axis], dtype=jnp.int32)
            else:
                back = jnp.zeros((1,), jnp.int32)
            digit = (self.place[axis] - back + self.axes[axis]) % self.axes[axis]
            shape = [1] * self.rank
            shape[axis] = digit.shape[0]
            index = index + digit.reshape(shape) * self.strides[axis]
        return index[..., None], first + jnp.arange(count, dtype=jnp.int32)


def together(*groups):
    flat = [v for g in groups for v in (g if isinstance(g, list) else [g])]
    flat = list(lax.optimization_barrier(tuple(flat)))
    out = []
    for g in groups:
        if isinstance(g, list):
            out.append([flat.pop(0) for _ in g])
        else:
            out.append(flat.pop(0))
    return out


def other_core(values):
    return lax.ppermute(values, "fsdp", [(0, 1), (1, 0)])


def both_cores(values, core, axis):
    other = other_core(values)
    first = jnp.where(core == 0, values, other)
    second = jnp.where(core == 0, other, values)
    return jnp.concatenate([first, second], axis=axis)


def own_core_sum(values, core, axis):
    mine = lax.dynamic_slice_in_dim(values, core, 1, axis=axis)
    theirs = lax.dynamic_slice_in_dim(values, 1 - core, 1, axis=axis)
    return mine + other_core(theirs)


def shards(
    tokens_in,
    deal_table,
    cont_id,
    position,
    qkv_weight,
    qkv_bias,
    out_weight,
    attn_gain,
    mlp_gain,
    gate_weight,
    up_weight,
    down_weight,
    cotangent,
):
    ctx_size = lax.axis_size("ctx")
    devices = 2 * ctx_size
    core = lax.axis_index("fsdp")
    grid = Grid(ctx_size)
    all_axes = tuple(range(grid.rank))
    tok_dev, width = tokens_in.shape[1], tokens_in.shape[2]
    block_len = tok_dev // BLOCKS_DEV
    prompt_len = tok_dev * ctx_size // 2
    group_size = H // KV
    score_scale = HD ** (-0.5)
    width_q = H * HD
    width_kv = KV * HD
    deal_row = deal_table[0]
    query_seq = cont_id[0]
    query_pos = position[0]
    hidden_in = tokens_in[0].astype(jnp.float32)
    rows_w = qkv_weight.shape[0]

    ff_axes = (0,) if grid.rank == 3 else all_axes
    far_axes = tuple(a for a in all_axes if a not in ff_axes)
    ff_size = 1
    for a in ff_axes:
        ff_size *= grid.axes[a]
    far_size = ctx_size // ff_size
    ff_total = gate_weight.shape[1]
    ff_cols = ff_total // ff_size
    ff_room = -(-ff_cols // 256) * 256
    members = {}
    for i in range(ctx_size):
        key = tuple((i // grid.strides[a]) % grid.axes[a] for a in far_axes)
        members.setdefault(key, []).append(i)
    groups = [members[k] for k in sorted(members)]

    if grid.rank == 3:
        wide_orders = [((0,), (1, 2))]
        ff_orders = [((0,),)]
        far_orders = [((1,), (2,)), ((2,), (1,))]
    else:
        wide_orders = [tuple((a,) for a in all_axes)]
        ff_orders = wide_orders[:1]
        far_orders = [(), ()]
    weight_order = wide_orders[:1]
    token_bounds = [0, tok_dev]
    ff_bounds = [0, tok_dev]
    far_shape = tuple(grid.axes[a] for a in far_axes)
    spots = ((core - jnp.arange(2, dtype=jnp.int32)) % 2) * rows_w
    spots = spots.reshape((2,) + (1,) * (len(far_axes) + 3))
    for slot, a in enumerate(far_axes):
        digit = (grid.place[a] - jnp.arange(grid.axes[a], dtype=jnp.int32)) % grid.axes[a]
        shape = [1] * (len(far_axes) + 4)
        shape[slot + 2] = grid.axes[a]
        spots = spots + digit.reshape(shape) * (grid.strides[a] * 2 * rows_w)
    steps = [0]
    for a in ff_axes:
        steps = [s + d * grid.strides[a] * 2 * rows_w for s in steps for d in range(grid.axes[a])]
    steps = jnp.array(steps, jnp.int32).reshape((1, 2) + (1,) * len(far_axes) + (ff_size // 2, 1))
    spots = (spots + steps + jnp.arange(rows_w, dtype=jnp.int32)).reshape(-1)
    arrival = (jnp.arange(width, dtype=jnp.int32)[:, None] == spots[None, :]).astype(low)

    def gather_tokens(values, bounds, orders):
        parts = [values[a:b] for a, b in zip(bounds[:-1], bounds[1:])]
        parts = [p.reshape((1,) * grid.rank + p.shape) for p in parts]
        parts = grid.gather(parts, orders)
        return jnp.concatenate([p.reshape(-1, p.shape[-1]) for p in parts], axis=0)

    def cut_tokens(values, bounds, over):
        parts = []
        start = 0
        lead = tuple(grid.axes[a] if a in over else 1 for a in all_axes)
        count = 1
        for e in lead:
            count *= e
        for a, b in zip(bounds[:-1], bounds[1:]):
            rows = count * (b - a)
            parts.append(values[start : start + rows].reshape(lead + (b - a, values.shape[-1])))
            start += rows
        return parts

    def join_tokens(parts):
        return jnp.concatenate([p.reshape(p.shape[grid.rank :]) for p in parts], axis=0)

    def cut_columns(grad, bounds):
        lead = grid.axes + (2, rows_w)
        return [
            own_core_sum(grad[:, a:b].astype(low).reshape(lead + (b - a,)), core, grid.rank)
            for a, b in zip(bounds[:-1], bounds[1:])
        ]

    def join_columns(parts):
        parts = [p.reshape(rows_w, p.shape[-1]) for p in parts]
        return jnp.concatenate(parts, axis=1).astype(jnp.float32)

    stages = len(wide_orders[0])
    ff_stages = len(ff_orders[0])

    bias_len = qkv_bias.shape[0]
    side_len = -(-(2 * rows_w + bias_len) // 128) * 128
    side_rows = jnp.concatenate([attn_gain, mlp_gain, qkv_bias])
    side_rows = jnp.pad(side_rows[None], ((0, rows_w - 1), (0, side_len - side_rows.shape[0])))
    gathered = lax.all_gather(
        jnp.concatenate([qkv_weight, side_rows], axis=1), ("ctx", "fsdp"), axis=0, tiled=True
    )
    def to_columns(weight):
        weight = jnp.swapaxes(weight.reshape(rows_w, ff_size, ff_cols), 0, 1)
        return jnp.pad(weight, ((0, 0), (0, 0), (0, ff_room - ff_cols)))

    gate_up = jnp.stack([to_columns(gate_weight), to_columns(up_weight)], axis=1)
    ones = (1,) * grid.rank
    rows_d = down_weight.shape[0]
    half = width // 2
    down_parts = [down_weight[:, :half].reshape(ones + (rows_d, half))]
    down_parts.append(down_weight[:, half:].reshape(ones + (rows_d, half)))
    out_low = cotangent[0]
    cot_all = gather_tokens(out_low, ff_bounds, ff_orders)

    def gather_far(parts, stage):
        if stage < len(far_orders[0]):
            parts = [grid.gather_stage(p, o[stage]) for p, o in zip(parts, far_orders)]
        return parts

    def scatter_far(parts, stage, absolute):
        if stage < len(far_orders[0]):
            parts = grid.scatter_round(parts, far_orders, stage, absolute)
        return parts

    down_parts = gather_far(down_parts, 0)
    gathered, out_weight, gate_up, cot_all, down_parts = together(
        gathered, out_weight, gate_up, cot_all, down_parts
    )
    gate_up = lax.all_to_all(
        gate_up, "ctx", split_axis=0, concat_axis=0, tiled=True, axis_index_groups=groups
    )
    few = ff_size // 2
    far_parts = [gate_up[:few], gate_up[few:]]
    far_parts = gather_far([p.reshape(ones + p.shape) for p in far_parts], 0)
    down_parts = gather_far(down_parts, 1)
    full_out = lax.all_gather(out_weight, ("ctx", "fsdp"), axis=0, tiled=True)

    full_qkv = gathered[:, : width_q + 2 * width_kv]
    side = gathered[:, width_q + 2 * width_kv :].reshape(devices, rows_w, side_len)[:, 0]
    side = side.astype(jnp.float32)
    full_attn_gain = side[:, :rows_w].reshape(-1)
    full_mlp_gain = side[:, rows_w : 2 * rows_w].reshape(-1)
    full_bias = side[:, 2 * rows_w : 2 * rows_w + bias_len].reshape(-1)

    normed = (rms_scale(hidden_in) * full_attn_gain).astype(low)
    projected = jnp.dot(normed, full_qkv, preferred_element_type=jnp.float32) + full_bias
    cosine, sine_table = rope_tables(query_pos)
    query_low = apply_rope(
        projected[:, :width_q].reshape(tok_dev, H, HD), cosine, sine_table
    ).astype(low)
    key_low = apply_rope(
        projected[:, width_q : width_q + width_kv].reshape(tok_dev, KV, HD), cosine, sine_table
    ).astype(low)
    value_low = projected[:, width_q + width_kv :].astype(low)
    query_group = query_low.reshape(tok_dev, KV, group_size, HD)

    kv_all = jnp.concatenate([key_low.reshape(tok_dev, width_kv), value_low], axis=1)
    kv_all = grid.gather_stage(kv_all.reshape(ones + kv_all.shape), wide_orders[0][0])
    kv_all, down_parts = together(kv_all, down_parts)
    for stage in range(1, len(wide_orders[0])):
        kv_all = grid.gather_stage(kv_all, wide_orders[0][stage])
    kv_all = kv_all.reshape(-1, 2 * width_kv)
    total_keys = kv_all.shape[0]
    key_all = kv_all[:, :width_kv].reshape(total_keys, KV, HD)
    value_all = kv_all[:, width_kv:].reshape(total_keys, KV, HD)
    row_ids = []
    for a, b in zip(token_bounds[:-1], token_bounds[1:]):
        chips, rows = grid.source_rows(a, b - a, all_axes)
        row_ids.append((chips * tok_dev + rows).reshape(-1))
    row_ids = jnp.concatenate(row_ids)
    key_seq, key_pos = key_meta(deal_row, row_ids, block_len, prompt_len)
    allowed = visible_pairs(query_seq, query_pos, key_seq, key_pos)[:, None, None, :]

    scores = (
        jnp.einsum("tkgd,nkd->tkgn", query_group, key_all, preferred_element_type=jnp.float32)
        * score_scale
    )
    scores = jnp.where(allowed, scores, neg_large)
    top = jnp.max(scores, axis=-1)
    weights = jnp.exp(scores - top[..., None])
    weight_sum = jnp.sum(weights, axis=-1)
    mixed = (
        jnp.einsum(
            "tkgn,nkd->tkgd", weights.astype(low), value_all, preferred_element_type=jnp.float32
        )
        / weight_sum[..., None]
    )
    log_total = top + jnp.log(weight_sum)
    attended = mixed.reshape(tok_dev, width_q).astype(low)
    resid = hidden_in + jnp.dot(attended, full_out, preferred_element_type=jnp.float32)
    normed_mlp = (rms_scale(resid) * full_mlp_gain).astype(low)

    arranged = jnp.dot(normed_mlp, arrival, preferred_element_type=jnp.float32).astype(low)
    for a in far_axes:
        down_parts = [grid.ordered(p, a) for p in down_parts]
    down = jnp.concatenate([p[..., None, :, :] for p in down_parts], axis=-1)
    down = both_cores(down, core, grid.rank).reshape(ff_cols, width)
    down = jnp.pad(down, ((0, ff_room - ff_cols), (0, 0)))
    arranged, far_parts, down = together(arranged, far_parts, down)
    mlp_all = gather_tokens(arranged, ff_bounds, ff_orders)
    far_parts = gather_far(far_parts, 1)
    mlp_all, far_parts = together(mlp_all, far_parts)
    far_parts = [p.reshape((-1,) + p.shape[-3:]) for p in far_parts]
    far_parts = far_parts + [other_core(p) for p in far_parts]

    out_grad = out_low.astype(jnp.float32)
    mlp_partial, out_partial, *far_grads, down_grad = feed_forward(
        mlp_all, cot_all, far_parts, down
    )
    far_lead = tuple(grid.axes[a] if a in far_axes else 1 for a in all_axes)
    far_grads = [
        (ours.astype(jnp.float32) + other_core(theirs).astype(jnp.float32)).astype(low)
        for ours, theirs in zip(far_grads[:2], far_grads[2:])
    ]
    far_grads = [g.reshape(far_lead + (few,) + g.shape[1:]) for g in far_grads]
    lead = tuple(grid.axes[a] if a in ff_axes else 1 for a in all_axes)
    out_partial = out_partial.reshape(lead + (tok_dev, width))
    for a in ff_axes:
        out_partial = grid.ordered(out_partial, a)
    down_grad = down_grad[:ff_cols].reshape(far_lead + (2, rows_d, width))
    down_grad = own_core_sum(down_grad, core, grid.rank)
    down_grads = [down_grad[..., :half], down_grad[..., half:]]
    mlp_partial, far_grads, down_grads = together(mlp_partial, far_grads, down_grads)
    mlp_parts = cut_tokens(mlp_partial, ff_bounds, ff_axes)
    for stage in range(ff_stages):
        mlp_parts = grid.scatter_round(mlp_parts, ff_orders, stage, False)
    far_grads = scatter_far(far_grads, 0, False)
    mlp_parts, far_grads, out_partial = together(mlp_parts, far_grads, out_partial)
    out_sum = lax.psum_scatter(
        out_partial.reshape(-1, width),
        "ctx",
        scatter_dimension=0,
        tiled=True,
        axis_index_groups=groups,
    )
    mlp_normed_grad = jnp.einsum(
        "tc,dc->td", join_tokens(mlp_parts), arrival, preferred_element_type=jnp.float32
    )
    resid_part, mlp_gain_grad = norm_back(resid, full_mlp_gain, mlp_normed_grad)
    resid_grad = out_grad + resid_part
    resid_low = resid_grad.astype(low)
    out_w_grad = jnp.einsum("tq,td->qd", attended, resid_low, preferred_element_type=jnp.float32)
    out_w_sum = lax.psum_scatter(
        out_w_grad.astype(low), ("ctx", "fsdp"), scatter_dimension=0, tiled=True
    )
    mixed_grad = (
        jnp.einsum("td,qd->tq", resid_low, full_out, preferred_element_type=jnp.float32)
        .astype(low)
        .reshape(tok_dev, KV, group_size, HD)
    )
    row_dot = jnp.sum(mixed_grad.astype(jnp.float32) * mixed, axis=-1)
    scores = (
        jnp.einsum("tkgd,nkd->tkgn", query_group, key_all, preferred_element_type=jnp.float32)
        * score_scale
    )
    probs = jnp.exp(jnp.where(allowed, scores - log_total[..., None], neg_large))
    prob_grad = jnp.einsum(
        "tkgd,nkd->tkgn", mixed_grad, value_all, preferred_element_type=jnp.float32
    )
    score_grad = (probs * (prob_grad - row_dot[..., None])).astype(low)
    query_rot = (
        jnp.einsum("tkgn,nkd->tkgd", score_grad, key_all, preferred_element_type=jnp.float32)
        * score_scale
    )
    key_rot = (
        jnp.einsum("tkgn,tkgd->nkd", score_grad, query_group, preferred_element_type=jnp.float32)
        * score_scale
    )
    value_rot = jnp.einsum(
        "tkgn,tkgd->nkd", probs.astype(low), mixed_grad, preferred_element_type=jnp.float32
    )
    kv_partial = jnp.concatenate(
        [key_rot.reshape(total_keys, width_kv), value_rot.reshape(total_keys, width_kv)], axis=1
    ).astype(low)
    query_grad = rope_back(query_rot.reshape(tok_dev, H, HD), cosine, sine_table)
    query_grad = query_grad.reshape(tok_dev, width_q)
    query_parts = cut_columns(
        jnp.einsum("td,tc->dc", normed, query_grad.astype(low), preferred_element_type=jnp.float32),
        (0, width_q),
    )

    kv_parts = cut_tokens(kv_partial, token_bounds, all_axes)
    kv_parts = grid.scatter_round(kv_parts, wide_orders, 0, False)
    kv_parts, far_grads, query_parts, down_grads = together(
        kv_parts, far_grads, query_parts, down_grads
    )
    for stage in range(1, stages):
        kv_parts = grid.scatter_round(kv_parts, wide_orders, stage, False)
    far_grads = scatter_far(far_grads, 1, False)
    kv_share = join_tokens(kv_parts).astype(jnp.float32)
    kv_share, query_parts, far_grads, down_grads = together(
        kv_share, query_parts, far_grads, down_grads
    )
    gate_up_grad = jnp.concatenate([g.reshape((few,) + g.shape[-3:]) for g in far_grads], axis=0)
    gate_up_grad = lax.all_to_all(
        gate_up_grad, "ctx", split_axis=0, concat_axis=0, tiled=True, axis_index_groups=groups
    )
    query_parts = grid.scatter_round(query_parts, weight_order, 0, True)
    down_grads = scatter_far(down_grads, 0, True)
    key_grad_own = rope_back(
        kv_share[:, :width_kv].reshape(tok_dev, KV, HD), cosine, sine_table
    )
    kv_grad = jnp.concatenate(
        [key_grad_own.reshape(tok_dev, width_kv), kv_share[:, width_kv:]], axis=1
    )
    proj_grad = jnp.concatenate([query_grad, kv_grad], axis=1)
    bias_grad = jnp.sum(proj_grad, axis=0)
    proj_low = proj_grad.astype(low)
    normed_grad = jnp.einsum("tc,dc->td", proj_low, full_qkv, preferred_element_type=jnp.float32)
    input_part, attn_gain_grad = norm_back(hidden_in, full_attn_gain, normed_grad)
    input_grad = resid_grad + input_part

    input_grad, out_sum, out_w_sum = together(input_grad, out_sum, out_w_sum)
    out_share = out_w_sum.astype(jnp.float32)
    layer_out = resid + out_sum.astype(jnp.float32)

    def to_rows(grad):
        return jnp.swapaxes(grad, 0, 1).reshape(rows_w, ff_total)

    small = [
        bias_grad[: width_q + width_kv],
        bias_grad[width_q + width_kv :],
        attn_gain_grad,
        mlp_gain_grad,
    ]
    small = jnp.concatenate([v.reshape(devices, 1, -1) for v in small], axis=2).astype(low)
    sizes = ((width_q + width_kv) // devices, width_kv // devices, rows_w, rows_w)
    small = jnp.pad(small, ((0, 0), (0, rows_w - 1), (0, -small.shape[2] % 128)))
    kv_w_grad = jnp.einsum(
        "td,tc->dc", normed, kv_grad.astype(low), preferred_element_type=jnp.float32
    ).astype(low)
    kv_w_grad = jnp.concatenate([kv_w_grad, small.reshape(width, -1)], axis=1)
    kv_w_parts = cut_columns(kv_w_grad, (0, kv_w_grad.shape[1]))
    query_parts, kv_w_parts, down_grads = together(query_parts, kv_w_parts, down_grads)
    down_grads = scatter_far(down_grads, 1, True)
    down_grad = jnp.concatenate(down_grads, axis=-1)
    down_share = down_grad.reshape(rows_d, width).astype(jnp.float32)
    for stage in range(1, stages):
        query_parts = grid.scatter_round(query_parts, weight_order, stage, True)
    for stage in range(stages):
        kv_w_parts = grid.scatter_round(kv_w_parts, weight_order, stage, True)
    kv_w_share = join_columns(kv_w_parts)
    small = kv_w_share[0, 2 * width_kv :]
    qkv_share = jnp.concatenate([join_columns(query_parts), kv_w_share[:, : 2 * width_kv]], axis=1)
    gate_up_grad = gate_up_grad.astype(jnp.float32)
    gate_share = to_rows(gate_up_grad[:, 0, :, :ff_cols])
    up_share = to_rows(gate_up_grad[:, 1, :, :ff_cols])
    vectors = []
    start = 0
    for count in sizes:
        vectors.append(small[start : start + count])
        start += count
    front_share, value_bias_share, attn_gain_share, mlp_gain_share = vectors
    return (
        layer_out.astype(low)[None],
        input_grad[None],
        qkv_share,
        front_share,
        value_bias_share,
        out_share,
        attn_gain_share,
        mlp_gain_share,
        gate_share,
        up_share,
        down_share,
    )


def solution(mesh):
    return jax.shard_map(
        shards,
        mesh=mesh,
        in_specs=(
            P("fsdp", "ctx", None),
            P("fsdp", None),
            P("fsdp", "ctx"),
            P("fsdp", "ctx"),
            P(("ctx", "fsdp"), None),
            P(("ctx", "fsdp")),
            P(("ctx", "fsdp"), None),
            P(("ctx", "fsdp")),
            P(("ctx", "fsdp")),
            P(("ctx", "fsdp"), None),
            P(("ctx", "fsdp"), None),
            P(("ctx", "fsdp"), None),
            P("fsdp", "ctx", None),
        ),
        out_specs=(
            P("fsdp", "ctx", None),
            P("fsdp", "ctx", None),
            P(("ctx", "fsdp"), None),
            P(("ctx", "fsdp")),
            P(("ctx", "fsdp")),
            P(("ctx", "fsdp"), None),
            P(("ctx", "fsdp")),
            P(("ctx", "fsdp")),
            P(("ctx", "fsdp"), None),
            P(("ctx", "fsdp"), None),
            P(("ctx", "fsdp"), None),
        ),
        check_vma=False,
    )
```

time: 845 us -> 665 us (0.79)
  starting transfers between devices: 223 us -> 76.3 us
  Pallas kernels: 0 us -> 49.7 us
  matrix products: 91.8 us -> 60.8 us
  other arithmetic: 106 us -> 78.1 us
  waiting for transfers between devices: 320 us -> 302 us
  local copies, waits for them, and re-layouts: 88.6 us -> 73.5 us
  between operations: 4.25 us -> 15.5 us
    ppermute x126 -> x49, starting transfers between devices: 207 us -> 66.1 us  [hop(): return lax.ppermute(values, 'ctx', pairs)]
    ppermute x126 -> x49, waiting for transfers between devices: 320 us -> 237 us  [hop(): return lax.ppermute(values, 'ctx', pairs)]
    pallas_call x0 -> x1, Pallas kernels: none -> 49.7 us  [feed_forward(): pl.pallas_call(ff_kernel, grid=(columns // tile,), in_specs=[whole, whole...]
    dot_general x7 -> x4, matrix products: 54.8 us -> 6.48 us  [the longest x1 2.27 us: shards(): jnp.einsum('tc,dc->td', join_tokens(mlp_parts), arrival, preferred_elemen...]
    all_gather x0 -> x2, waiting for transfers between devices: none -> 45.8 us  [the longest x1 45.8 us: shards(): lax.all_gather(jnp.concatenate([qkv_weight, side_rows], axis=1), ('ctx',...]
    ppermute x16 -> x8, waiting for transfers between devices: 0.04 us -> 19.2 us  [other_core(): return lax.ppermute(values, 'fsdp', [(0, 1), (1, 0)])]
    add x50 -> x5, other arithmetic: 16.9 us -> 1.5 us  [the longest x1 1.19 us: shards(): input_grad = resid_grad + input_part]
    convert_element_type x7 -> x20, other arithmetic: 3.02 us -> 16.1 us  [the longest x12 9.54 us: scatter_stage(): return total.astype(values.dtype)]
  transfers between devices with their start and end apart: 145 -> 63, of which waited for: 73 -> 33; matrix products, arithmetic and copies ran while one was open for 26% -> 27% of each run, Pallas kernels for 0% -> 0%
where the time goes in v2:
time: 665 us; the launch traced here: 655 us
  waiting for transfers between devices  302 us (45%)
  other arithmetic  78.1 us (12%)
  starting transfers between devices  76.3 us (11%)
  local copies, waits for them, and re-layouts  73.5 us (11%)
  matrix products  60.8 us (9%)
  Pallas kernels  49.7 us (7%)
  between operations  15.5 us (2%)
    ppermute x49, waiting for transfers between devices, hop(): return lax.ppermute(values, 'ctx', pairs)  237 us
    ppermute x49, starting transfers between devices, hop(): return lax.ppermute(values, 'ctx', pairs)  66.1 us
    pallas_call x1, Pallas kernels, feed_forward(): pl.pallas_call(ff_kernel, grid=(columns // tile,), in_specs=[whole, whole...  49.7 us
    all_gather x1, waiting for transfers between devices, shards(): lax.all_gather(jnp.concatenate([qkv_weight, side_rows], axis=1), ('ctx',...  45.8 us
    ppermute x8, waiting for transfers between devices, other_core(): return lax.ppermute(values, 'fsdp', [(0, 1), (1, 0)])  19.2 us
    concatenate x12, other arithmetic, join(): jnp.concatenate([join(prefix + (j,)) for j in range(self.axes[axes[depth]...  17.2 us
    unnamed x139, local copies, waits for them, and re-layouts  15.1 us
  transfers between devices with their start and end apart: 63, of which 33 were waited for; matrix products, arithmetic and copies ran while one was open for 27% of the time, Pallas kernels for 0%

profile of v2, /device:TPU:0, one launch (start us, length us, event | category | flops | bytes accessed | tf_op | source)
XLA Modules:
  0.0 655.4 jit_solution(7103753599867670846)
XLA Ops:
  9.8 5.1 collective-permute-start.2
  22.1 2.7 reshape.725
  32.5 21.0 %collective-permute-done.1 = bf16[1,1,1,128,1536]{4,3,2,1,0:T(8,128)(2,1)} collective-permute-done((bf16[1,1,1,128,1536]{4,3,2,1,0:T(8,128)(2,1)}, bf16[1,1,1,128,1536]{4,3,2,1,0:T(8,128)(2,1)}, u32[]{:S(2)}, u32[]{:S(2)}) %collective-permute-start.1) | collective-permute-done | bytes 393248 | tf_op jit(solution)/shard_map/ppermute | solution.py:202
  58.5 45.8 %all-gather.3.cloned.1.call-done = bf16[1536,2304]{1,0:T(8,128)(2,1)} async-done(((bf16[48,2304]{1,0:T(8,128)(2,1)}), bf16[1536,2304]{1,0:T(8,128)(2,1)}) %all-gather.3.cloned.1.call-update) | async-done | bytes 7077904 | tf_op jit(solution)/shard_map/all_gather | solution.py:419
  105.8 3.8 fusion.34
  118.7 4.4 all-to-all-start
  125.9 16.9 %collective-permute-done.6 = bf16[1,1,1,128,512]{4,3,2,1,0:T(8,128)(2,1)} collective-permute-done((bf16[1,1,1,128,512]{4,3,2,1,0:T(8,128)(2,1)}, bf16[1,1,1,128,512]{4,3,2,1,0:T(8,128)(2,1)}, u32[]{:S(2)}, u32[]{:S(2)}) %collective-permute-start.6) | collective-permute-done | bytes 131104 | tf_op jit(solution)/shard_map/ppermute | solution.py:202
  154.2 8.4 %collective-permute-done.12 = bf16[4,1,1,128,512]{4,3,2,1,0:T(8,128)(2,1)S(1)} collective-permute-done((bf16[4,1,1,128,512]{4,3,2,1,0:T(8,128)(2,1)S(1)}, bf16[4,1,1,128,512]{4,3,2,1,0:T(8,128)(2,1)S(1)}, u32[]{:S(2)}, u32[]{:S(2)}) %collective-permute-start.12) | collective-permute-done | bytes 524320 | tf_op jit(solution)/shard_map/ppermute | solution.py:202
  162.6 9.0 %collective-permute-done.11 = bf16[4,1,1,128,512]{4,3,2,1,0:T(8,128)(2,1)S(1)} collective-permute-done((bf16[4,1,1,128,512]{4,3,2,1,0:T(8,128)(2,1)S(1)}, bf16[4,1,1,128,512]{4,3,2,1,0:T(8,128)(2,1)S(1)}, u32[]{:S(2)}, u32[]{:S(2)}) %collective-permute-start.11) | collective-permute-done | bytes 524320 | tf_op jit(solution)/shard_map/ppermute | solution.py:202
  178.9 3.5 fusion.4
  182.4 4.6 copy-done
  193.4 8.7 %fusion.138 = (bf16[128,2,6,128]{0,3,2,1:T(8,128)(2,1)}, f32[128,2,6,128]{0,3,2,1:T(8,128)}) fusion(f32[128,2,6]{0,2,1:T(8,128)S(1)} %fusion.5, bf16[2048,2,128,1]{0,2,3,1:T(8,128)(2,1)S(1)} %bitcast.336, f32[2,2048,128,6]{2,1,3,0:T(8,128)} %copy-done, f32[128,2,6]{0,2,1:T(8,128)S(1)} %get-tuple-element.171, pred[128,2048]{0,1:T(8,128)(4,1)S(1)} %copy-done.6), kind=kOutput, calls=%fused_computation.326 | convolution fusion | flops 818282496 | bytes 15085568 | tf_op jit(solution)/shard_map/tkgn,nkd->tkgd/dot_general | solution.py:503
  202.1 9.7 %collective-permute-done.14 = bf16[1,1,1,2,2,48,2304]{6,5,4,3,2,1,0:T(8,128)(2,1)S(1)} collective-permute-done((bf16[1,1,1,2,2,48,2304]{6,5,4,3,2,1,0:T(8,128)(2,1)S(1)}, bf16[1,1,1,2,2,48,2304]{6,5,4,3,2,1,0:T(8,128)(2,1)S(1)}, u32[]{:S(2)}, u32[]{:S(2)}) %collective-permute-start.14) | collective-permute-done | bytes 884768 | tf_op jit(solution)/shard_map/ppermute | solution.py:202
  214.5 4.0 broadcast_select_fusion.1
  221.2 3.4 pad.22.down
  224.6 3.2 multiply_reduce_fusion.3
  237.0 5.6 collective-permute-done.18
  242.5 24.9 %collective-permute-done.17 = bf16[1,1,1,128,1536]{4,3,2,1,0:T(8,128)(2,1)S(1)} collective-permute-done((bf16[1,1,1,128,1536]{4,3,2,1,0:T(8,128)(2,1)S(1)}, bf16[1,1,1,128,1536]{4,3,2,1,0:T(8,128)(2,1)S(1)}, u32[]{:S(2)}, u32[]{:S(2)}) %collective-permute-start.17) | collective-permute-done | bytes 393248 | tf_op jit(solution)/shard_map/ppermute | solution.py:202
  273.9 6.1 collective-permute-done.21.w2
  279.9 5.1 collective-permute-done.22.w3
  285.0 49.7 %shard_map.221 = (bf16[512,1536]{1,0:T(8,128)(2,1)S(1)}, bf16[512,1536]{1,0:T(8,128)(2,1)S(1)}, bf16[8,2,48,2304]{3,2,1,0:T(8,128)(2,1)}, bf16[8,2,48,2304]{3,2,...) custom-call(bf16[512,1536]{1,0:T(8,128)(2,1)} %bitcast.327, ...), custom_call_target="tpu_custom_call" | custom-call | flops 32614907904 | bytes 51904512 | tf_op jit(solution)/shard_map/pallas_call | solution.py:163
  334.6 3.4 slice.284
  344.0 8.1 %collective-permute-done.25 = bf16[1,2,2,1,280,1536]{5,4,3,2,1,0:T(8,128)(2,1)} collective-permute-done((bf16[1,2,2,1,280,1536]{5,4,3,2,1,0:T(8,128)(2,1)}, bf16[1,2,2,1,280,1536]{5,4,3,2,1,0:T(8,128)(2,1)}, u32[]{:S(2)}, u32[]{:S(2)}) %collective-permute-start.25) | collective-permute-done | bytes 3440672 | tf_op jit(solution)/shard_map/ppermute | solution.py:289
  352.1 3.4 dynamic-slice_add_fusion
  370.3 6.0 collective-permute-done.26
  376.3 9.5 %collective-permute-done.28 = bf16[1,1,1,128,1536]{4,3,2,1,0:T(8,128)(2,1)S(1)} collective-permute-done((bf16[1,1,1,128,1536]{4,3,2,1,0:T(8,128)(2,1)S(1)}, bf16[1,1,1,128,1536]{4,3,2,1,0:T(8,128)(2,1)S(1)}, u32[]{:S(2)}, u32[]{:S(2)}) %collective-permute-start.28) | collective-permute-done | bytes 393248 | tf_op jit(solution)/shard_map/ppermute | solution.py:202
  385.8 14.4 %collective-permute-done.27 = bf16[1,1,1,128,1536]{4,3,2,1,0:T(8,128)(2,1)S(1)} collective-permute-done((bf16[1,1,1,128,1536]{4,3,2,1,0:T(8,128)(2,1)S(1)}, bf16[1,1,1,128,1536]{4,3,2,1,0:T(8,128)(2,1)S(1)}, u32[]{:S(2)}, u32[]{:S(2)}) %collective-permute-start.27) | collective-permute-done | bytes 393248 | tf_op jit(solution)/shard_map/ppermute | solution.py:202
  404.4 3.1 collective-permute-done.29
  411.9 4.4 convolution_convert_fusion.3
  417.3 7.8 %fusion.1 = bf16[128,2,6,2048]{0,3,2,1:T(8,128)(2,1)S(1)} fusion(f32[2,2048,128,6]{2,1,3,0:T(8,128)} %copy-done, f32[128,2,6]{0,2,1:T(8,128)S(1)} %multiply_reduce_fusion.1, f32[128,2,6]{0,2,1:T(8,128)S(1)} %copy-done.56, pred[128,2048]{0,1:T(8,128)(4,1)S(1)} %copy-done.7, bf16[2048,2,128,1]{0,2,3,1:T(8,128)(2,1)} %bitcast.335, ...), kind=kOutput, calls=%fused_computation.2 | convolution fusion | flops 824180736 | bytes 20590592 | tf_op jit(solution)/shard_map/tkgd,nkd->tkgn/dot_general | solution.py:577
  432.5 3.1 fusion.33
  440.6 8.9 %fusion.30 = bf16[2048,2,128]{0,2,1:T(8,128)(2,1)} fusion(bf16[128,2,6,128]{0,3,2,1:T(8,128)(2,1)} %bitcast.332, f32[2,2048,128,6]{2,1,3,0:T(8,128)} %copy-done, f32[128,2,6]{0,2,1:T(8,128)S(1)} %copy-done.57, pred[128,2048]{0,1:T(8,128)(4,1)S(1)} %copy-done.7), kind=kOutput, calls=%fused_computation.61 | convolution fusion | flops 818413568 | bytes 14292992 | tf_op jit(solution)/shard_map/tkgn,tkgd->nkd/dot_general | solution.py:589
  452.1 3.7 copy.113
  460.7 11.2 %collective-permute-done.31 = bf16[4,1,1,128,512]{4,3,2,1,0:T(8,128)(2,1)S(1)} collective-permute-done((bf16[4,1,1,128,512]{4,3,2,1,0:T(8,128)(2,1)S(1)}, bf16[4,1,1,128,512]{4,3,2,1,0:T(8,128)(2,1)S(1)}, u32[]{:S(2)}, u32[]{:S(2)}) %collective-permute-start.31) | collective-permute-done | bytes 524320 | tf_op jit(solution)/shard_map/ppermute | solution.py:202
  471.9 11.1 %collective-permute-done.33 = bf16[4,1,1,128,512]{4,3,2,1,0:T(8,128)(2,1)S(1)} collective-permute-done((bf16[4,1,1,128,512]{4,3,2,1,0:T(8,128)(2,1)S(1)}, bf16[4,1,1,128,512]{4,3,2,1,0:T(8,128)(2,1)S(1)}, u32[]{:S(2)}, u32[]{:S(2)}) %collective-permute-start.33) | collective-permute-done | bytes 524320 | tf_op jit(solution)/shard_map/ppermute | solution.py:202
  486.4 3.5 dynamic-slice_add_fusion.1
  496.0 3.5 convolution_convert_fusion
  503.3 3.2 collective-permute-done.36
  507.6 4.3 collective-permute-done.39
  513.3 8.8 %collective-permute-done.38 = bf16[1,1,1,2,2,48,2304]{6,5,4,3,2,1,0:T(8,128)(2,1)S(1)} collective-permute-done((bf16[1,1,1,2,2,48,2304]{6,5,4,3,2,1,0:T(8,128)(2,1)S(1)}, bf16[1,1,1,2,2,48,2304]{6,5,4,3,2,1,0:T(8,128)(2,1)S(1)}, u32[]{:S(2)}, u32[]{:S(2)}) %collective-permute-start.38) | collective-permute-done | bytes 884768 | tf_op jit(solution)/shard_map/ppermute | solution.py:202
  523.8 4.5 all-to-all-start.1
  529.9 6.2 fusion.67
  545.9 10.1 %collective-permute-done.40 = bf16[4,1,1,1,48,1536]{5,4,3,2,1,0:T(8,128)(2,1)} collective-permute-done((bf16[4,1,1,1,48,1536]{5,4,3,2,1,0:T(8,128)(2,1)}, bf16[4,1,1,1,48,1536]{5,4,3,2,1,0:T(8,128)(2,1)}, u32[]{:S(2)}, u32[]{:S(2)}) %collective-permute-start.40) | collective-permute-done | bytes 589856 | tf_op jit(solution)/shard_map/ppermute | solution.py:202
  557.2 34.9 %collective-permute-done.42 = bf16[4,1,1,1,48,1536]{5,4,3,2,1,0:T(8,128)(2,1)S(1)} collective-permute-done((bf16[4,1,1,1,48,1536]{5,4,3,2,1,0:T(8,128)(2,1)}, bf16[4,1,1,1,48,1536]{5,4,3,2,1,0:T(8,128)(2,1)S(1)}, u32[]{:S(2)}, u32[]{:S(2)}) %collective-permute-start.42) | collective-permute-done | bytes 589856 | tf_op jit(solution)/shard_map/ppermute | solution.py:202
  592.1 7.7 %collective-permute-done.41 = bf16[4,1,1,1,48,1536]{5,4,3,2,1,0:T(8,128)(2,1)S(1)} collective-permute-done((bf16[4,1,1,1,48,1536]{5,4,3,2,1,0:T(8,128)(2,1)}, bf16[4,1,1,1,48,1536]{5,4,3,2,1,0:T(8,128)(2,1)S(1)}, u32[]{:S(2)}, u32[]{:S(2)}) %collective-permute-start.41) | collective-permute-done | bytes 589856 | tf_op jit(solution)/shard_map/ppermute | solution.py:202
  609.1 3.6 collective-permute-start.46
  621.8 4.0 collective-permute-done.47
  628.5 3.3 collective-permute-done.53
  (413 shorter events, 198.6 us)
Async XLA Ops:
  7.2 97.1 %all-gather.3.cloned.1.call-start = ((), (), s32[]{:S(2)}) async-start(), calls=%async_computation.4 | async-start | bytes 7299072 | tf_op jit(solution)/shard_map/all_gather | solution.py:419
  9.7 214.8 %all-gather.5.cloned.1.call-start = ((), (), s32[]{:S(2)}) async-start(), calls=%async_computation.5 | async-start | bytes 4866048 | tf_op jit(solution)/shard_map/all_gather | solution.py:456
  9.8 22.8 %collective-permute-start.2 = (bf16[1,1,1,128,1536]{4,3,2,1,0:T(8,128)(2,1)}, bf16[1,1,1,128,1536]{4,3,2,1,0:T(8,128)(2,1)}, u32[]{:S(2)}, u32[]{:S(2)}) collective-permute-start(bf16[1,1,1,128,1536]{4,3,2,1,0:T(8,128)(2,1)} %bitcast.322), channel_id=1, source_target_pairs={{0,24},{2,26},{4,28},{6,30},{8,0},{10,2},{12,4},{14,6},{16,8},{18,... | collective-permute-start | bytes 1179656 | tf_op jit(solution)/shard_map/ppermute | solution.py:202
  14.9 38.7 %collective-permute-start.1 = (bf16[1,1,1,128,1536]{4,3,2,1,0:T(8,128)(2,1)}, bf16[1,1,1,128,1536]{4,3,2,1,0:T(8,128)(2,1)}, u32[]{:S(2)}, u32[]{:S(2)}) collective-permute-start(bf16[1,1,1,128,1536]{4,3,2,1,0:T(8,128)(2,1)} %bitcast.323), channel_id=1, source_target_pairs={{0,16},{2,18},{4,20},{6,22},{8,24},{10,26},{12,28},{14,30},{16,0},... | collective-permute-start | bytes 1179656 | tf_op jit(solution)/shard_map/ppermute | solution.py:202
  14.9 38.7 %collective-permute-start = (bf16[1,1,1,128,1536]{4,3,2,1,0:T(8,128)(2,1)}, bf16[1,1,1,128,1536]{4,3,2,1,0:T(8,128)(2,1)}, u32[]{:S(2)}, u32[]{:S(2)}) collective-permute-start(bf16[1,1,1,128,1536]{4,3,2,1,0:T(8,128)(2,1)} %bitcast.324), channel_id=1, source_target_pairs={{0,8},{2,10},{4,12},{6,14},{8,16},{10,18},{12,20},{14,22},{16,24},... | collective-permute-start | bytes 1179656 | tf_op jit(solution)/shard_map/ppermute | solution.py:202
  17.8 38.3 %collective-permute-start.4 = (bf16[1,1,1,280,768]{4,3,2,1,0:T(8,128)(2,1)}, bf16[1,1,1,280,768]{4,3,2,1,0:T(8,128)(2,1)}, u32[]{:S(2)}, u32[]{:S(2)}) collective-permute-start(bf16[1,1,1,280,768]{4,3,2,1,0:T(8,128)(2,1)} %get-tuple-element.143), channel_id=1, source_target_pairs={{0,2},{2,0},{4,6},{6,4},{8,10},{10,8},{12,14},{14,12},{16,18},{18,... | collective-permute-start | bytes 1290248 | tf_op jit(solution)/shard_map/ppermute | solution.py:202
  19.3 38.0 %collective-permute-start.3 = (bf16[1,1,1,280,768]{4,3,2,1,0:T(8,128)(2,1)S(1)}, bf16[1,1,1,280,768]{4,3,2,1,0:T(8,128)(2,1)}, u32[]{:S(2)}, u32[]{:S(2)}) collective-permute-start(bf16[1,1,1,280,768]{4,3,2,1,0:T(8,128)(2,1)S(1)} %get-tuple-element.144), channel_id=1, source_target_pairs={{0,4},{2,6},{4,0},{6,2},{8,12},{10,14},{12,8},{14,10},{16,20},{18,... | collective-permute-start | bytes 1290248 | tf_op jit(solution)/shard_map/ppermute | solution.py:202
  110.6 33.4 %collective-permute-start.8 = (bf16[1,2,1,280,768]{4,3,2,1,0:T(8,128)(2,1)S(1)}, bf16[1,2,1,280,768]{4,3,2,1,0:T(8,128)(2,1)}, u32[]{:S(2)}, u32[]{:S(2)}) collective-permute-start(bf16[1,2,1,280,768]{4,3,2,1,0:T(8,128)(2,1)S(1)} %pad_maximum_fusion.13), channel_id=1, source_target_pairs={{0,2},{2,0},{4,6},{6,4},{8,10},{10,8},{12,14},{14,12},{16,18},{18,... | collective-permute-start | bytes 2580488 | tf_op jit(solution)/shard_map/ppermute | solution.py:202
  112.0 33.4 %collective-permute-start.9 = (bf16[1,1,2,280,768]{4,3,2,1,0:T(8,128)(2,1)S(1)}, bf16[1,1,2,280,768]{4,3,2,1,0:T(8,128)(2,1)}, u32[]{:S(2)}, u32[]{:S(2)}) collective-permute-start(bf16[1,1,2,280,768]{4,3,2,1,0:T(8,128)(2,1)S(1)} %pad_maximum_fusion.14), channel_id=1, source_target_pairs={{0,4},{2,6},{4,0},{6,2},{8,12},{10,14},{12,8},{14,10},{16,20},{18,... | collective-permute-start | bytes 2580488 | tf_op jit(solution)/shard_map/ppermute | solution.py:202
  116.7 26.1 %collective-permute-start.6 = (bf16[1,1,1,128,512]{4,3,2,1,0:T(8,128)(2,1)}, bf16[1,1,1,128,512]{4,3,2,1,0:T(8,128)(2,1)}, u32[]{:S(2)}, u32[]{:S(2)}) collective-permute-start(bf16[1,1,1,128,512]{4,3,2,1,0:T(8,128)(2,1)} %maximum_bitcast_fusion.1), channel_id=1, source_target_pairs={{0,16},{2,18},{4,20},{6,22},{8,24},{10,26},{12,28},{14,30},{16,0},... | collective-permute-start | bytes 393224 | tf_op jit(solution)/shard_map/ppermute | solution.py:202
  117.8 25.0 %collective-permute-start.5 = (bf16[1,1,1,128,512]{4,3,2,1,0:T(8,128)(2,1)}, bf16[1,1,1,128,512]{4,3,2,1,0:T(8,128)(2,1)}, u32[]{:S(2)}, u32[]{:S(2)}) collective-permute-start(bf16[1,1,1,128,512]{4,3,2,1,0:T(8,128)(2,1)} %maximum_bitcast_fusion.1), channel_id=1, source_target_pairs={{0,8},{2,10},{4,12},{6,14},{8,16},{10,18},{12,20},{14,22},{16,24},... | collective-permute-start | bytes 393224 | tf_op jit(solution)/shard_map/ppermute | solution.py:202
  118.7 70.8 %all-to-all-start = ((bf16[4,2,48,2304]{3,2,1,0:T(8,128)(2,1)}), bf16[4,2,48,2304]{3,2,1,0:T(8,128)(2,1)}, u32[]{:S(2)}, u32[]{:S(2)}) async-start(bf16[4,2,48,2304]{3,2,1,0:T(8,128)(2,1)} %pad_maximum_fusion.4), calls=%async_computation | async-start | bytes 3538944 | tf_op jit(solution)/shard_map/all_to_all | solution.py:449
  123.1 522.1 %reduce-scatter.3.cloned.1.call-start = ((), (), s32[]{:S(2)}) async-start(), calls=%async_computation.6 | async-start | bytes 1966080 | tf_op jit(solution)/shard_map/reduce_scatter | solution.py:549
  146.7 15.9 %collective-permute-start.12 = (bf16[4,1,1,128,512]{4,3,2,1,0:T(8,128)(2,1)S(1)}, bf16[4,1,1,128,512]{4,3,2,1,0:T(8,128)(2,1)S(1)}, u32[]{:S(2)}, u32[]{:S(2)}) collective-permute-start(bf16[4,1,1,128,512]{4,3,2,1,0:T(8,128)(2,1)S(1)} %pad_maximum_fusion.17), channel_id=1, source_target_pairs={{0,6},{2,4},{4,2},{6,0},{8,14},{10,12},{12,10},{14,8},{16,22},{18,... | collective-permute-start | bytes 1572872 | tf_op jit(solution)/shard_map/ppermute | solution.py:202
  148.5 23.1 %collective-permute-start.11 = (bf16[4,1,1,128,512]{4,3,2,1,0:T(8,128)(2,1)S(1)}, bf16[4,1,1,128,512]{4,3,2,1,0:T(8,128)(2,1)S(1)}, u32[]{:S(2)}, u32[]{:S(2)}) collective-permute-start(bf16[4,1,1,128,512]{4,3,2,1,0:T(8,128)(2,1)S(1)} %pad_maximum_fusion.17), channel_id=1, source_target_pairs={{0,4},{2,6},{4,0},{6,2},{8,12},{10,14},{12,8},{14,10},{16,20},{18,... | collective-permute-start | bytes 1572872 | tf_op jit(solution)/shard_map/ppermute | solution.py:202
  149.7 22.5 %collective-permute-start.10 = (bf16[4,1,1,128,512]{4,3,2,1,0:T(8,128)(2,1)S(1)}, bf16[4,1,1,128,512]{4,3,2,1,0:T(8,128)(2,1)S(1)}, u32[]{:S(2)}, u32[]{:S(2)}) collective-permute-start(bf16[4,1,1,128,512]{4,3,2,1,0:T(8,128)(2,1)S(1)} %pad_maximum_fusion.17), channel_id=1, source_target_pairs={{0,2},{2,0},{4,6},{6,4},{8,10},{10,8},{12,14},{14,12},{16,18},{18,... | collective-permute-start | bytes 1572872 | tf_op jit(solution)/shard_map/ppermute | solution.py:202
  154.2 60.3 %collective-permute-start.15 = (bf16[1,2,2,1,280,1536]{5,4,3,2,1,0:T(8,128)(2,1)}, bf16[1,2,2,1,280,1536]{5,4,3,2,1,0:T(8,128)(2,1)}, u32[]{:S(2)}, u32[]{:S(2)}) collective-permute-start(bf16[1,2,2,1,280,1536]{5,4,3,2,1,0:T(8,128)(2,1)} %pad_maximum_fusion.3), channel_id=1, source_target_pairs={{0,1},{1,0},{2,3},{3,2},{4,5},{5,4},{6,7},{7,6},{8,9},{9,8},{10,11... | collective-permute-start | bytes 10321928 | tf_op jit(solution)/shard_map/ppermute | solution.py:289
  191.3 20.5 %collective-permute-start.14 = (bf16[1,1,1,2,2,48,2304]{6,5,4,3,2,1,0:T(8,128)(2,1)S(1)}, bf16[1,1,1,2,2,48,2304]{6,5,4,3,2,1,0:T(8,128)(2,1)S(1)}, u32[]{:S(2)}, u32[]{:S(2)}) collective-permute-start(bf16[1,1,1,2,2,48,2304]{6,5,4,3,2,1,0:T(8,128)(2,1)S(1)} %get-tuple-element.135), channel_id=1, source_target_pairs={{0,2},{2,0},{4,6},{6,4},{8,10},{10,8},{12,14},{14,12},{16,18},{18,... | collective-permute-start | bytes 2654216 | tf_op jit(solution)/shard_map/ppermute | solution.py:202
  192.2 20.9 %collective-permute-start.13 = (bf16[1,1,1,2,2,48,2304]{6,5,4,3,2,1,0:T(8,128)(2,1)S(1)}, bf16[1,1,1,2,2,48,2304]{6,5,4,3,2,1,0:T(8,128)(2,1)S(1)}, u32[]{:S(2)}, u32[]{:S(2)}) collective-permute-start(bf16[1,1,1,2,2,48,2304]{6,5,4,3,2,1,0:T(8,128)(2,1)S(1)} %get-tuple-element.136), channel_id=1, source_target_pairs={{0,4},{2,6},{4,0},{6,2},{8,12},{10,14},{12,8},{14,10},{16,20},{18,... | collective-permute-start | bytes 2654216 | tf_op jit(solution)/shard_map/ppermute | solution.py:202
  230.0 39.2 %collective-permute-start.19 = (bf16[1,2,1,2,2,48,2304]{6,5,4,3,2,1,0:T(8,128)(2,1)S(1)}, bf16[1,2,1,2,2,48,2304]{6,5,4,3,2,1,0:T(8,128)(2,1)S(1)}, u32[]{:S(2)}, u32[]{:S(2)}) collective-permute-start(bf16[1,2,1,2,2,48,2304]{6,5,4,3,2,1,0:T(8,128)(2,1)S(1)} %copy-done.11), channel_id=1, source_target_pairs={{0,2},{2,0},{4,6},{6,4},{8,10},{10,8},{12,14},{14,12},{16,18},{18,... | collective-permute-start | bytes 5308424 | tf_op jit(solution)/shard_map/ppermute | solution.py:202
  231.7 39.5 %collective-permute-start.20 = (bf16[1,1,2,2,2,48,2304]{6,5,4,3,2,1,0:T(8,128)(2,1)S(1)}, bf16[1,1,2,2,2,48,2304]{6,5,4,3,2,1,0:T(8,128)(2,1)S(1)}, u32[]{:S(2)}, u32[]{:S(2)}) collective-permute-start(bf16[1,1,2,2,2,48,2304]{6,5,4,3,2,1,0:T(8,128)(2,1)S(1)} %copy-done.10), channel_id=1, source_target_pairs={{0,4},{2,6},{4,0},{6,2},{8,12},{10,14},{12,8},{14,10},{16,20},{18,... | collective-permute-start | bytes 5308424 | tf_op jit(solution)/shard_map/ppermute | solution.py:202
  232.4 35.0 %collective-permute-start.17 = (bf16[1,1,1,128,1536]{4,3,2,1,0:T(8,128)(2,1)S(1)}, bf16[1,1,1,128,1536]{4,3,2,1,0:T(8,128)(2,1)S(1)}, u32[]{:S(2)}, u32[]{:S(2)}) collective-permute-start(bf16[1,1,1,128,1536]{4,3,2,1,0:T(8,128)(2,1)S(1)} %bitcast.342), channel_id=1, source_target_pairs={{0,16},{2,18},{4,20},{6,22},{8,24},{10,26},{12,28},{14,30},{16,0},... | collective-permute-start | bytes 1179656 | tf_op jit(solution)/shard_map/ppermute | solution.py:202
  235.0 32.5 %collective-permute-start.16 = (bf16[1,1,1,128,1536]{4,3,2,1,0:T(8,128)(2,1)S(1)}, bf16[1,1,1,128,1536]{4,3,2,1,0:T(8,128)(2,1)S(1)}, u32[]{:S(2)}, u32[]{:S(2)}) collective-permute-start(bf16[1,1,1,128,1536]{4,3,2,1,0:T(8,128)(2,1)S(1)} %bitcast.343), channel_id=1, source_target_pairs={{0,8},{2,10},{4,12},{6,14},{8,16},{10,18},{12,20},{14,22},{16,24},... | collective-permute-start | bytes 1179656 | tf_op jit(solution)/shard_map/ppermute | solution.py:202
  273.3 11.6 %collective-permute-start.22 = (bf16[8,2,48,2304]{3,2,1,0:T(8,128)(2,1)}, bf16[8,2,48,2304]{3,2,1,0:T(8,128)(2,1)}, u32[]{:S(2)}, u32[]{:S(2)}) collective-permute-start(bf16[8,2,48,2304]{3,2,1,0:T(8,128)(2,1)} %bitcast.37.w1), channel_id=1, source_target_pairs={{0,1},{1,0},{2,3},{3,2},{4,5},{5,4},{6,7},{7,6},{8,9},{9,8},{10,11... | collective-permute-start | bytes 10616840 | tf_op jit(solution)/shard_map/ppermute | solution.py:289
  342.0 15.4 %collective-permute-start.23 = (bf16[8,2,48,2304]{3,2,1,0:T(8,128)(2,1)}, bf16[8,2,48,2304]{3,2,1,0:T(8,128)(2,1)S(1)}, u32[]{:S(2)}, u32[]{:S(2)}) collective-permute-start(bf16[8,2,48,2304]{3,2,1,0:T(8,128)(2,1)} %get-tuple-element.80), channel_id=1, source_target_pairs={{0,1},{1,0},{2,3},{3,2},{4,5},{5,4},{6,7},{7,6},{8,9},{9,8},{10,11... | collective-permute-start | bytes 10616840 | tf_op jit(solution)/shard_map/ppermute | solution.py:289
  343.7 15.9 %collective-permute-start.24 = (bf16[8,2,48,2304]{3,2,1,0:T(8,128)(2,1)}, bf16[8,2,48,2304]{3,2,1,0:T(8,128)(2,1)S(1)}, u32[]{:S(2)}, u32[]{:S(2)}) collective-permute-start(bf16[8,2,48,2304]{3,2,1,0:T(8,128)(2,1)} %get-tuple-element.82), channel_id=1, source_target_pairs={{0,1},{1,0},{2,3},{3,2},{4,5},{5,4},{6,7},{7,6},{8,9},{9,8},{10,11... | collective-permute-start | bytes 10616840 | tf_op jit(solution)/shard_map/ppermute | solution.py:289
  361.8 40.9 %collective-permute-start.30 = (bf16[1,1,2,2,2,48,2304]{6,5,4,3,2,1,0:T(8,128)(2,1)S(1)}, bf16[1,1,2,2,2,48,2304]{6,5,4,3,2,1,0:T(8,128)(2,1)S(1)}, u32[]{:S(2)}, u32[]{:S(2)}) collective-permute-start(bf16[1,1,2,2,2,48,2304]{6,5,4,3,2,1,0:T(8,128)(2,1)S(1)} %slice.297), channel_id=1, source_target_pairs={{0,4},{2,6},{4,0},{6,2},{8,12},{10,14},{12,8},{14,10},{16,20},{18,... | collective-permute-start | bytes 5308424 | tf_op jit(solution)/shard_map/ppermute | solution.py:202
  364.0 12.3 %collective-permute-start.26 = (bf16[1,1,1,128,1536]{4,3,2,1,0:T(8,128)(2,1)S(1)}, bf16[1,1,1,128,1536]{4,3,2,1,0:T(8,128)(2,1)S(1)}, u32[]{:S(2)}, u32[]{:S(2)}) collective-permute-start(bf16[1,1,1,128,1536]{4,3,2,1,0:T(8,128)(2,1)S(1)} %get-tuple-element.137), channel_id=1, source_target_pairs={{0,24},{2,26},{4,28},{6,30},{8,0},{10,2},{12,4},{14,6},{16,8},{18,... | collective-permute-start | bytes 1179656 | tf_op jit(solution)/shard_map/ppermute | solution.py:202
  364.0 21.7 %collective-permute-start.28 = (bf16[1,1,1,128,1536]{4,3,2,1,0:T(8,128)(2,1)S(1)}, bf16[1,1,1,128,1536]{4,3,2,1,0:T(8,128)(2,1)S(1)}, u32[]{:S(2)}, u32[]{:S(2)}) collective-permute-start(bf16[1,1,1,128,1536]{4,3,2,1,0:T(8,128)(2,1)S(1)} %get-tuple-element.138), channel_id=1, source_target_pairs={{0,8},{2,10},{4,12},{6,14},{8,16},{10,18},{12,20},{14,22},{16,24},... | collective-permute-start | bytes 1179656 | tf_op jit(solution)/shard_map/ppermute | solution.py:202
  366.0 34.2 %collective-permute-start.27 = (bf16[1,1,1,128,1536]{4,3,2,1,0:T(8,128)(2,1)S(1)}, bf16[1,1,1,128,1536]{4,3,2,1,0:T(8,128)(2,1)S(1)}, u32[]{:S(2)}, u32[]{:S(2)}) collective-permute-start(bf16[1,1,1,128,1536]{4,3,2,1,0:T(8,128)(2,1)S(1)} %get-tuple-element.139), channel_id=1, source_target_pairs={{0,16},{2,18},{4,20},{6,22},{8,24},{10,26},{12,28},{14,30},{16,0},... | collective-permute-start | bytes 1179656 | tf_op jit(solution)/shard_map/ppermute | solution.py:202
  368.0 39.6 %collective-permute-start.29 = (bf16[1,2,1,2,2,48,2304]{6,5,4,3,2,1,0:T(8,128)(2,1)S(1)}, bf16[1,2,1,2,2,48,2304]{6,5,4,3,2,1,0:T(8,128)(2,1)S(1)}, u32[]{:S(2)}, u32[]{:S(2)}) collective-permute-start(bf16[1,2,1,2,2,48,2304]{6,5,4,3,2,1,0:T(8,128)(2,1)S(1)} %slice.295), channel_id=1, source_target_pairs={{0,2},{2,0},{4,6},{6,4},{8,10},{10,8},{12,14},{14,12},{16,18},{18,... | collective-permute-start | bytes 5308424 | tf_op jit(solution)/shard_map/ppermute | solution.py:202
  409.2 236.0 %reduce-scatter.5.cloned.1.call-start = ((), (), s32[]{:S(2)}) async-start(), calls=%async_computation.7 | async-start | bytes 4866048 | tf_op jit(solution)/shard_map/reduce_scatter | solution.py:563
  432.5 54.0 %collective-permute-start.34 = (bf16[4,2,2,1,48,1536]{5,4,3,2,1,0:T(8,128)(2,1)}, bf16[4,2,2,1,48,1536]{5,4,3,2,1,0:T(8,128)(2,1)}, u32[]{:S(2)}, u32[]{:S(2)}) collective-permute-start(bf16[4,2,2,1,48,1536]{5,4,3,2,1,0:T(8,128)(2,1)} %constant_dynamic-slice_fusion.15), channel_id=1, source_target_pairs={{0,1},{1,0},{2,3},{3,2},{4,5},{5,4},{6,7},{7,6},{8,9},{9,8},{10,11... | collective-permute-start | bytes 7077896 | tf_op jit(solution)/shard_map/ppermute | solution.py:289
  457.1 14.8 %collective-permute-start.31 = (bf16[4,1,1,128,512]{4,3,2,1,0:T(8,128)(2,1)S(1)}, bf16[4,1,1,128,512]{4,3,2,1,0:T(8,128)(2,1)S(1)}, u32[]{:S(2)}, u32[]{:S(2)}) collective-permute-start(bf16[4,1,1,128,512]{4,3,2,1,0:T(8,128)(2,1)S(1)} %get-tuple-element.130), channel_id=1, source_target_pairs={{0,2},{2,0},{4,6},{6,4},{8,10},{10,8},{12,14},{14,12},{16,18},{18,... | collective-permute-start | bytes 1572872 | tf_op jit(solution)/shard_map/ppermute | solution.py:202
  458.2 24.8 %collective-permute-start.33 = (bf16[4,1,1,128,512]{4,3,2,1,0:T(8,128)(2,1)S(1)}, bf16[4,1,1,128,512]{4,3,2,1,0:T(8,128)(2,1)S(1)}, u32[]{:S(2)}, u32[]{:S(2)}) collective-permute-start(bf16[4,1,1,128,512]{4,3,2,1,0:T(8,128)(2,1)S(1)} %get-tuple-element.131), channel_id=1, source_target_pairs={{0,6},{2,4},{4,2},{6,0},{8,14},{10,12},{12,10},{14,8},{16,22},{18,... | collective-permute-start | bytes 1572872 | tf_op jit(solution)/shard_map/ppermute | solution.py:202
  459.4 25.0 %collective-permute-start.32 = (bf16[4,1,1,128,512]{4,3,2,1,0:T(8,128)(2,1)S(1)}, bf16[4,1,1,128,512]{4,3,2,1,0:T(8,128)(2,1)S(1)}, u32[]{:S(2)}, u32[]{:S(2)}) collective-permute-start(bf16[4,1,1,128,512]{4,3,2,1,0:T(8,128)(2,1)S(1)} %get-tuple-element.132), channel_id=1, source_target_pairs={{0,4},{2,6},{4,0},{6,2},{8,12},{10,14},{12,8},{14,10},{16,20},{18,... | collective-permute-start | bytes 1572872 | tf_op jit(solution)/shard_map/ppermute | solution.py:202
  490.9 21.0 %collective-permute-start.39 = (bf16[1,1,1,2,2,48,2304]{6,5,4,3,2,1,0:T(8,128)(2,1)}, bf16[1,1,1,2,2,48,2304]{6,5,4,3,2,1,0:T(8,128)(2,1)}, u32[]{:S(2)}, u32[]{:S(2)}) collective-permute-start(bf16[1,1,1,2,2,48,2304]{6,5,4,3,2,1,0:T(8,128)(2,1)} %slice.319), channel_id=1, source_target_pairs={{0,2},{2,0},{4,6},{6,4},{8,10},{10,8},{12,14},{14,12},{16,18},{18,... | collective-permute-start | bytes 2654216 | tf_op jit(solution)/shard_map/ppermute | solution.py:202
  494.6 11.9 %collective-permute-start.36 = (bf16[1,1,1,128,512]{4,3,2,1,0:T(8,128)(2,1)S(1)}, bf16[1,1,1,128,512]{4,3,2,1,0:T(8,128)(2,1)}, u32[]{:S(2)}, u32[]{:S(2)}) collective-permute-start(bf16[1,1,1,128,512]{4,3,2,1,0:T(8,128)(2,1)S(1)} %get-tuple-element.156), channel_id=1, source_target_pairs={{0,16},{2,18},{4,20},{6,22},{8,24},{10,26},{12,28},{14,30},{16,0},... | collective-permute-start | bytes 393224 | tf_op jit(solution)/shard_map/ppermute | solution.py:202
  502.6 19.5 %collective-permute-start.38 = (bf16[1,1,1,2,2,48,2304]{6,5,4,3,2,1,0:T(8,128)(2,1)S(1)}, bf16[1,1,1,2,2,48,2304]{6,5,4,3,2,1,0:T(8,128)(2,1)S(1)}, u32[]{:S(2)}, u32[]{:S(2)}) collective-permute-start(bf16[1,1,1,2,2,48,2304]{6,5,4,3,2,1,0:T(8,128)(2,1)S(1)} %slice.317), channel_id=1, source_target_pairs={{0,4},{2,6},{4,0},{6,2},{8,12},{10,14},{12,8},{14,10},{16,20},{18,... | collective-permute-start | bytes 2654216 | tf_op jit(solution)/shard_map/ppermute | solution.py:202
  523.8 112.2 %all-to-all-start.1 = ((bf16[4,2,48,2304]{3,2,1,0:T(8,128)(2,1)}), bf16[4,2,48,2304]{3,2,1,0:T(8,128)(2,1)}, u32[]{:S(2)}, u32[]{:S(2)}) async-start(bf16[4,2,48,2304]{3,2,1,0:T(8,128)(2,1)} %pad_maximum_fusion.7), calls=%async_computation.3 | async-start | bytes 3538944 | tf_op jit(solution)/shard_map/all_to_all | solution.py:615
  537.4 18.6 %collective-permute-start.40 = (bf16[4,1,1,1,48,1536]{5,4,3,2,1,0:T(8,128)(2,1)}, bf16[4,1,1,1,48,1536]{5,4,3,2,1,0:T(8,128)(2,1)}, u32[]{:S(2)}, u32[]{:S(2)}) collective-permute-start(bf16[4,1,1,1,48,1536]{5,4,3,2,1,0:T(8,128)(2,1)} %get-tuple-element.127), channel_id=1, source_target_pairs={{0,2},{2,0},{4,6},{6,4},{8,10},{10,8},{12,14},{14,12},{16,18},{18,... | collective-permute-start | bytes 1769480 | tf_op jit(solution)/shard_map/ppermute | solution.py:202
  539.9 61.5 %collective-permute-start.45 = (bf16[1,1,2,1,280,768]{5,4,3,2,1,0:T(8,128)(2,1)}, bf16[1,1,2,1,280,768]{5,4,3,2,1,0:T(8,128)(2,1)S(1)}, u32[]{:S(2)}, u32[]{:S(2)}) collective-permute-start(bf16[1,1,2,1,280,768]{5,4,3,2,1,0:T(8,128)(2,1)} %constant_dynamic-slice_fusion.10), channel_id=1, source_target_pairs={{0,4},{2,6},{4,0},{6,2},{8,12},{10,14},{12,8},{14,10},{16,20},{18,... | collective-permute-start | bytes 2580488 | tf_op jit(solution)/shard_map/ppermute | solution.py:202
  541.4 60.2 %collective-permute-start.44 = (bf16[1,2,1,1,280,768]{5,4,3,2,1,0:T(8,128)(2,1)S(1)}, bf16[1,2,1,1,280,768]{5,4,3,2,1,0:T(8,128)(2,1)S(1)}, u32[]{:S(2)}, u32[]{:S(2)}) collective-permute-start(bf16[1,2,1,1,280,768]{5,4,3,2,1,0:T(8,128)(2,1)S(1)} %constant_dynamic-slice_fusion.11), channel_id=1, source_target_pairs={{0,2},{2,0},{4,6},{6,4},{8,10},{10,8},{12,14},{14,12},{16,18},{18,... | collective-permute-start | bytes 2580488 | tf_op jit(solution)/shard_map/ppermute | solution.py:202
  542.2 49.9 %collective-permute-start.42 = (bf16[4,1,1,1,48,1536]{5,4,3,2,1,0:T(8,128)(2,1)}, bf16[4,1,1,1,48,1536]{5,4,3,2,1,0:T(8,128)(2,1)S(1)}, u32[]{:S(2)}, u32[]{:S(2)}) collective-permute-start(bf16[4,1,1,1,48,1536]{5,4,3,2,1,0:T(8,128)(2,1)} %get-tuple-element.128), channel_id=1, source_target_pairs={{0,6},{2,4},{4,2},{6,0},{8,14},{10,12},{12,10},{14,8},{16,22},{18,... | collective-permute-start | bytes 1769480 | tf_op jit(solution)/shard_map/ppermute | solution.py:202
  543.4 56.4 %collective-permute-start.41 = (bf16[4,1,1,1,48,1536]{5,4,3,2,1,0:T(8,128)(2,1)}, bf16[4,1,1,1,48,1536]{5,4,3,2,1,0:T(8,128)(2,1)S(1)}, u32[]{:S(2)}, u32[]{:S(2)}) collective-permute-start(bf16[4,1,1,1,48,1536]{5,4,3,2,1,0:T(8,128)(2,1)} %get-tuple-element.129), channel_id=1, source_target_pairs={{0,4},{2,6},{4,0},{6,2},{8,12},{10,14},{12,8},{14,10},{16,20},{18,... | collective-permute-start | bytes 1769480 | tf_op jit(solution)/shard_map/ppermute | solution.py:202
  556.0 45.9 %collective-permute-start.43 = (bf16[4,2,2,1,48,768]{5,4,3,2,1,0:T(8,128)(2,1)S(1)}, bf16[4,2,2,1,48,768]{5,4,3,2,1,0:T(8,128)(2,1)S(1)}, u32[]{:S(2)}, u32[]{:S(2)}) collective-permute-start(bf16[4,2,2,1,48,768]{5,4,3,2,1,0:T(8,128)(2,1)S(1)} %fusion.47), channel_id=1, source_target_pairs={{0,1},{1,0},{2,3},{3,2},{4,5},{5,4},{6,7},{7,6},{8,9},{9,8},{10,11... | collective-permute-start | bytes 3538952 | tf_op jit(solution)/shard_map/ppermute | solution.py:289
  605.9 28.4 %collective-permute-start.56 = (bf16[1,1,1,1,280,768]{5,4,3,2,1,0:T(8,128)(2,1)S(1)}, bf16[1,1,1,1,280,768]{5,4,3,2,1,0:T(8,128)(2,1)S(1)}, u32[]{:S(2)}, u32[]{:S(2)}) collective-permute-start(bf16[1,1,1,1,280,768]{5,4,3,2,1,0:T(8,128)(2,1)S(1)} %constant_dynamic-slice_fusion.18), channel_id=1, source_target_pairs={{0,2},{2,0},{4,6},{6,4},{8,10},{10,8},{12,14},{14,12},{16,18},{18,... | collective-permute-start | bytes 1290248 | tf_op jit(solution)/shard_map/ppermute | solution.py:202
  606.9 27.5 %collective-permute-start.55 = (bf16[1,1,1,1,280,768]{5,4,3,2,1,0:T(8,128)(2,1)S(1)}, bf16[1,1,1,1,280,768]{5,4,3,2,1,0:T(8,128)(2,1)S(1)}, u32[]{:S(2)}, u32[]{:S(2)}) collective-permute-start(bf16[1,1,1,1,280,768]{5,4,3,2,1,0:T(8,128)(2,1)S(1)} %constant_dynamic-slice_fusion), channel_id=1, source_target_pairs={{0,4},{2,6},{4,0},{6,2},{8,12},{10,14},{12,8},{14,10},{16,20},{18,... | collective-permute-start | bytes 1290248 | tf_op jit(solution)/shard_map/ppermute | solution.py:202
  (80 other events, 727.4 us)
Sparse Core Ops, SparseCore 0:
  11.5 92.7 all-gather.2
  107.1 85.4 all-gather.4
  409.3 32.8 reduce-scatter.2
  501.4 128.9 reduce-scatter.4

commit v3 on v2

--- a/solution.py
+++ b/solution.py
@@ -88,6 +88,101 @@
 
 def dot_tn(a, b):
     return lax.dot_general(a, b, (((0,), (0,)), ((), ())), preferred_element_type=jnp.float32)
+
+
+def side_by_side(values, first, count):
+    return jnp.concatenate(
+        [values[:, (first + h) * HD : (first + h + 1) * HD] for h in range(count)], axis=0
+    )
+
+
+def attend_kernel(queries, keys_values, hidden_by, mixed, attended, log_total):
+    group_size = H // KV
+    tokens = queries.shape[0]
+    for g in range(KV):
+        query = side_by_side(queries[...], g * group_size, group_size)
+        keys = keys_values[:, g * HD : (g + 1) * HD]
+        values = keys_values[:, (KV + g) * HD : (KV + g + 1) * HD]
+        scores = dot_nt(keys, query) * HD ** (-0.5)
+        scores = scores + jnp.concatenate([hidden_by[...]] * group_size, axis=1)
+        top = jnp.max(scores, axis=0, keepdims=True)
+        weights = jnp.exp(scores - top)
+        total = jnp.sum(weights, axis=0, keepdims=True)
+        result = dot_tn(values, weights.astype(low)) / total
+        log_total[g : g + 1, :] = top + jnp.log(total)
+        for h in range(group_size):
+            turned = result[:, h * tokens : (h + 1) * tokens].T
+            spot = slice((g * group_size + h) * HD, (g * group_size + h + 1) * HD)
+            mixed[:, spot] = turned
+            attended[:, spot] = turned.astype(low)
+
+
+def attend(queries, keys_values, hidden_by):
+    tokens, width = queries.shape
+    columns = H // KV * tokens
+    pairs = keys_values.shape[0] * H * tokens
+    return pl.pallas_call(
+        attend_kernel,
+        out_shape=[
+            jax.ShapeDtypeStruct((tokens, width), jnp.float32),
+            jax.ShapeDtypeStruct((tokens, width), low),
+            jax.ShapeDtypeStruct((KV, columns), jnp.float32),
+        ],
+        compiler_params=pltpu.CompilerParams(vmem_limit_bytes=50 * 1024 * 1024),
+        cost_estimate=pl.CostEstimate(
+            flops=4 * pairs * HD, bytes_accessed=2 * keys_values.size, transcendentals=pairs
+        ),
+    )(queries, keys_values, hidden_by)
+
+
+def attend_back_kernel(queries, keys_values, hidden_by, mixed, log_total, mixed_grad, query_grad, kv_grad):
+    group_size = H // KV
+    tokens = queries.shape[0]
+    total_keys = keys_values.shape[0]
+    chunk = min(total_keys, 512)
+    scale = HD ** (-0.5)
+    for g in range(KV):
+        query = side_by_side(queries[...], g * group_size, group_size)
+        incoming = side_by_side(mixed_grad[...], g * group_size, group_size)
+        rows = []
+        for h in range(group_size):
+            spot = slice((g * group_size + h) * HD, (g * group_size + h + 1) * HD)
+            product = mixed_grad[:, spot].astype(jnp.float32) * mixed[:, spot]
+            rows.append(jnp.sum(product.T, axis=0, keepdims=True))
+        row_dot = jnp.concatenate(rows, axis=1)
+        turned_grad = jnp.zeros((HD, group_size * tokens), jnp.float32)
+        for start in range(0, total_keys, chunk):
+            part = slice(start, start + chunk)
+            keys = keys_values[part, g * HD : (g + 1) * HD]
+            values = keys_values[part, (KV + g) * HD : (KV + g + 1) * HD]
+            scores = dot_nt(keys, query) * scale
+            scores = scores + jnp.concatenate([hidden_by[part, :]] * group_size, axis=1)
+            probs = jnp.exp(scores - log_total[g : g + 1, :])
+            score_grad = (probs * (dot_nt(values, incoming) - row_dot)).astype(low)
+            kv_grad[part, g * HD : (g + 1) * HD] = (dot_nn(score_grad, query) * scale).astype(low)
+            kv_grad[part, (KV + g) * HD : (KV + g + 1) * HD] = dot_nn(
+                probs.astype(low), incoming
+            ).astype(low)
+            turned_grad += dot_tn(keys, score_grad)
+        for h in range(group_size):
+            spot = slice((g * group_size + h) * HD, (g * group_size + h + 1) * HD)
+            query_grad[:, spot] = turned_grad[:, h * tokens : (h + 1) * tokens].T * scale
+
+
+def attend_back(queries, keys_values, hidden_by, mixed, log_total, mixed_grad):
+    tokens, width = queries.shape
+    pairs = keys_values.shape[0] * H * tokens
+    return pl.pallas_call(
+        attend_back_kernel,
+        out_shape=[
+            jax.ShapeDtypeStruct((tokens, width), jnp.float32),
+            jax.ShapeDtypeStruct(keys_values.shape, low),
+        ],
+        compiler_params=pltpu.CompilerParams(vmem_limit_bytes=50 * 1024 * 1024),
+        cost_estimate=pl.CostEstimate(
+            flops=10 * pairs * HD, bytes_accessed=4 * keys_values.size, transcendentals=pairs
+        ),
+    )(queries, keys_values, hidden_by, mixed, log_total, mixed_grad)
 
 
 def ff_tile(tokens, cots, gate, up, down):
@@ -325,8 +420,6 @@
     tok_dev, width = tokens_in.shape[1], tokens_in.shape[2]
     block_len = tok_dev // BLOCKS_DEV
     prompt_len = tok_dev * ctx_size // 2
-    group_size = H // KV
-    score_scale = HD ** (-0.5)
     width_q = H * HD
     width_kv = KV * HD
     deal_row = deal_table[0]
@@ -443,16 +536,16 @@
         return parts
 
     down_parts = gather_far(down_parts, 0)
-    gathered, out_weight, gate_up, cot_all, down_parts = together(
-        gathered, out_weight, gate_up, cot_all, down_parts
-    )
-    gate_up = lax.all_to_all(
-        gate_up, "ctx", split_axis=0, concat_axis=0, tiled=True, axis_index_groups=groups
-    )
-    few = ff_size // 2
-    far_parts = [gate_up[:few], gate_up[few:]]
-    far_parts = gather_far([p.reshape(ones + p.shape) for p in far_parts], 0)
+    cot_all, down_parts = together(cot_all, down_parts)
     down_parts = gather_far(down_parts, 1)
+    for a in far_axes:
+        down_parts = [grid.ordered(p, a) for p in down_parts]
+    down = jnp.concatenate([p[..., None, :, :] for p in down_parts], axis=-1)
+    down = both_cores(down, core, grid.rank).reshape(ff_cols, width)
+    down = jnp.pad(down, ((0, ff_room - ff_cols), (0, 0)))
+    gathered, out_weight, gate_up, cot_all, down = together(
+        gathered, out_weight, gate_up, cot_all, down
+    )
     full_out = lax.all_gather(out_weight, ("ctx", "fsdp"), axis=0, tiled=True)
 
     full_qkv = gathered[:, : width_q + 2 * width_kv]
@@ -472,51 +565,35 @@
         projected[:, width_q : width_q + width_kv].reshape(tok_dev, KV, HD), cosine, sine_table
     ).astype(low)
     value_low = projected[:, width_q + width_kv :].astype(low)
-    query_group = query_low.reshape(tok_dev, KV, group_size, HD)
+    query_low = query_low.reshape(tok_dev, width_q)
 
     kv_all = jnp.concatenate([key_low.reshape(tok_dev, width_kv), value_low], axis=1)
     kv_all = grid.gather_stage(kv_all.reshape(ones + kv_all.shape), wide_orders[0][0])
-    kv_all, down_parts = together(kv_all, down_parts)
+    kv_all, gate_up = together(kv_all, gate_up)
+    gate_up = lax.all_to_all(
+        gate_up, "ctx", split_axis=0, concat_axis=0, tiled=True, axis_index_groups=groups
+    )
     for stage in range(1, len(wide_orders[0])):
         kv_all = grid.gather_stage(kv_all, wide_orders[0][stage])
     kv_all = kv_all.reshape(-1, 2 * width_kv)
-    total_keys = kv_all.shape[0]
-    key_all = kv_all[:, :width_kv].reshape(total_keys, KV, HD)
-    value_all = kv_all[:, width_kv:].reshape(total_keys, KV, HD)
     row_ids = []
     for a, b in zip(token_bounds[:-1], token_bounds[1:]):
         chips, rows = grid.source_rows(a, b - a, all_axes)
         row_ids.append((chips * tok_dev + rows).reshape(-1))
     row_ids = jnp.concatenate(row_ids)
     key_seq, key_pos = key_meta(deal_row, row_ids, block_len, prompt_len)
-    allowed = visible_pairs(query_seq, query_pos, key_seq, key_pos)[:, None, None, :]
-
-    scores = (
-        jnp.einsum("tkgd,nkd->tkgn", query_group, key_all, preferred_element_type=jnp.float32)
-        * score_scale
-    )
-    scores = jnp.where(allowed, scores, neg_large)
-    top = jnp.max(scores, axis=-1)
-    weights = jnp.exp(scores - top[..., None])
-    weight_sum = jnp.sum(weights, axis=-1)
-    mixed = (
-        jnp.einsum(
-            "tkgn,nkd->tkgd", weights.astype(low), value_all, preferred_element_type=jnp.float32
-        )
-        / weight_sum[..., None]
-    )
-    log_total = top + jnp.log(weight_sum)
-    attended = mixed.reshape(tok_dev, width_q).astype(low)
+    allowed = visible_pairs(query_seq, query_pos, key_seq, key_pos).T
+    hidden_by = jnp.where(allowed, 0.0, neg_large).astype(jnp.float32)
+    mixed, attended, log_total = attend(query_low, kv_all, hidden_by)
+    attended, gate_up = together(attended, gate_up)
+    few = ff_size // 2
+    far_parts = [gate_up[:few], gate_up[few:]]
+    far_parts = gather_far([p.reshape(ones + p.shape) for p in far_parts], 0)
     resid = hidden_in + jnp.dot(attended, full_out, preferred_element_type=jnp.float32)
     normed_mlp = (rms_scale(resid) * full_mlp_gain).astype(low)
 
     arranged = jnp.dot(normed_mlp, arrival, preferred_element_type=jnp.float32).astype(low)
-    for a in far_axes:
-        down_parts = [grid.ordered(p, a) for p in down_parts]
-    down = jnp.concatenate([p[..., None, :, :] for p in down_parts], axis=-1)
-    down = both_cores(down, core, grid.rank).reshape(ff_cols, width)
-    down = jnp.pad(down, ((0, ff_room - ff_cols), (0, 0)))
-    arranged, far_parts, down = together(arranged, far_parts, down)
+    arranged, far_parts = together(arranged, far_parts)
     mlp_all = gather_tokens(arranged, ff_bounds, ff_orders)
     far_parts = gather_far(far_parts, 1)
     mlp_all, far_parts = together(mlp_all, far_parts)
@@ -540,12 +617,14 @@
     down_grad = down_grad[:ff_cols].reshape(far_lead + (2, rows_d, width))
     down_grad = own_core_sum(down_grad, core, grid.rank)
     down_grads = [down_grad[..., :half], down_grad[..., half:]]
-    mlp_partial, far_grads, down_grads = together(mlp_partial, far_grads, down_grads)
+    mlp_partial, far_grads = together(mlp_partial, far_grads)
     mlp_parts = cut_tokens(mlp_partial, ff_bounds, ff_axes)
     for stage in range(ff_stages):
         mlp_parts = grid.scatter_round(mlp_parts, ff_orders, stage, False)
     far_grads = scatter_far(far_grads, 0, False)
-    mlp_parts, far_grads, out_partial = together(mlp_parts, far_grads, out_partial)
+    mlp_parts, far_grads, out_partial, down_grads = together(
+        mlp_parts, far_grads, out_partial, down_grads
+    )
     out_sum = lax.psum_scatter(
         out_partial.reshape(-1, width),
         "ctx",
@@ -560,38 +639,16 @@
     resid_grad = out_grad + resid_part
     resid_low = resid_grad.astype(low)
     out_w_grad = jnp.einsum("tq,td->qd", attended, resid_low, preferred_element_type=jnp.float32)
+    out_w_grad, resid_low = together(out_w_grad.astype(low), resid_low)
     out_w_sum = lax.psum_scatter(
-        out_w_grad.astype(low), ("ctx", "fsdp"), scatter_dimension=0, tiled=True
-    )
-    mixed_grad = (
-        jnp.einsum("td,qd->tq", resid_low, full_out, preferred_element_type=jnp.float32)
-        .astype(low)
-        .reshape(tok_dev, KV, group_size, HD)
-    )
-    row_dot = jnp.sum(mixed_grad.astype(jnp.float32) * mixed, axis=-1)
-    scores = (
-        jnp.einsum("tkgd,nkd->tkgn", query_group, key_all, preferred_element_type=jnp.float32)
-        * score_scale
-    )
-    probs = jnp.exp(jnp.where(allowed, scores - log_total[..., None], neg_large))
-    prob_grad = jnp.einsum(
-        "tkgd,nkd->tkgn", mixed_grad, value_all, preferred_element_type=jnp.float32
-    )
-    score_grad = (probs * (prob_grad - row_dot[..., None])).astype(low)
-    query_rot = (
-        jnp.einsum("tkgn,nkd->tkgd", score_grad, key_all, preferred_element_type=jnp.float32)
-        * score_scale
-    )
-    key_rot = (
-        jnp.einsum("tkgn,tkgd->nkd", score_grad, query_group, preferred_element_type=jnp.float32)
-        * score_scale
-    )
-    value_rot = jnp.einsum(
-        "tkgn,tkgd->nkd", probs.astype(low), mixed_grad, preferred_element_type=jnp.float32
-    )
-    kv_partial = jnp.concatenate(
-        [key_rot.reshape(total_keys, width_kv), value_rot.reshape(total_keys, width_kv)], axis=1
+        out_w_grad, ("ctx", "fsdp"), scatter_dimension=0, tiled=True
+    )
+    mixed_grad = jnp.einsum(
+        "td,qd->tq", resid_low, full_out, preferred_element_type=jnp.float32
     ).astype(low)
+    query_rot, kv_partial = attend_back(
+        query_low, kv_all, hidden_by, mixed, log_total, mixed_grad
+    )
     query_grad = rope_back(query_rot.reshape(tok_dev, H, HD), cosine, sine_table)
     query_grad = query_grad.reshape(tok_dev, width_q)
     query_parts = cut_columns(

time: 665 us -> 648 us (0.974)
  matrix products: 60.8 us -> 28.3 us
  Pallas kernels: 49.7 us -> 67 us
  waiting for transfers between devices: 302 us -> 290 us
    all_gather x1, waiting for transfers between devices: 45.8 us -> 0.01 us  [shards(): lax.all_gather(jnp.concatenate([qkv_weight, side_rows], axis=1), ('ctx',...]
    dot_general x6 -> x0, matrix products: 33.1 us -> none  [the longest x1 8.88 us: shards(): jnp.einsum('tkgn,tkgd->nkd', probs.astype(low), mixed_grad, preferred_ele...]
    ppermute x49, waiting for transfers between devices: 237 us -> 265 us  [hop(): return lax.ppermute(values, 'ctx', pairs)]
    pallas_call x0 -> x2, Pallas kernels: none -> 17.5 us  [the longest x1 11 us: attend_back(): pl.pallas_call(attend_back_kernel, out_shape=[jax.ShapeDtypeStruct((token...]
    all_to_all x1, waiting for transfers between devices: 0.01 us -> 14.3 us  [shards(): lax.all_to_all(gate_up, 'ctx', split_axis=0, concat_axis=0, tiled=True, a...]
    concatenate x4 -> x2, local copies, waits for them, and re-layouts: 11.3 us -> 1.21 us  [the longest x1 1.15 us: rotate_half(): jnp.concatenate([-values[..., half_dim:], values[..., :half_dim]], axis=-1)]
    unnamed x139 -> x125, local copies, waits for them, and re-layouts: 15.1 us -> 6.41 us
    ppermute x8, waiting for transfers between devices: 19.2 us -> 11.1 us  [other_core(): return lax.ppermute(values, 'fsdp', [(0, 1), (1, 0)])]
  transfers between devices with their start and end apart: 63 -> 63, of which waited for: 33 -> 36; matrix products, arithmetic and copies ran while one was open for 27% -> 22% of each run, Pallas kernels for 0% -> 1%
where the time goes in v3:
time: 648 us; the launch traced here: 637 us
  waiting for transfers between devices  290 us (45%)
  other arithmetic  83 us (13%)
  starting transfers between devices  82.7 us (13%)
  local copies, waits for them, and re-layouts  70.6 us (11%)
  Pallas kernels  67 us (10%)
  matrix products  28.3 us (4%)
  between operations  15.6 us (2%)
    ppermute x49, waiting for transfers between devices, hop(): return lax.ppermute(values, 'ctx', pairs)  265 us
    ppermute x49, starting transfers between devices, hop(): return lax.ppermute(values, 'ctx', pairs)  71.9 us
    pallas_call x1, Pallas kernels, feed_forward(): pl.pallas_call(ff_kernel, grid=(columns // tile,), in_specs=[whole, whole...  49.5 us
    convert_element_type x12, other arithmetic, scatter_stage(): return total.astype(values.dtype)  16.4 us
    concatenate x10, other arithmetic, join(): jnp.concatenate([join(prefix + (j,)) for j in range(self.axes[axes[depth]...  15 us
    all_to_all x1, waiting for transfers between devices, shards(): lax.all_to_all(gate_up, 'ctx', split_axis=0, concat_axis=0, tiled=True, a...  14.3 us
  transfers between devices with their start and end apart: 63, of which 36 were waited for; matrix products, arithmetic and copies ran while one was open for 22% of the time, Pallas kernels for 1%

profile of v3, /device:TPU:0, one launch (start us, length us, event | category | flops | bytes accessed | tf_op | source)
XLA Modules:
  0.0 637.4 jit_solution(6057998687068938315)
XLA Ops:
  9.8 5.1 collective-permute-start.2
  20.1 5.6 collective-permute-done.2
  25.8 27.6 %collective-permute-done.1 = bf16[1,1,1,128,1536]{4,3,2,1,0:T(8,128)(2,1)S(1)} collective-permute-done((bf16[1,1,1,128,1536]{4,3,2,1,0:T(8,128)(2,1)}, bf16[1,1,1,128,1536]{4,3,2,1,0:T(8,128)(2,1)S(1)}, u32[]{:S(2)}, u32[]{:S(2)}) %collective-permute-start.1) | collective-permute-done | bytes 393248 | tf_op jit(solution)/shard_map/ppermute | solution.py:297
  58.1 20.0 %collective-permute-done.6 = bf16[1,1,2,280,768]{4,3,2,1,0:T(8,128)(2,1)S(1)} collective-permute-done((bf16[1,1,2,280,768]{4,3,2,1,0:T(8,128)(2,1)S(1)}, bf16[1,1,2,280,768]{4,3,2,1,0:T(8,128)(2,1)S(1)}, u32[]{:S(2)}, u32[]{:S(2)}) %collective-permute-start.6) | collective-permute-done | bytes 860192 | tf_op jit(solution)/shard_map/ppermute | solution.py:297
  79.0 3.5 collective-permute-done.5
  88.7 3.4 reshape.599
  94.3 3.4 reshape.598
  102.9 4.0 broadcast_select_fusion.1
  109.6 3.3 pad.22.down
  115.0 3.9 fusion.8
  126.5 11.9 %collective-permute-done.9 = bf16[1,1,1,128,512]{4,3,2,1,0:T(8,128)(2,1)S(1)} collective-permute-done((bf16[1,1,1,128,512]{4,3,2,1,0:T(8,128)(2,1)S(1)}, bf16[1,1,1,128,512]{4,3,2,1,0:T(8,128)(2,1)S(1)}, u32[]{:S(2)}, u32[]{:S(2)}) %collective-permute-start.9) | collective-permute-done | bytes 131104 | tf_op jit(solution)/shard_map/ppermute | solution.py:297
  139.3 4.6 all-to-all-start
  155.8 10.9 %collective-permute-done.13 = bf16[4,1,1,128,512]{4,3,2,1,0:T(8,128)(2,1)S(1)} collective-permute-done((bf16[4,1,1,128,512]{4,3,2,1,0:T(8,128)(2,1)}, bf16[4,1,1,128,512]{4,3,2,1,0:T(8,128)(2,1)S(1)}, u32[]{:S(2)}, u32[]{:S(2)}) %collective-permute-start.13) | collective-permute-done | bytes 524320 | tf_op jit(solution)/shard_map/ppermute | solution.py:297
  166.7 14.0 %collective-permute-done.12 = bf16[4,1,1,128,512]{4,3,2,1,0:T(8,128)(2,1)S(1)} collective-permute-done((bf16[4,1,1,128,512]{4,3,2,1,0:T(8,128)(2,1)}, bf16[4,1,1,128,512]{4,3,2,1,0:T(8,128)(2,1)S(1)}, u32[]{:S(2)}, u32[]{:S(2)}) %collective-permute-start.12) | collective-permute-done | bytes 524320 | tf_op jit(solution)/shard_map/ppermute | solution.py:297
  182.2 6.6 %shard_map.221 = (f32[128,1536]{1,0:T(8,128)S(1)}, bf16[128,1536]{1,0:T(8,128)(2,1)S(1)}, f32[2,768]{1,0:T(2,128)S(1)}) custom-call(bf16[128,1536]{1,0:T(8,128)(2,1)S(1)} %add_convert_fusion.13.queries, bf16[2048,512]{1,0:T(8,128)(2,1)} %bitcast.192, f32[2048,128]{1,0:T(8,128)S(1)} %fusion.27.hidden_by), custom_call_target="tpu_custom_call" | custom-call | flops 1610612736 | bytes 2097152 | tf_op jit(solution)/shard_map/pallas_call | solution.py:124
  188.8 14.3 %all-to-all-done = bf16[4,2,48,2304]{3,2,1,0:T(8,128)(2,1)} async-done(((bf16[4,2,48,2304]{3,2,1,0:T(8,128)(2,1)}), bf16[4,2,48,2304]{3,2,1,0:T(8,128)(2,1)}, u32[]{:S(2)}, u32[]{:S(2)}) %all-to-all-start) | async-done | bytes 1769504 | tf_op jit(solution)/shard_map/all_to_all | solution.py:573
  210.5 16.9 %collective-permute-done.14 = bf16[1,1,1,2,2,48,2304]{6,5,4,3,2,1,0:T(8,128)(2,1)} collective-permute-done((bf16[1,1,1,2,2,48,2304]{6,5,4,3,2,1,0:T(8,128)(2,1)}, bf16[1,1,1,2,2,48,2304]{6,5,4,3,2,1,0:T(8,128)(2,1)}, u32[]{:S(2)}, u32[]{:S(2)}) %collective-permute-start.14) | collective-permute-done | bytes 884768 | tf_op jit(solution)/shard_map/ppermute | solution.py:297
  244.2 9.1 %collective-permute-done.18 = bf16[1,1,1,128,1536]{4,3,2,1,0:T(8,128)(2,1)S(1)} collective-permute-done((bf16[1,1,1,128,1536]{4,3,2,1,0:T(8,128)(2,1)S(1)}, bf16[1,1,1,128,1536]{4,3,2,1,0:T(8,128)(2,1)S(1)}, u32[]{:S(2)}, u32[]{:S(2)}) %collective-permute-start.18) | collective-permute-done | bytes 393248 | tf_op jit(solution)/shard_map/ppermute | solution.py:297
  253.2 21.5 %collective-permute-done.17 = bf16[1,1,1,128,1536]{4,3,2,1,0:T(8,128)(2,1)S(1)} collective-permute-done((bf16[1,1,1,128,1536]{4,3,2,1,0:T(8,128)(2,1)S(1)}, bf16[1,1,1,128,1536]{4,3,2,1,0:T(8,128)(2,1)S(1)}, u32[]{:S(2)}, u32[]{:S(2)}) %collective-permute-start.17) | collective-permute-done | bytes 393248 | tf_op jit(solution)/shard_map/ppermute | solution.py:297
  282.5 6.1 collective-permute-done.21.w2
  288.6 5.1 collective-permute-done.22.w3
  293.6 49.5 %shard_map.222 = (bf16[512,1536]{1,0:T(8,128)(2,1)S(1)}, bf16[512,1536]{1,0:T(8,128)(2,1)S(1)}, bf16[8,2,48,2304]{3,2,1,0:T(8,128)(2,1)}, bf16[8,2,48,2304]{3,2,...) custom-call(bf16[512,1536]{1,0:T(8,128)(2,1)} %bitcast.195, ...), custom_call_target="tpu_custom_call" | custom-call | flops 32614907904 | bytes 51904512 | tf_op jit(solution)/shard_map/pallas_call | solution.py:258
  343.7 3.4 slice.289
  369.6 4.7 collective-permute-done.27
  374.2 15.9 %collective-permute-done.26 = bf16[1,1,1,128,1536]{4,3,2,1,0:T(8,128)(2,1)} collective-permute-done((bf16[1,1,1,128,1536]{4,3,2,1,0:T(8,128)(2,1)S(1)}, bf16[1,1,1,128,1536]{4,3,2,1,0:T(8,128)(2,1)}, u32[]{:S(2)}, u32[]{:S(2)}) %collective-permute-start.26) | collective-permute-done | bytes 393248 | tf_op jit(solution)/shard_map/ppermute | solution.py:297
  391.6 7.7 %collective-permute-done.28 = bf16[1,2,1,2,2,48,2304]{6,5,4,3,2,1,0:T(8,128)(2,1)} collective-permute-done((bf16[1,2,1,2,2,48,2304]{6,5,4,3,2,1,0:T(8,128)(2,1)S(1)}, bf16[1,2,1,2,2,48,2304]{6,5,4,3,2,1,0:T(8,128)(2,1)}, u32[]{:S(2)}, u32[]{:S(2)}) %collective-permute-start.28) | collective-permute-done | bytes 1769504 | tf_op jit(solution)/shard_map/ppermute | solution.py:297
  402.4 3.5 collective-permute-done.29
  413.8 3.7 convolution_convert_fusion.1
  417.5 4.1 convolution_convert_fusion.3.mixed_grad
  421.6 11.0 %shard_map.223 = (f32[128,1536]{1,0:T(8,128)S(1)}, bf16[2048,512]{1,0:T(8,128)(2,1)}) custom-call(bf16[128,1536]{1,0:T(8,128)(2,1)S(1)} %add_convert_fusion.13.queries, bf16[2048,512]{1,0:T(8,128)(2,1)} %bitcast.193, f32[2048,128]{1,0:T(8,128)S(1)} %fusion.27.hidden_by, f32[128,1536]{1,0:T(8,128)S(1)} %get-tuple-element.101.mixed, ...), custom_call_target="tpu_custom_call" | custom-call | flops 4026531840 | bytes 4194304 | tf_op jit(solution)/shard_map/pallas_call | solution.py:175
  445.2 12.2 %collective-permute-done.33 = bf16[4,1,1,128,512]{4,3,2,1,0:T(8,128)(2,1)S(1)} collective-permute-done((bf16[4,1,1,128,512]{4,3,2,1,0:T(8,128)(2,1)S(1)}, bf16[4,1,1,128,512]{4,3,2,1,0:T(8,128)(2,1)S(1)}, u32[]{:S(2)}, u32[]{:S(2)}) %collective-permute-start.33) | collective-permute-done | bytes 524320 | tf_op jit(solution)/shard_map/ppermute | solution.py:297
  457.4 10.8 %collective-permute-done.32 = bf16[4,1,1,128,512]{4,3,2,1,0:T(8,128)(2,1)S(1)} collective-permute-done((bf16[4,1,1,128,512]{4,3,2,1,0:T(8,128)(2,1)S(1)}, bf16[4,1,1,128,512]{4,3,2,1,0:T(8,128)(2,1)S(1)}, u32[]{:S(2)}, u32[]{:S(2)}) %collective-permute-start.32) | collective-permute-done | bytes 524320 | tf_op jit(solution)/shard_map/ppermute | solution.py:297
  483.0 4.1 collective-permute-done.36
  488.2 6.6 %collective-permute-done.38 = bf16[1,1,1,2,2,48,2304]{6,5,4,3,2,1,0:T(8,128)(2,1)} collective-permute-done((bf16[1,1,1,2,2,48,2304]{6,5,4,3,2,1,0:T(8,128)(2,1)}, bf16[1,1,1,2,2,48,2304]{6,5,4,3,2,1,0:T(8,128)(2,1)}, u32[]{:S(2)}, u32[]{:S(2)}) %collective-permute-start.38) | collective-permute-done | bytes 884768 | tf_op jit(solution)/shard_map/ppermute | solution.py:297
  497.1 4.3 collective-permute-done.39
  504.2 6.4 %fusion.35 = (bf16[1536]{0:T(1024)(128)(2,1)S(1)}, f32[128]{0:T(128)S(1)}, f32[128,1536]{1,0:T(8,128)}) fusion(bf16[1,128,1536]{2,1,0:T(8,128)(2,1)S(1)} %copy-done.2, f32[128]{0:T(128)S(1)} %copy-done.45, f32[1536]{0:T(1024)S(1)} %mul.266, bf16[1536,2304]{1,0:T(8,128)(2,1)} %all-gather.3.cloned.1.call-done, f32[128,256]{1,0:T(8,128)S(1)} %get-tuple-element.174, ...), kind=kOutput, calls=%fused_computation.95 | convolution fusion | flops 808253824 | bytes 8529920 | tf_op jit(solution)/shard_map/tc,dc->td/dot_general | solution.py:686
  523.6 4.8 all-to-all-start.1
  533.9 13.3 %collective-permute-done.41 = bf16[4,1,1,1,48,1536]{5,4,3,2,1,0:T(8,128)(2,1)} collective-permute-done((bf16[4,1,1,1,48,1536]{5,4,3,2,1,0:T(8,128)(2,1)}, bf16[4,1,1,1,48,1536]{5,4,3,2,1,0:T(8,128)(2,1)}, u32[]{:S(2)}, u32[]{:S(2)}) %collective-permute-start.41) | collective-permute-done | bytes 589856 | tf_op jit(solution)/shard_map/ppermute | solution.py:297
  547.2 3.4 collective-permute-done.40
  552.6 13.4 %collective-permute-done.44 = bf16[1,2,1,1,280,768]{5,4,3,2,1,0:T(8,128)(2,1)} collective-permute-done((bf16[1,2,1,1,280,768]{5,4,3,2,1,0:T(8,128)(2,1)}, bf16[1,2,1,1,280,768]{5,4,3,2,1,0:T(8,128)(2,1)}, u32[]{:S(2)}, u32[]{:S(2)}) %collective-permute-start.44) | collective-permute-done | bytes 860192 | tf_op jit(solution)/shard_map/ppermute | solution.py:297
  574.3 5.9 collective-permute-done.51
  580.6 5.6 collective-permute-done.50
  588.9 7.2 %collective-permute-start.54 = (bf16[1,1,1,1,48,768]{5,4,3,2,1,0:T(8,128)(2,1)S(1)}, bf16[1,1,1,1,48,768]{5,4,3,2,1,0:T(8,128)(2,1)S(1)}, u32[]{:S(2)}, u32[]{:S(2)}) collective-permute-start(bf16[1,1,1,1,48,768]{5,4,3,2,1,0:T(8,128)(2,1)S(1)} %get-tuple-element.172), channel_id=1, source_target_pairs={{0,8},{2,10},{4,12},{6,14},{8,16},{10,18},{12,20},{14,22},{16,24},... | collective-permute-start | bytes 221192 | tf_op jit(solution)/shard_map/ppermute | solution.py:297
  596.1 3.5 collective-permute-done.47
  602.6 3.8 collective-permute-done.53
  616.4 3.3 reshape.626
  619.7 3.9 copy.54
  623.6 3.3 reshape.627
  (388 shorter events, 201.8 us)
Async XLA Ops:
  7.2 105.8 %all-gather.3.cloned.1.call-start = ((), (), s32[]{:S(2)}) async-start(), calls=%async_computation.4 | async-start | bytes 7299072 | tf_op jit(solution)/shard_map/all_gather | solution.py:512
  9.7 223.3 %all-gather.5.cloned.1.call-start = ((), (), s32[]{:S(2)}) async-start(), calls=%async_computation.5 | async-start | bytes 4866048 | tf_op jit(solution)/shard_map/all_gather | solution.py:549
  9.8 16.0 %collective-permute-start.2 = (bf16[1,1,1,128,1536]{4,3,2,1,0:T(8,128)(2,1)}, bf16[1,1,1,128,1536]{4,3,2,1,0:T(8,128)(2,1)S(1)}, u32[]{:S(2)}, u32[]{:S(2)}) collective-permute-start(bf16[1,1,1,128,1536]{4,3,2,1,0:T(8,128)(2,1)} %bitcast.181), channel_id=1, source_target_pairs={{0,24},{2,26},{4,28},{6,30},{8,0},{10,2},{12,4},{14,6},{16,8},{18,... | collective-permute-start | bytes 1179656 | tf_op jit(solution)/shard_map/ppermute | solution.py:297
  14.9 38.6 %collective-permute-start.1 = (bf16[1,1,1,128,1536]{4,3,2,1,0:T(8,128)(2,1)}, bf16[1,1,1,128,1536]{4,3,2,1,0:T(8,128)(2,1)S(1)}, u32[]{:S(2)}, u32[]{:S(2)}) collective-permute-start(bf16[1,1,1,128,1536]{4,3,2,1,0:T(8,128)(2,1)} %bitcast.182), channel_id=1, source_target_pairs={{0,16},{2,18},{4,20},{6,22},{8,24},{10,26},{12,28},{14,30},{16,0},... | collective-permute-start | bytes 1179656 | tf_op jit(solution)/shard_map/ppermute | solution.py:297
  14.9 38.6 %collective-permute-start = (bf16[1,1,1,128,1536]{4,3,2,1,0:T(8,128)(2,1)}, bf16[1,1,1,128,1536]{4,3,2,1,0:T(8,128)(2,1)S(1)}, u32[]{:S(2)}, u32[]{:S(2)}) collective-permute-start(bf16[1,1,1,128,1536]{4,3,2,1,0:T(8,128)(2,1)} %bitcast.183), channel_id=1, source_target_pairs={{0,8},{2,10},{4,12},{6,14},{8,16},{10,18},{12,20},{14,22},{16,24},... | collective-permute-start | bytes 1179656 | tf_op jit(solution)/shard_map/ppermute | solution.py:297
  17.1 37.7 %collective-permute-start.3 = (bf16[1,1,1,280,768]{4,3,2,1,0:T(8,128)(2,1)S(1)}, bf16[1,1,1,280,768]{4,3,2,1,0:T(8,128)(2,1)S(1)}, u32[]{:S(2)}, u32[]{:S(2)}) collective-permute-start(bf16[1,1,1,280,768]{4,3,2,1,0:T(8,128)(2,1)S(1)} %get-tuple-element.160), channel_id=1, source_target_pairs={{0,4},{2,6},{4,0},{6,2},{8,12},{10,14},{12,8},{14,10},{16,20},{18,... | collective-permute-start | bytes 1290248 | tf_op jit(solution)/shard_map/ppermute | solution.py:297
  18.7 36.2 %collective-permute-start.4 = (bf16[1,1,1,280,768]{4,3,2,1,0:T(8,128)(2,1)S(1)}, bf16[1,1,1,280,768]{4,3,2,1,0:T(8,128)(2,1)S(1)}, u32[]{:S(2)}, u32[]{:S(2)}) collective-permute-start(bf16[1,1,1,280,768]{4,3,2,1,0:T(8,128)(2,1)S(1)} %get-tuple-element.159), channel_id=1, source_target_pairs={{0,2},{2,0},{4,6},{6,4},{8,10},{10,8},{12,14},{14,12},{16,18},{18,... | collective-permute-start | bytes 1290248 | tf_op jit(solution)/shard_map/ppermute | solution.py:297
  54.9 23.2 %collective-permute-start.6 = (bf16[1,1,2,280,768]{4,3,2,1,0:T(8,128)(2,1)S(1)}, bf16[1,1,2,280,768]{4,3,2,1,0:T(8,128)(2,1)S(1)}, u32[]{:S(2)}, u32[]{:S(2)}) collective-permute-start(bf16[1,1,2,280,768]{4,3,2,1,0:T(8,128)(2,1)S(1)} %pad_maximum_fusion.12), channel_id=1, source_target_pairs={{0,4},{2,6},{4,0},{6,2},{8,12},{10,14},{12,8},{14,10},{16,20},{18,... | collective-permute-start | bytes 2580488 | tf_op jit(solution)/shard_map/ppermute | solution.py:297
  56.5 26.0 %collective-permute-start.5 = (bf16[1,2,1,280,768]{4,3,2,1,0:T(8,128)(2,1)S(1)}, bf16[1,2,1,280,768]{4,3,2,1,0:T(8,128)(2,1)S(1)}, u32[]{:S(2)}, u32[]{:S(2)}) collective-permute-start(bf16[1,2,1,280,768]{4,3,2,1,0:T(8,128)(2,1)S(1)} %pad_maximum_fusion.11), channel_id=1, source_target_pairs={{0,2},{2,0},{4,6},{6,4},{8,10},{10,8},{12,14},{14,12},{16,18},{18,... | collective-permute-start | bytes 2580488 | tf_op jit(solution)/shard_map/ppermute | solution.py:297
  119.6 18.8 %collective-permute-start.9 = (bf16[1,1,1,128,512]{4,3,2,1,0:T(8,128)(2,1)S(1)}, bf16[1,1,1,128,512]{4,3,2,1,0:T(8,128)(2,1)S(1)}, u32[]{:S(2)}, u32[]{:S(2)}) collective-permute-start(bf16[1,1,1,128,512]{4,3,2,1,0:T(8,128)(2,1)S(1)} %maximum_bitcast_fusion.1), channel_id=1, source_target_pairs={{0,16},{2,18},{4,20},{6,22},{8,24},{10,26},{12,28},{14,30},{16,0},... | collective-permute-start | bytes 393224 | tf_op jit(solution)/shard_map/ppermute | solution.py:297
  122.9 15.6 %collective-permute-start.8 = (bf16[1,1,1,128,512]{4,3,2,1,0:T(8,128)(2,1)S(1)}, bf16[1,1,1,128,512]{4,3,2,1,0:T(8,128)(2,1)S(1)}, u32[]{:S(2)}, u32[]{:S(2)}) collective-permute-start(bf16[1,1,1,128,512]{4,3,2,1,0:T(8,128)(2,1)S(1)} %maximum_bitcast_fusion.1), channel_id=1, source_target_pairs={{0,8},{2,10},{4,12},{6,14},{8,16},{10,18},{12,20},{14,22},{16,24},... | collective-permute-start | bytes 393224 | tf_op jit(solution)/shard_map/ppermute | solution.py:297
  139.3 63.8 %all-to-all-start = ((bf16[4,2,48,2304]{3,2,1,0:T(8,128)(2,1)}), bf16[4,2,48,2304]{3,2,1,0:T(8,128)(2,1)}, u32[]{:S(2)}, u32[]{:S(2)}) async-start(bf16[4,2,48,2304]{3,2,1,0:T(8,128)(2,1)} %pad_maximum_fusion.4), calls=%async_computation | async-start | bytes 3538944 | tf_op jit(solution)/shard_map/all_to_all | solution.py:573
  144.0 482.9 %reduce-scatter.3.cloned.1.call-start = ((), (), s32[]{:S(2)}) async-start(), calls=%async_computation.6 | async-start | bytes 1966080 | tf_op jit(solution)/shard_map/reduce_scatter | solution.py:628
  150.8 15.9 %collective-permute-start.13 = (bf16[4,1,1,128,512]{4,3,2,1,0:T(8,128)(2,1)}, bf16[4,1,1,128,512]{4,3,2,1,0:T(8,128)(2,1)S(1)}, u32[]{:S(2)}, u32[]{:S(2)}) collective-permute-start(bf16[4,1,1,128,512]{4,3,2,1,0:T(8,128)(2,1)} %pad_maximum_fusion.14), channel_id=1, source_target_pairs={{0,6},{2,4},{4,2},{6,0},{8,14},{10,12},{12,10},{14,8},{16,22},{18,... | collective-permute-start | bytes 1572872 | tf_op jit(solution)/shard_map/ppermute | solution.py:297
  151.8 28.9 %collective-permute-start.12 = (bf16[4,1,1,128,512]{4,3,2,1,0:T(8,128)(2,1)}, bf16[4,1,1,128,512]{4,3,2,1,0:T(8,128)(2,1)S(1)}, u32[]{:S(2)}, u32[]{:S(2)}) collective-permute-start(bf16[4,1,1,128,512]{4,3,2,1,0:T(8,128)(2,1)} %pad_maximum_fusion.14), channel_id=1, source_target_pairs={{0,4},{2,6},{4,0},{6,2},{8,12},{10,14},{12,8},{14,10},{16,20},{18,... | collective-permute-start | bytes 1572872 | tf_op jit(solution)/shard_map/ppermute | solution.py:297
  153.4 27.3 %collective-permute-start.11 = (bf16[4,1,1,128,512]{4,3,2,1,0:T(8,128)(2,1)}, bf16[4,1,1,128,512]{4,3,2,1,0:T(8,128)(2,1)S(1)}, u32[]{:S(2)}, u32[]{:S(2)}) collective-permute-start(bf16[4,1,1,128,512]{4,3,2,1,0:T(8,128)(2,1)} %pad_maximum_fusion.14), channel_id=1, source_target_pairs={{0,2},{2,0},{4,6},{6,4},{8,10},{10,8},{12,14},{14,12},{16,18},{18,... | collective-permute-start | bytes 1572872 | tf_op jit(solution)/shard_map/ppermute | solution.py:297
  205.8 21.5 %collective-permute-start.14 = (bf16[1,1,1,2,2,48,2304]{6,5,4,3,2,1,0:T(8,128)(2,1)}, bf16[1,1,1,2,2,48,2304]{6,5,4,3,2,1,0:T(8,128)(2,1)}, u32[]{:S(2)}, u32[]{:S(2)}) collective-permute-start(bf16[1,1,1,2,2,48,2304]{6,5,4,3,2,1,0:T(8,128)(2,1)} %get-tuple-element.152), channel_id=1, source_target_pairs={{0,4},{2,6},{4,0},{6,2},{8,12},{10,14},{12,8},{14,10},{16,20},{18,... | collective-permute-start | bytes 2654216 | tf_op jit(solution)/shard_map/ppermute | solution.py:297
  207.5 22.8 %collective-permute-start.15 = (bf16[1,1,1,2,2,48,2304]{6,5,4,3,2,1,0:T(8,128)(2,1)}, bf16[1,1,1,2,2,48,2304]{6,5,4,3,2,1,0:T(8,128)(2,1)}, u32[]{:S(2)}, u32[]{:S(2)}) collective-permute-start(bf16[1,1,1,2,2,48,2304]{6,5,4,3,2,1,0:T(8,128)(2,1)} %get-tuple-element.151), channel_id=1, source_target_pairs={{0,2},{2,0},{4,6},{6,4},{8,10},{10,8},{12,14},{14,12},{16,18},{18,... | collective-permute-start | bytes 2654216 | tf_op jit(solution)/shard_map/ppermute | solution.py:297
  238.4 39.4 %collective-permute-start.19 = (bf16[1,2,1,2,2,48,2304]{6,5,4,3,2,1,0:T(8,128)(2,1)S(1)}, bf16[1,2,1,2,2,48,2304]{6,5,4,3,2,1,0:T(8,128)(2,1)S(1)}, u32[]{:S(2)}, u32[]{:S(2)}) collective-permute-start(bf16[1,2,1,2,2,48,2304]{6,5,4,3,2,1,0:T(8,128)(2,1)S(1)} %copy-done.8), channel_id=1, source_target_pairs={{0,2},{2,0},{4,6},{6,4},{8,10},{10,8},{12,14},{14,12},{16,18},{18,... | collective-permute-start | bytes 5308424 | tf_op jit(solution)/shard_map/ppermute | solution.py:297
  240.1 39.8 %collective-permute-start.20 = (bf16[1,1,2,2,2,48,2304]{6,5,4,3,2,1,0:T(8,128)(2,1)S(1)}, bf16[1,1,2,2,2,48,2304]{6,5,4,3,2,1,0:T(8,128)(2,1)S(1)}, u32[]{:S(2)}, u32[]{:S(2)}) collective-permute-start(bf16[1,1,2,2,2,48,2304]{6,5,4,3,2,1,0:T(8,128)(2,1)S(1)} %copy-done.9), channel_id=1, source_target_pairs={{0,4},{2,6},{4,0},{6,2},{8,12},{10,14},{12,8},{14,10},{16,20},{18,... | collective-permute-start | bytes 5308424 | tf_op jit(solution)/shard_map/ppermute | solution.py:297
  243.2 31.5 %collective-permute-start.17 = (bf16[1,1,1,128,1536]{4,3,2,1,0:T(8,128)(2,1)S(1)}, bf16[1,1,1,128,1536]{4,3,2,1,0:T(8,128)(2,1)S(1)}, u32[]{:S(2)}, u32[]{:S(2)}) collective-permute-start(bf16[1,1,1,128,1536]{4,3,2,1,0:T(8,128)(2,1)S(1)} %bitcast.203), channel_id=1, source_target_pairs={{0,16},{2,18},{4,20},{6,22},{8,24},{10,26},{12,28},{14,30},{16,0},... | collective-permute-start | bytes 1179656 | tf_op jit(solution)/shard_map/ppermute | solution.py:297
  243.2 31.5 %collective-permute-start.16 = (bf16[1,1,1,128,1536]{4,3,2,1,0:T(8,128)(2,1)S(1)}, bf16[1,1,1,128,1536]{4,3,2,1,0:T(8,128)(2,1)S(1)}, u32[]{:S(2)}, u32[]{:S(2)}) collective-permute-start(bf16[1,1,1,128,1536]{4,3,2,1,0:T(8,128)(2,1)S(1)} %bitcast.204), channel_id=1, source_target_pairs={{0,8},{2,10},{4,12},{6,14},{8,16},{10,18},{12,20},{14,22},{16,24},... | collective-permute-start | bytes 1179656 | tf_op jit(solution)/shard_map/ppermute | solution.py:297
  349.1 16.5 %collective-permute-start.30 = (bf16[1,2,2,1,280,1536]{5,4,3,2,1,0:T(8,128)(2,1)}, bf16[1,2,2,1,280,1536]{5,4,3,2,1,0:T(8,128)(2,1)S(1)}, u32[]{:S(2)}, u32[]{:S(2)}) collective-permute-start(bf16[1,2,2,1,280,1536]{5,4,3,2,1,0:T(8,128)(2,1)} %constant_dynamic-slice_fusion.16), channel_id=1, source_target_pairs={{0,1},{1,0},{2,3},{3,2},{4,5},{5,4},{6,7},{7,6},{8,9},{9,8},{10,11... | collective-permute-start | bytes 10321928 | tf_op jit(solution)/shard_map/ppermute | solution.py:384
  358.2 41.0 %collective-permute-start.28 = (bf16[1,2,1,2,2,48,2304]{6,5,4,3,2,1,0:T(8,128)(2,1)S(1)}, bf16[1,2,1,2,2,48,2304]{6,5,4,3,2,1,0:T(8,128)(2,1)}, u32[]{:S(2)}, u32[]{:S(2)}) collective-permute-start(bf16[1,2,1,2,2,48,2304]{6,5,4,3,2,1,0:T(8,128)(2,1)S(1)} %slice.278), channel_id=1, source_target_pairs={{0,2},{2,0},{4,6},{6,4},{8,10},{10,8},{12,14},{14,12},{16,18},{18,... | collective-permute-start | bytes 5308424 | tf_op jit(solution)/shard_map/ppermute | solution.py:297
  360.2 29.9 %collective-permute-start.26 = (bf16[1,1,1,128,1536]{4,3,2,1,0:T(8,128)(2,1)S(1)}, bf16[1,1,1,128,1536]{4,3,2,1,0:T(8,128)(2,1)}, u32[]{:S(2)}, u32[]{:S(2)}) collective-permute-start(bf16[1,1,1,128,1536]{4,3,2,1,0:T(8,128)(2,1)S(1)} %get-tuple-element.155), channel_id=1, source_target_pairs={{0,16},{2,18},{4,20},{6,22},{8,24},{10,26},{12,28},{14,30},{16,0},... | collective-permute-start | bytes 1179656 | tf_op jit(solution)/shard_map/ppermute | solution.py:297
  362.0 28.1 %collective-permute-start.25 = (bf16[1,1,1,128,1536]{4,3,2,1,0:T(8,128)(2,1)S(1)}, bf16[1,1,1,128,1536]{4,3,2,1,0:T(8,128)(2,1)}, u32[]{:S(2)}, u32[]{:S(2)}) collective-permute-start(bf16[1,1,1,128,1536]{4,3,2,1,0:T(8,128)(2,1)S(1)} %get-tuple-element.153), channel_id=1, source_target_pairs={{0,24},{2,26},{4,28},{6,30},{8,0},{10,2},{12,4},{14,6},{16,8},{18,... | collective-permute-start | bytes 1179656 | tf_op jit(solution)/shard_map/ppermute | solution.py:297
  365.6 40.3 %collective-permute-start.29 = (bf16[1,1,2,2,2,48,2304]{6,5,4,3,2,1,0:T(8,128)(2,1)}, bf16[1,1,2,2,2,48,2304]{6,5,4,3,2,1,0:T(8,128)(2,1)}, u32[]{:S(2)}, u32[]{:S(2)}) collective-permute-start(bf16[1,1,2,2,2,48,2304]{6,5,4,3,2,1,0:T(8,128)(2,1)} %slice.280), channel_id=1, source_target_pairs={{0,4},{2,6},{4,0},{6,2},{8,12},{10,14},{12,8},{14,10},{16,20},{18,... | collective-permute-start | bytes 5308424 | tf_op jit(solution)/shard_map/ppermute | solution.py:297
  440.0 29.8 %collective-permute-start.34 = (bf16[4,2,2,1,48,1536]{5,4,3,2,1,0:T(8,128)(2,1)S(1)}, bf16[4,2,2,1,48,1536]{5,4,3,2,1,0:T(8,128)(2,1)}, u32[]{:S(2)}, u32[]{:S(2)}) collective-permute-start(bf16[4,2,2,1,48,1536]{5,4,3,2,1,0:T(8,128)(2,1)S(1)} %constant_dynamic-slice_fusion.15), channel_id=1, source_target_pairs={{0,1},{1,0},{2,3},{3,2},{4,5},{5,4},{6,7},{7,6},{8,9},{9,8},{10,11... | collective-permute-start | bytes 7077896 | tf_op jit(solution)/shard_map/ppermute | solution.py:384
  440.0 186.9 %reduce-scatter.5.cloned.1.call-start = ((), (), s32[]{:S(2)}) async-start(), calls=%async_computation.7 | async-start | bytes 4866048 | tf_op jit(solution)/shard_map/reduce_scatter | solution.py:643
  441.7 15.7 %collective-permute-start.33 = (bf16[4,1,1,128,512]{4,3,2,1,0:T(8,128)(2,1)S(1)}, bf16[4,1,1,128,512]{4,3,2,1,0:T(8,128)(2,1)S(1)}, u32[]{:S(2)}, u32[]{:S(2)}) collective-permute-start(bf16[4,1,1,128,512]{4,3,2,1,0:T(8,128)(2,1)S(1)} %get-tuple-element.149), channel_id=1, source_target_pairs={{0,6},{2,4},{4,2},{6,0},{8,14},{10,12},{12,10},{14,8},{16,22},{18,... | collective-permute-start | bytes 1572872 | tf_op jit(solution)/shard_map/ppermute | solution.py:297
  443.3 24.9 %collective-permute-start.32 = (bf16[4,1,1,128,512]{4,3,2,1,0:T(8,128)(2,1)S(1)}, bf16[4,1,1,128,512]{4,3,2,1,0:T(8,128)(2,1)S(1)}, u32[]{:S(2)}, u32[]{:S(2)}) collective-permute-start(bf16[4,1,1,128,512]{4,3,2,1,0:T(8,128)(2,1)S(1)} %get-tuple-element.150), channel_id=1, source_target_pairs={{0,4},{2,6},{4,0},{6,2},{8,12},{10,14},{12,8},{14,10},{16,20},{18,... | collective-permute-start | bytes 1572872 | tf_op jit(solution)/shard_map/ppermute | solution.py:297
  443.9 24.5 %collective-permute-start.31 = (bf16[4,1,1,128,512]{4,3,2,1,0:T(8,128)(2,1)S(1)}, bf16[4,1,1,128,512]{4,3,2,1,0:T(8,128)(2,1)S(1)}, u32[]{:S(2)}, u32[]{:S(2)}) collective-permute-start(bf16[4,1,1,128,512]{4,3,2,1,0:T(8,128)(2,1)S(1)} %get-tuple-element.148), channel_id=1, source_target_pairs={{0,2},{2,0},{4,6},{6,4},{8,10},{10,8},{12,14},{14,12},{16,18},{18,... | collective-permute-start | bytes 1572872 | tf_op jit(solution)/shard_map/ppermute | solution.py:297
  472.9 21.8 %collective-permute-start.38 = (bf16[1,1,1,2,2,48,2304]{6,5,4,3,2,1,0:T(8,128)(2,1)}, bf16[1,1,1,2,2,48,2304]{6,5,4,3,2,1,0:T(8,128)(2,1)}, u32[]{:S(2)}, u32[]{:S(2)}) collective-permute-start(bf16[1,1,1,2,2,48,2304]{6,5,4,3,2,1,0:T(8,128)(2,1)} %slice.303), channel_id=1, source_target_pairs={{0,4},{2,6},{4,0},{6,2},{8,12},{10,14},{12,8},{14,10},{16,20},{18,... | collective-permute-start | bytes 2654216 | tf_op jit(solution)/shard_map/ppermute | solution.py:297
  481.1 20.3 %collective-permute-start.39 = (bf16[1,1,1,2,2,48,2304]{6,5,4,3,2,1,0:T(8,128)(2,1)S(1)}, bf16[1,1,1,2,2,48,2304]{6,5,4,3,2,1,0:T(8,128)(2,1)S(1)}, u32[]{:S(2)}, u32[]{:S(2)}) collective-permute-start(bf16[1,1,1,2,2,48,2304]{6,5,4,3,2,1,0:T(8,128)(2,1)S(1)} %slice.305), channel_id=1, source_target_pairs={{0,2},{2,0},{4,6},{6,4},{8,10},{10,8},{12,14},{14,12},{16,18},{18,... | collective-permute-start | bytes 2654216 | tf_op jit(solution)/shard_map/ppermute | solution.py:297
  512.0 17.5 %collective-permute-start.42 = (bf16[4,1,1,1,48,1536]{5,4,3,2,1,0:T(8,128)(2,1)}, bf16[4,1,1,1,48,1536]{5,4,3,2,1,0:T(8,128)(2,1)}, u32[]{:S(2)}, u32[]{:S(2)}) collective-permute-start(bf16[4,1,1,1,48,1536]{5,4,3,2,1,0:T(8,128)(2,1)} %get-tuple-element.146), channel_id=1, source_target_pairs={{0,6},{2,4},{4,2},{6,0},{8,14},{10,12},{12,10},{14,8},{16,22},{18,... | collective-permute-start | bytes 1769480 | tf_op jit(solution)/shard_map/ppermute | solution.py:297
  513.5 33.7 %collective-permute-start.41 = (bf16[4,1,1,1,48,1536]{5,4,3,2,1,0:T(8,128)(2,1)}, bf16[4,1,1,1,48,1536]{5,4,3,2,1,0:T(8,128)(2,1)}, u32[]{:S(2)}, u32[]{:S(2)}) collective-permute-start(bf16[4,1,1,1,48,1536]{5,4,3,2,1,0:T(8,128)(2,1)} %get-tuple-element.147), channel_id=1, source_target_pairs={{0,4},{2,6},{4,0},{6,2},{8,12},{10,14},{12,8},{14,10},{16,20},{18,... | collective-permute-start | bytes 1769480 | tf_op jit(solution)/shard_map/ppermute | solution.py:297
  515.2 35.5 %collective-permute-start.40 = (bf16[4,1,1,1,48,1536]{5,4,3,2,1,0:T(8,128)(2,1)}, bf16[4,1,1,1,48,1536]{5,4,3,2,1,0:T(8,128)(2,1)}, u32[]{:S(2)}, u32[]{:S(2)}) collective-permute-start(bf16[4,1,1,1,48,1536]{5,4,3,2,1,0:T(8,128)(2,1)} %get-tuple-element.145), channel_id=1, source_target_pairs={{0,2},{2,0},{4,6},{6,4},{8,10},{10,8},{12,14},{14,12},{16,18},{18,... | collective-permute-start | bytes 1769480 | tf_op jit(solution)/shard_map/ppermute | solution.py:297
  517.8 49.8 %collective-permute-start.43 = (bf16[4,2,2,1,48,768]{5,4,3,2,1,0:T(8,128)(2,1)}, bf16[4,2,2,1,48,768]{5,4,3,2,1,0:T(8,128)(2,1)}, u32[]{:S(2)}, u32[]{:S(2)}) collective-permute-start(bf16[4,2,2,1,48,768]{5,4,3,2,1,0:T(8,128)(2,1)} %fusion.23), channel_id=1, source_target_pairs={{0,1},{1,0},{2,3},{3,2},{4,5},{5,4},{6,7},{7,6},{8,9},{9,8},{10,11... | collective-permute-start | bytes 3538952 | tf_op jit(solution)/shard_map/ppermute | solution.py:384
  519.5 46.5 %collective-permute-start.44 = (bf16[1,2,1,1,280,768]{5,4,3,2,1,0:T(8,128)(2,1)}, bf16[1,2,1,1,280,768]{5,4,3,2,1,0:T(8,128)(2,1)}, u32[]{:S(2)}, u32[]{:S(2)}) collective-permute-start(bf16[1,2,1,1,280,768]{5,4,3,2,1,0:T(8,128)(2,1)} %constant_dynamic-slice_fusion.11), channel_id=1, source_target_pairs={{0,2},{2,0},{4,6},{6,4},{8,10},{10,8},{12,14},{14,12},{16,18},{18,... | collective-permute-start | bytes 2580488 | tf_op jit(solution)/shard_map/ppermute | solution.py:297
  523.6 87.1 %all-to-all-start.1 = ((bf16[4,2,48,2304]{3,2,1,0:T(8,128)(2,1)}), bf16[4,2,48,2304]{3,2,1,0:T(8,128)(2,1)}, u32[]{:S(2)}, u32[]{:S(2)}) async-start(bf16[4,2,48,2304]{3,2,1,0:T(8,128)(2,1)} %pad_maximum_fusion.7), calls=%async_computation.3 | async-start | bytes 3538944 | tf_op jit(solution)/shard_map/all_to_all | solution.py:672
  529.5 37.9 %collective-permute-start.45 = (bf16[1,1,2,1,280,768]{5,4,3,2,1,0:T(8,128)(2,1)}, bf16[1,1,2,1,280,768]{5,4,3,2,1,0:T(8,128)(2,1)S(1)}, u32[]{:S(2)}, u32[]{:S(2)}) collective-permute-start(bf16[1,1,2,1,280,768]{5,4,3,2,1,0:T(8,128)(2,1)} %constant_dynamic-slice_fusion.10), channel_id=1, source_target_pairs={{0,4},{2,6},{4,0},{6,2},{8,12},{10,14},{12,8},{14,10},{16,20},{18,... | collective-permute-start | bytes 2580488 | tf_op jit(solution)/shard_map/ppermute | solution.py:297
  571.2 15.0 %collective-permute-start.50 = (bf16[4,1,1,1,48,768]{5,4,3,2,1,0:T(8,128)(2,1)S(1)}, bf16[4,1,1,1,48,768]{5,4,3,2,1,0:T(8,128)(2,1)S(1)}, u32[]{:S(2)}, u32[]{:S(2)}) collective-permute-start(bf16[4,1,1,1,48,768]{5,4,3,2,1,0:T(8,128)(2,1)S(1)} %get-tuple-element.158), channel_id=1, source_target_pairs={{0,4},{2,6},{4,0},{6,2},{8,12},{10,14},{12,8},{14,10},{16,20},{18,... | collective-permute-start | bytes 884744 | tf_op jit(solution)/shard_map/ppermute | solution.py:297
  571.2 16.7 %collective-permute-start.49 = (bf16[4,1,1,1,48,768]{5,4,3,2,1,0:T(8,128)(2,1)S(1)}, bf16[4,1,1,1,48,768]{5,4,3,2,1,0:T(8,128)(2,1)S(1)}, u32[]{:S(2)}, u32[]{:S(2)}) collective-permute-start(bf16[4,1,1,1,48,768]{5,4,3,2,1,0:T(8,128)(2,1)S(1)} %get-tuple-element.156), channel_id=1, source_target_pairs={{0,2},{2,0},{4,6},{6,4},{8,10},{10,8},{12,14},{14,12},{16,18},{18,... | collective-permute-start | bytes 884744 | tf_op jit(solution)/shard_map/ppermute | solution.py:297
  572.9 16.0 %collective-permute-start.48 = (bf16[1,1,1,1,48,1536]{5,4,3,2,1,0:T(8,128)(2,1)S(1)}, bf16[1,1,1,1,48,1536]{5,4,3,2,1,0:T(8,128)(2,1)S(1)}, u32[]{:S(2)}, u32[]{:S(2)}) collective-permute-start(bf16[1,1,1,1,48,1536]{5,4,3,2,1,0:T(8,128)(2,1)S(1)} %get-tuple-element.166), channel_id=1, source_target_pairs={{0,8},{2,10},{4,12},{6,14},{8,16},{10,18},{12,20},{14,22},{16,24},... | collective-permute-start | bytes 442376 | tf_op jit(solution)/shard_map/ppermute | solution.py:297
  573.2 26.4 %collective-permute-start.47 = (bf16[1,1,1,1,48,1536]{5,4,3,2,1,0:T(8,128)(2,1)S(1)}, bf16[1,1,1,1,48,1536]{5,4,3,2,1,0:T(8,128)(2,1)S(1)}, u32[]{:S(2)}, u32[]{:S(2)}) collective-permute-start(bf16[1,1,1,1,48,1536]{5,4,3,2,1,0:T(8,128)(2,1)S(1)} %get-tuple-element.167), channel_id=1, source_target_pairs={{0,16},{2,18},{4,20},{6,22},{8,24},{10,26},{12,28},{14,30},{16,0},... | collective-permute-start | bytes 442376 | tf_op jit(solution)/shard_map/ppermute | solution.py:297
  580.2 19.5 %collective-permute-start.46 = (bf16[1,1,1,1,48,1536]{5,4,3,2,1,0:T(8,128)(2,1)S(1)}, bf16[1,1,1,1,48,1536]{5,4,3,2,1,0:T(8,128)(2,1)S(1)}, u32[]{:S(2)}, u32[]{:S(2)}) collective-permute-start(bf16[1,1,1,1,48,1536]{5,4,3,2,1,0:T(8,128)(2,1)S(1)} %get-tuple-element.165), channel_id=1, source_target_pairs={{0,24},{2,26},{4,28},{6,30},{8,0},{10,2},{12,4},{14,6},{16,8},{18,... | collective-permute-start | bytes 442376 | tf_op jit(solution)/shard_map/ppermute | solution.py:297
  586.2 22.9 %collective-permute-start.56 = (bf16[1,1,1,1,280,768]{5,4,3,2,1,0:T(8,128)(2,1)S(1)}, bf16[1,1,1,1,280,768]{5,4,3,2,1,0:T(8,128)(2,1)S(1)}, u32[]{:S(2)}, u32[]{:S(2)}) collective-permute-start(bf16[1,1,1,1,280,768]{5,4,3,2,1,0:T(8,128)(2,1)S(1)} %constant_dynamic-slice_fusion.18), channel_id=1, source_target_pairs={{0,2},{2,0},{4,6},{6,4},{8,10},{10,8},{12,14},{14,12},{16,18},{18,... | collective-permute-start | bytes 1290248 | tf_op jit(solution)/shard_map/ppermute | solution.py:297
  588.0 21.3 %collective-permute-start.55 = (bf16[1,1,1,1,280,768]{5,4,3,2,1,0:T(8,128)(2,1)S(1)}, bf16[1,1,1,1,280,768]{5,4,3,2,1,0:T(8,128)(2,1)S(1)}, u32[]{:S(2)}, u32[]{:S(2)}) collective-permute-start(bf16[1,1,1,1,280,768]{5,4,3,2,1,0:T(8,128)(2,1)S(1)} %constant_dynamic-slice_fusion), channel_id=1, source_target_pairs={{0,4},{2,6},{4,0},{6,2},{8,12},{10,14},{12,8},{14,10},{16,20},{18,... | collective-permute-start | bytes 1290248 | tf_op jit(solution)/shard_map/ppermute | solution.py:297
  (76 other events, 672.2 us)
Sparse Core Ops, SparseCore 0:
  11.5 98.2 all-gather.2
  113.1 89.6 all-gather.4
  440.1 33.9 reduce-scatter.2
  479.9 138.4 reduce-scatter.4

commit v4 on v3

--- a/solution.py
+++ b/solution.py
@@ -640,14 +640,20 @@
     resid_low = resid_grad.astype(low)
     out_w_grad = jnp.einsum("tq,td->qd", attended, resid_low, preferred_element_type=jnp.float32)
     out_w_grad, resid_low = together(out_w_grad.astype(low), resid_low)
-    out_w_sum = lax.psum_scatter(
-        out_w_grad, ("ctx", "fsdp"), scatter_dimension=0, tiled=True
-    )
+    out_w_sum = own_core_sum(out_w_grad.reshape(ctx_size, 2, rows_w, width), core, 1)
     mixed_grad = jnp.einsum(
         "td,qd->tq", resid_low, full_out, preferred_element_type=jnp.float32
     ).astype(low)
     query_rot, kv_partial = attend_back(
         query_low, kv_all, hidden_by, mixed, log_total, mixed_grad
+    )
+    kv_partial, query_rot, out_w_sum = together(kv_partial, query_rot, out_w_sum)
+    out_w_sum = lax.psum_scatter(
+        out_w_sum.reshape(ctx_size * rows_w, width),
+        "ctx",
+        scatter_dimension=0,
+        tiled=True,
+        axis_index_groups=groups,
     )
     query_grad = rope_back(query_rot.reshape(tok_dev, H, HD), cosine, sine_table)
     query_grad = query_grad.reshape(tok_dev, width_q)
@@ -687,8 +693,7 @@
     input_part, attn_gain_grad = norm_back(hidden_in, full_attn_gain, normed_grad)
     input_grad = resid_grad + input_part
 
-    input_grad, out_sum, out_w_sum = together(input_grad, out_sum, out_w_sum)
-    out_share = out_w_sum.astype(jnp.float32)
+    input_grad, out_sum = together(input_grad, out_sum)
     layer_out = resid + out_sum.astype(jnp.float32)
 
     def to_rows(grad):
@@ -708,7 +713,13 @@
     ).astype(low)
     kv_w_grad = jnp.concatenate([kv_w_grad, small.reshape(width, -1)], axis=1)
     kv_w_parts = cut_columns(kv_w_grad, (0, kv_w_grad.shape[1]))
-    query_parts, kv_w_parts, down_grads = together(query_parts, kv_w_parts, down_grads)
+    if far_axes:
+        out_w_sum = out_w_sum.reshape(far_lead + (rows_w, width))
+        out_w_sum = grid.scatter_stage(out_w_sum, far_axes, True)
+    query_parts, kv_w_parts, down_grads, out_w_sum, gate_up_grad = together(
+        query_parts, kv_w_parts, down_grads, out_w_sum, gate_up_grad
+    )
+    out_share = out_w_sum.reshape(rows_w, width).astype(jnp.float32)
     down_grads = scatter_far(down_grads, 1, True)
     down_grad = jnp.concatenate(down_grads, axis=-1)
     down_share = down_grad.reshape(rows_d, width).astype(jnp.float32)

time: 648 us -> 621 us (0.958)
  waiting for transfers between devices: 290 us -> 276 us
  local copies, waits for them, and re-layouts: 70.6 us -> 63.1 us
    ppermute x49 -> x52, waiting for transfers between devices: 265 us -> 249 us  [hop(): return lax.ppermute(values, 'ctx', pairs)]
    ppermute x49 -> x52, starting transfers between devices: 71.9 us -> 68.4 us  [hop(): return lax.ppermute(values, 'ctx', pairs)]
    convert_element_type x12 -> x13, other arithmetic: 16.4 us -> 19.8 us  [scatter_stage(): return total.astype(values.dtype)]
  transfers between devices with their start and end apart: 63 -> 67, of which waited for: 36 -> 34; matrix products, arithmetic and copies ran while one was open for 22% -> 23% of each run, Pallas kernels for 1% -> 3%
where the time goes in v4:
time: 621 us; the launch traced here: 611 us
  waiting for transfers between devices  276 us (44%)
  other arithmetic  87.1 us (14%)
  starting transfers between devices  79.8 us (13%)
  Pallas kernels  67.1 us (11%)
  local copies, waits for them, and re-layouts  63.1 us (10%)
  matrix products  22.4 us (4%)
  between operations  15.6 us (3%)
    ppermute x52, waiting for transfers between devices, hop(): return lax.ppermute(values, 'ctx', pairs)  249 us
    ppermute x52, starting transfers between devices, hop(): return lax.ppermute(values, 'ctx', pairs)  68.4 us
    pallas_call x1, Pallas kernels, feed_forward(): pl.pallas_call(ff_kernel, grid=(columns // tile,), in_specs=[whole, whole...  49.5 us
    convert_element_type x13, other arithmetic, scatter_stage(): return total.astype(values.dtype)  19.8 us
    concatenate x10, other arithmetic, join(): jnp.concatenate([join(prefix + (j,)) for j in range(self.axes[axes[depth]...  16 us
    all_to_all x1, waiting for transfers between devices, shards(): lax.all_to_all(gate_up, 'ctx', split_axis=0, concat_axis=0, tiled=True, a...  15.9 us
  transfers between devices with their start and end apart: 67, of which 34 were waited for; matrix products, arithmetic and copies ran while one was open for 23% of the time, Pallas kernels for 3%

profile of v4, /device:TPU:0, one launch (start us, length us, event | category | flops | bytes accessed | tf_op | source)
XLA Modules:
  0.0 611.1 jit_solution(972257042062717343)
XLA Ops:
  9.8 5.1 collective-permute-start.2
  20.1 5.6 collective-permute-done.2
  25.8 27.6 %collective-permute-done.1 = bf16[1,1,1,128,1536]{4,3,2,1,0:T(8,128)(2,1)S(1)} collective-permute-done((bf16[1,1,1,128,1536]{4,3,2,1,0:T(8,128)(2,1)}, bf16[1,1,1,128,1536]{4,3,2,1,0:T(8,128)(2,1)S(1)}, u32[]{:S(2)}, u32[]{:S(2)}) %collective-permute-start.1) | collective-permute-done | bytes 393248 | tf_op jit(solution)/shard_map/ppermute | solution.py:297
  58.1 20.0 %collective-permute-done.6 = bf16[1,1,2,280,768]{4,3,2,1,0:T(8,128)(2,1)S(1)} collective-permute-done((bf16[1,1,2,280,768]{4,3,2,1,0:T(8,128)(2,1)S(1)}, bf16[1,1,2,280,768]{4,3,2,1,0:T(8,128)(2,1)S(1)}, u32[]{:S(2)}, u32[]{:S(2)}) %collective-permute-start.6) | collective-permute-done | bytes 860192 | tf_op jit(solution)/shard_map/ppermute | solution.py:297
  79.1 3.4 collective-permute-done.5
  85.9 3.4 reshape.611
  91.5 3.4 reshape.610
  100.0 4.0 broadcast_select_fusion.1
  106.8 3.3 pad.22.down
  112.2 3.9 fusion.8
  123.2 12.4 %collective-permute-done.9 = bf16[1,1,1,128,512]{4,3,2,1,0:T(8,128)(2,1)S(1)} collective-permute-done((bf16[1,1,1,128,512]{4,3,2,1,0:T(8,128)(2,1)S(1)}, bf16[1,1,1,128,512]{4,3,2,1,0:T(8,128)(2,1)S(1)}, u32[]{:S(2)}, u32[]{:S(2)}) %collective-permute-start.9) | collective-permute-done | bytes 131104 | tf_op jit(solution)/shard_map/ppermute | solution.py:297
  136.6 4.7 all-to-all-start
  152.9 10.9 %collective-permute-done.13 = bf16[4,1,1,128,512]{4,3,2,1,0:T(8,128)(2,1)S(1)} collective-permute-done((bf16[4,1,1,128,512]{4,3,2,1,0:T(8,128)(2,1)}, bf16[4,1,1,128,512]{4,3,2,1,0:T(8,128)(2,1)S(1)}, u32[]{:S(2)}, u32[]{:S(2)}) %collective-permute-start.13) | collective-permute-done | bytes 524320 | tf_op jit(solution)/shard_map/ppermute | solution.py:297
  163.8 12.4 %collective-permute-done.12 = bf16[4,1,1,128,512]{4,3,2,1,0:T(8,128)(2,1)S(1)} collective-permute-done((bf16[4,1,1,128,512]{4,3,2,1,0:T(8,128)(2,1)}, bf16[4,1,1,128,512]{4,3,2,1,0:T(8,128)(2,1)S(1)}, u32[]{:S(2)}, u32[]{:S(2)}) %collective-permute-start.12) | collective-permute-done | bytes 524320 | tf_op jit(solution)/shard_map/ppermute | solution.py:297
  178.7 6.5 %shard_map.221 = (f32[128,1536]{1,0:T(8,128)S(1)}, bf16[128,1536]{1,0:T(8,128)(2,1)S(1)}, f32[2,768]{1,0:T(2,128)S(1)}) custom-call(bf16[128,1536]{1,0:T(8,128)(2,1)S(1)} %add_convert_fusion.13.queries, bf16[2048,512]{1,0:T(8,128)(2,1)} %bitcast.203, f32[2048,128]{1,0:T(8,128)S(1)} %fusion.27.hidden_by), custom_call_target="tpu_custom_call" | custom-call | flops 1610612736 | bytes 2097152 | tf_op jit(solution)/shard_map/pallas_call | solution.py:124
  185.3 15.9 %all-to-all-done = bf16[4,2,48,2304]{3,2,1,0:T(8,128)(2,1)} async-done(((bf16[4,2,48,2304]{3,2,1,0:T(8,128)(2,1)}), bf16[4,2,48,2304]{3,2,1,0:T(8,128)(2,1)}, u32[]{:S(2)}, u32[]{:S(2)}) %all-to-all-start) | async-done | bytes 1769504 | tf_op jit(solution)/shard_map/all_to_all | solution.py:573
  208.3 17.5 %collective-permute-done.14 = bf16[1,1,1,2,2,48,2304]{6,5,4,3,2,1,0:T(8,128)(2,1)} collective-permute-done((bf16[1,1,1,2,2,48,2304]{6,5,4,3,2,1,0:T(8,128)(2,1)}, bf16[1,1,1,2,2,48,2304]{6,5,4,3,2,1,0:T(8,128)(2,1)}, u32[]{:S(2)}, u32[]{:S(2)}) %collective-permute-start.14) | collective-permute-done | bytes 884768 | tf_op jit(solution)/shard_map/ppermute | solution.py:297
  231.4 3.2 multiply_reduce_fusion.2
  241.8 9.0 %collective-permute-done.18 = bf16[1,1,1,128,1536]{4,3,2,1,0:T(8,128)(2,1)S(1)} collective-permute-done((bf16[1,1,1,128,1536]{4,3,2,1,0:T(8,128)(2,1)S(1)}, bf16[1,1,1,128,1536]{4,3,2,1,0:T(8,128)(2,1)S(1)}, u32[]{:S(2)}, u32[]{:S(2)}) %collective-permute-start.18) | collective-permute-done | bytes 393248 | tf_op jit(solution)/shard_map/ppermute | solution.py:297
  250.8 21.4 %collective-permute-done.17 = bf16[1,1,1,128,1536]{4,3,2,1,0:T(8,128)(2,1)S(1)} collective-permute-done((bf16[1,1,1,128,1536]{4,3,2,1,0:T(8,128)(2,1)S(1)}, bf16[1,1,1,128,1536]{4,3,2,1,0:T(8,128)(2,1)S(1)}, u32[]{:S(2)}, u32[]{:S(2)}) %collective-permute-start.17) | collective-permute-done | bytes 393248 | tf_op jit(solution)/shard_map/ppermute | solution.py:297
  273.5 2.9 collective-permute-done.19
  281.0 6.1 collective-permute-done.21.w2
  287.1 5.1 collective-permute-done.22.w3
  292.1 49.5 %shard_map.222 = (bf16[512,1536]{1,0:T(8,128)(2,1)S(1)}, bf16[512,1536]{1,0:T(8,128)(2,1)S(1)}, bf16[8,2,48,2304]{3,2,1,0:T(8,128)(2,1)}, bf16[8,2,48,2304]{3,2,...) custom-call(bf16[512,1536]{1,0:T(8,128)(2,1)} %bitcast.206, ...), custom_call_target="tpu_custom_call" | custom-call | flops 32614907904 | bytes 51904512 | tf_op jit(solution)/shard_map/pallas_call | solution.py:258
  342.2 3.4 slice.289
  350.5 3.1 add_convert_fusion.1
  353.6 3.0 add_convert_fusion
  367.0 5.4 collective-permute-done.27
  372.4 15.9 %collective-permute-done.26 = bf16[1,1,1,128,1536]{4,3,2,1,0:T(8,128)(2,1)} collective-permute-done((bf16[1,1,1,128,1536]{4,3,2,1,0:T(8,128)(2,1)S(1)}, bf16[1,1,1,128,1536]{4,3,2,1,0:T(8,128)(2,1)}, u32[]{:S(2)}, u32[]{:S(2)}) %collective-permute-start.26) | collective-permute-done | bytes 393248 | tf_op jit(solution)/shard_map/ppermute | solution.py:297
  389.8 7.9 %collective-permute-done.28 = bf16[1,2,1,2,2,48,2304]{6,5,4,3,2,1,0:T(8,128)(2,1)} collective-permute-done((bf16[1,2,1,2,2,48,2304]{6,5,4,3,2,1,0:T(8,128)(2,1)S(1)}, bf16[1,2,1,2,2,48,2304]{6,5,4,3,2,1,0:T(8,128)(2,1)}, u32[]{:S(2)}, u32[]{:S(2)}) %collective-permute-start.28) | collective-permute-done | bytes 1769504 | tf_op jit(solution)/shard_map/ppermute | solution.py:297
  397.7 3.2 add_convert_fusion.3
  400.9 3.2 collective-permute-done.29
  404.1 3.1 add_convert_fusion.2
  415.1 11.0 %shard_map.223 = (f32[128,1536]{1,0:T(8,128)S(1)}, bf16[2048,512]{1,0:T(8,128)(2,1)}) custom-call(bf16[128,1536]{1,0:T(8,128)(2,1)S(1)} %add_convert_fusion.13.queries, bf16[2048,512]{1,0:T(8,128)(2,1)} %bitcast.204, f32[2048,128]{1,0:T(8,128)S(1)} %fusion.27.hidden_by, f32[128,1536]{1,0:T(8,128)S(1)} %get-tuple-element.105.mixed, ...), custom_call_target="tpu_custom_call" | custom-call | flops 4026531840 | bytes 4194304 | tf_op jit(solution)/shard_map/pallas_call | solution.py:175
  426.1 3.3 dynamic-slice_add_fusion.2
  442.6 12.2 %collective-permute-done.34 = bf16[4,1,1,128,512]{4,3,2,1,0:T(8,128)(2,1)S(1)} collective-permute-done((bf16[4,1,1,128,512]{4,3,2,1,0:T(8,128)(2,1)S(1)}, bf16[4,1,1,128,512]{4,3,2,1,0:T(8,128)(2,1)S(1)}, u32[]{:S(2)}, u32[]{:S(2)}) %collective-permute-start.34) | collective-permute-done | bytes 524320 | tf_op jit(solution)/shard_map/ppermute | solution.py:297
  454.9 9.7 %collective-permute-done.33 = bf16[4,1,1,128,512]{4,3,2,1,0:T(8,128)(2,1)S(1)} collective-permute-done((bf16[4,1,1,128,512]{4,3,2,1,0:T(8,128)(2,1)S(1)}, bf16[4,1,1,128,512]{4,3,2,1,0:T(8,128)(2,1)S(1)}, u32[]{:S(2)}, u32[]{:S(2)}) %collective-permute-start.33) | collective-permute-done | bytes 524320 | tf_op jit(solution)/shard_map/ppermute | solution.py:297
  465.9 3.5 dynamic-slice_add_fusion.1
  472.8 2.8 collective-permute-start.36
  479.2 7.3 %collective-permute-done.37 = bf16[1,1,1,128,512]{4,3,2,1,0:T(8,128)(2,1)S(1)} collective-permute-done((bf16[1,1,1,128,512]{4,3,2,1,0:T(8,128)(2,1)S(1)}, bf16[1,1,1,128,512]{4,3,2,1,0:T(8,128)(2,1)S(1)}, u32[]{:S(2)}, u32[]{:S(2)}) %collective-permute-start.37) | collective-permute-done | bytes 131104 | tf_op jit(solution)/shard_map/ppermute | solution.py:297
  486.6 4.2 collective-permute-done.39
  492.3 5.4 collective-permute-done.40
  500.2 5.2 fusion.35
  515.9 4.8 all-to-all-start.1
  527.0 9.9 %collective-permute-done.42 = bf16[4,1,1,1,48,1536]{5,4,3,2,1,0:T(8,128)(2,1)} collective-permute-done((bf16[4,1,1,1,48,1536]{5,4,3,2,1,0:T(8,128)(2,1)}, bf16[4,1,1,1,48,1536]{5,4,3,2,1,0:T(8,128)(2,1)}, u32[]{:S(2)}, u32[]{:S(2)}) %collective-permute-start.42) | collective-permute-done | bytes 589856 | tf_op jit(solution)/shard_map/ppermute | solution.py:297
  541.3 12.3 %collective-permute-done.45 = bf16[1,2,1,1,280,768]{5,4,3,2,1,0:T(8,128)(2,1)S(1)} collective-permute-done((bf16[1,2,1,1,280,768]{5,4,3,2,1,0:T(8,128)(2,1)S(1)}, bf16[1,2,1,1,280,768]{5,4,3,2,1,0:T(8,128)(2,1)S(1)}, u32[]{:S(2)}, u32[]{:S(2)}) %collective-permute-start.45) | collective-permute-done | bytes 860192 | tf_op jit(solution)/shard_map/ppermute | solution.py:297
  586.3 2.9 collective-permute-start.50
  594.5 3.0 collective-permute-start.56
  (404 shorter events, 192.2 us)
Async XLA Ops:
  7.2 102.9 %all-gather.3.cloned.1.call-start = ((), (), s32[]{:S(2)}) async-start(), calls=%async_computation.4 | async-start | bytes 7299072 | tf_op jit(solution)/shard_map/all_gather | solution.py:512
  9.7 221.7 %all-gather.5.cloned.1.call-start = ((), (), s32[]{:S(2)}) async-start(), calls=%async_computation.5 | async-start | bytes 4866048 | tf_op jit(solution)/shard_map/all_gather | solution.py:549
  9.8 16.0 %collective-permute-start.2 = (bf16[1,1,1,128,1536]{4,3,2,1,0:T(8,128)(2,1)}, bf16[1,1,1,128,1536]{4,3,2,1,0:T(8,128)(2,1)S(1)}, u32[]{:S(2)}, u32[]{:S(2)}) collective-permute-start(bf16[1,1,1,128,1536]{4,3,2,1,0:T(8,128)(2,1)} %bitcast.192), channel_id=1, source_target_pairs={{0,24},{2,26},{4,28},{6,30},{8,0},{10,2},{12,4},{14,6},{16,8},{18,... | collective-permute-start | bytes 1179656 | tf_op jit(solution)/shard_map/ppermute | solution.py:297
  14.9 38.6 %collective-permute-start.1 = (bf16[1,1,1,128,1536]{4,3,2,1,0:T(8,128)(2,1)}, bf16[1,1,1,128,1536]{4,3,2,1,0:T(8,128)(2,1)S(1)}, u32[]{:S(2)}, u32[]{:S(2)}) collective-permute-start(bf16[1,1,1,128,1536]{4,3,2,1,0:T(8,128)(2,1)} %bitcast.193), channel_id=1, source_target_pairs={{0,16},{2,18},{4,20},{6,22},{8,24},{10,26},{12,28},{14,30},{16,0},... | collective-permute-start | bytes 1179656 | tf_op jit(solution)/shard_map/ppermute | solution.py:297
  14.9 38.6 %collective-permute-start = (bf16[1,1,1,128,1536]{4,3,2,1,0:T(8,128)(2,1)}, bf16[1,1,1,128,1536]{4,3,2,1,0:T(8,128)(2,1)S(1)}, u32[]{:S(2)}, u32[]{:S(2)}) collective-permute-start(bf16[1,1,1,128,1536]{4,3,2,1,0:T(8,128)(2,1)} %bitcast.194), channel_id=1, source_target_pairs={{0,8},{2,10},{4,12},{6,14},{8,16},{10,18},{12,20},{14,22},{16,24},... | collective-permute-start | bytes 1179656 | tf_op jit(solution)/shard_map/ppermute | solution.py:297
  17.1 37.7 %collective-permute-start.3 = (bf16[1,1,1,280,768]{4,3,2,1,0:T(8,128)(2,1)S(1)}, bf16[1,1,1,280,768]{4,3,2,1,0:T(8,128)(2,1)S(1)}, u32[]{:S(2)}, u32[]{:S(2)}) collective-permute-start(bf16[1,1,1,280,768]{4,3,2,1,0:T(8,128)(2,1)S(1)} %get-tuple-element.168), channel_id=1, source_target_pairs={{0,4},{2,6},{4,0},{6,2},{8,12},{10,14},{12,8},{14,10},{16,20},{18,... | collective-permute-start | bytes 1290248 | tf_op jit(solution)/shard_map/ppermute | solution.py:297
  18.6 36.2 %collective-permute-start.4 = (bf16[1,1,1,280,768]{4,3,2,1,0:T(8,128)(2,1)S(1)}, bf16[1,1,1,280,768]{4,3,2,1,0:T(8,128)(2,1)S(1)}, u32[]{:S(2)}, u32[]{:S(2)}) collective-permute-start(bf16[1,1,1,280,768]{4,3,2,1,0:T(8,128)(2,1)S(1)} %get-tuple-element.167), channel_id=1, source_target_pairs={{0,2},{2,0},{4,6},{6,4},{8,10},{10,8},{12,14},{14,12},{16,18},{18,... | collective-permute-start | bytes 1290248 | tf_op jit(solution)/shard_map/ppermute | solution.py:297
  54.9 23.2 %collective-permute-start.6 = (bf16[1,1,2,280,768]{4,3,2,1,0:T(8,128)(2,1)S(1)}, bf16[1,1,2,280,768]{4,3,2,1,0:T(8,128)(2,1)S(1)}, u32[]{:S(2)}, u32[]{:S(2)}) collective-permute-start(bf16[1,1,2,280,768]{4,3,2,1,0:T(8,128)(2,1)S(1)} %pad_maximum_fusion.12), channel_id=1, source_target_pairs={{0,4},{2,6},{4,0},{6,2},{8,12},{10,14},{12,8},{14,10},{16,20},{18,... | collective-permute-start | bytes 2580488 | tf_op jit(solution)/shard_map/ppermute | solution.py:297
  56.5 26.0 %collective-permute-start.5 = (bf16[1,2,1,280,768]{4,3,2,1,0:T(8,128)(2,1)S(1)}, bf16[1,2,1,280,768]{4,3,2,1,0:T(8,128)(2,1)S(1)}, u32[]{:S(2)}, u32[]{:S(2)}) collective-permute-start(bf16[1,2,1,280,768]{4,3,2,1,0:T(8,128)(2,1)S(1)} %pad_maximum_fusion.11), channel_id=1, source_target_pairs={{0,2},{2,0},{4,6},{6,4},{8,10},{10,8},{12,14},{14,12},{16,18},{18,... | collective-permute-start | bytes 2580488 | tf_op jit(solution)/shard_map/ppermute | solution.py:297
  85.9 14.1 %collective-permute-start.7 = (bf16[1,2,2,1,280,1536]{5,4,3,2,1,0:T(8,128)(2,1)}, bf16[1,2,2,1,280,1536]{5,4,3,2,1,0:T(8,128)(2,1)}, u32[]{:S(2)}, u32[]{:S(2)}) collective-permute-start(bf16[1,2,2,1,280,1536]{5,4,3,2,1,0:T(8,128)(2,1)} %pad_maximum_fusion.3), channel_id=1, source_target_pairs={{0,1},{1,0},{2,3},{3,2},{4,5},{5,4},{6,7},{7,6},{8,9},{9,8},{10,11... | collective-permute-start | bytes 10321928 | tf_op jit(solution)/shard_map/ppermute | solution.py:384
  118.3 17.3 %collective-permute-start.9 = (bf16[1,1,1,128,512]{4,3,2,1,0:T(8,128)(2,1)S(1)}, bf16[1,1,1,128,512]{4,3,2,1,0:T(8,128)(2,1)S(1)}, u32[]{:S(2)}, u32[]{:S(2)}) collective-permute-start(bf16[1,1,1,128,512]{4,3,2,1,0:T(8,128)(2,1)S(1)} %maximum_bitcast_fusion.1), channel_id=1, source_target_pairs={{0,16},{2,18},{4,20},{6,22},{8,24},{10,26},{12,28},{14,30},{16,0},... | collective-permute-start | bytes 393224 | tf_op jit(solution)/shard_map/ppermute | solution.py:297
  119.9 15.8 %collective-permute-start.8 = (bf16[1,1,1,128,512]{4,3,2,1,0:T(8,128)(2,1)S(1)}, bf16[1,1,1,128,512]{4,3,2,1,0:T(8,128)(2,1)S(1)}, u32[]{:S(2)}, u32[]{:S(2)}) collective-permute-start(bf16[1,1,1,128,512]{4,3,2,1,0:T(8,128)(2,1)S(1)} %maximum_bitcast_fusion.1), channel_id=1, source_target_pairs={{0,8},{2,10},{4,12},{6,14},{8,16},{10,18},{12,20},{14,22},{16,24},... | collective-permute-start | bytes 393224 | tf_op jit(solution)/shard_map/ppermute | solution.py:297
  136.6 64.7 %all-to-all-start = ((bf16[4,2,48,2304]{3,2,1,0:T(8,128)(2,1)}), bf16[4,2,48,2304]{3,2,1,0:T(8,128)(2,1)}, u32[]{:S(2)}, u32[]{:S(2)}) async-start(bf16[4,2,48,2304]{3,2,1,0:T(8,128)(2,1)} %pad_maximum_fusion.4), calls=%async_computation | async-start | bytes 3538944 | tf_op jit(solution)/shard_map/all_to_all | solution.py:573
  141.3 365.5 %reduce-scatter.3.cloned.1.call-start = ((), (), s32[]{:S(2)}) async-start(), calls=%async_computation.6 | async-start | bytes 1966080 | tf_op jit(solution)/shard_map/reduce_scatter | solution.py:628
  147.9 16.0 %collective-permute-start.13 = (bf16[4,1,1,128,512]{4,3,2,1,0:T(8,128)(2,1)}, bf16[4,1,1,128,512]{4,3,2,1,0:T(8,128)(2,1)S(1)}, u32[]{:S(2)}, u32[]{:S(2)}) collective-permute-start(bf16[4,1,1,128,512]{4,3,2,1,0:T(8,128)(2,1)} %pad_maximum_fusion.14), channel_id=1, source_target_pairs={{0,6},{2,4},{4,2},{6,0},{8,14},{10,12},{12,10},{14,8},{16,22},{18,... | collective-permute-start | bytes 1572872 | tf_op jit(solution)/shard_map/ppermute | solution.py:297
  149.3 26.9 %collective-permute-start.12 = (bf16[4,1,1,128,512]{4,3,2,1,0:T(8,128)(2,1)}, bf16[4,1,1,128,512]{4,3,2,1,0:T(8,128)(2,1)S(1)}, u32[]{:S(2)}, u32[]{:S(2)}) collective-permute-start(bf16[4,1,1,128,512]{4,3,2,1,0:T(8,128)(2,1)} %pad_maximum_fusion.14), channel_id=1, source_target_pairs={{0,4},{2,6},{4,0},{6,2},{8,12},{10,14},{12,8},{14,10},{16,20},{18,... | collective-permute-start | bytes 1572872 | tf_op jit(solution)/shard_map/ppermute | solution.py:297
  150.8 25.4 %collective-permute-start.11 = (bf16[4,1,1,128,512]{4,3,2,1,0:T(8,128)(2,1)}, bf16[4,1,1,128,512]{4,3,2,1,0:T(8,128)(2,1)S(1)}, u32[]{:S(2)}, u32[]{:S(2)}) collective-permute-start(bf16[4,1,1,128,512]{4,3,2,1,0:T(8,128)(2,1)} %pad_maximum_fusion.14), channel_id=1, source_target_pairs={{0,2},{2,0},{4,6},{6,4},{8,10},{10,8},{12,14},{14,12},{16,18},{18,... | collective-permute-start | bytes 1572872 | tf_op jit(solution)/shard_map/ppermute | solution.py:297
  204.0 21.8 %collective-permute-start.14 = (bf16[1,1,1,2,2,48,2304]{6,5,4,3,2,1,0:T(8,128)(2,1)}, bf16[1,1,1,2,2,48,2304]{6,5,4,3,2,1,0:T(8,128)(2,1)}, u32[]{:S(2)}, u32[]{:S(2)}) collective-permute-start(bf16[1,1,1,2,2,48,2304]{6,5,4,3,2,1,0:T(8,128)(2,1)} %get-tuple-element.160), channel_id=1, source_target_pairs={{0,4},{2,6},{4,0},{6,2},{8,12},{10,14},{12,8},{14,10},{16,20},{18,... | collective-permute-start | bytes 2654216 | tf_op jit(solution)/shard_map/ppermute | solution.py:297
  204.5 24.1 %collective-permute-start.15 = (bf16[1,1,1,2,2,48,2304]{6,5,4,3,2,1,0:T(8,128)(2,1)}, bf16[1,1,1,2,2,48,2304]{6,5,4,3,2,1,0:T(8,128)(2,1)}, u32[]{:S(2)}, u32[]{:S(2)}) collective-permute-start(bf16[1,1,1,2,2,48,2304]{6,5,4,3,2,1,0:T(8,128)(2,1)} %get-tuple-element.159), channel_id=1, source_target_pairs={{0,2},{2,0},{4,6},{6,4},{8,10},{10,8},{12,14},{14,12},{16,18},{18,... | collective-permute-start | bytes 2654216 | tf_op jit(solution)/shard_map/ppermute | solution.py:297
  236.8 39.6 %collective-permute-start.19 = (bf16[1,2,1,2,2,48,2304]{6,5,4,3,2,1,0:T(8,128)(2,1)S(1)}, bf16[1,2,1,2,2,48,2304]{6,5,4,3,2,1,0:T(8,128)(2,1)S(1)}, u32[]{:S(2)}, u32[]{:S(2)}) collective-permute-start(bf16[1,2,1,2,2,48,2304]{6,5,4,3,2,1,0:T(8,128)(2,1)S(1)} %copy-done.6), channel_id=1, source_target_pairs={{0,2},{2,0},{4,6},{6,4},{8,10},{10,8},{12,14},{14,12},{16,18},{18,... | collective-permute-start | bytes 5308424 | tf_op jit(solution)/shard_map/ppermute | solution.py:297
  238.3 40.1 %collective-permute-start.20 = (bf16[1,1,2,2,2,48,2304]{6,5,4,3,2,1,0:T(8,128)(2,1)S(1)}, bf16[1,1,2,2,2,48,2304]{6,5,4,3,2,1,0:T(8,128)(2,1)S(1)}, u32[]{:S(2)}, u32[]{:S(2)}) collective-permute-start(bf16[1,1,2,2,2,48,2304]{6,5,4,3,2,1,0:T(8,128)(2,1)S(1)} %copy-done.7), channel_id=1, source_target_pairs={{0,4},{2,6},{4,0},{6,2},{8,12},{10,14},{12,8},{14,10},{16,20},{18,... | collective-permute-start | bytes 5308424 | tf_op jit(solution)/shard_map/ppermute | solution.py:297
  240.9 31.3 %collective-permute-start.17 = (bf16[1,1,1,128,1536]{4,3,2,1,0:T(8,128)(2,1)S(1)}, bf16[1,1,1,128,1536]{4,3,2,1,0:T(8,128)(2,1)S(1)}, u32[]{:S(2)}, u32[]{:S(2)}) collective-permute-start(bf16[1,1,1,128,1536]{4,3,2,1,0:T(8,128)(2,1)S(1)} %bitcast.216), channel_id=1, source_target_pairs={{0,16},{2,18},{4,20},{6,22},{8,24},{10,26},{12,28},{14,30},{16,0},... | collective-permute-start | bytes 1179656 | tf_op jit(solution)/shard_map/ppermute | solution.py:297
  240.9 31.3 %collective-permute-start.16 = (bf16[1,1,1,128,1536]{4,3,2,1,0:T(8,128)(2,1)S(1)}, bf16[1,1,1,128,1536]{4,3,2,1,0:T(8,128)(2,1)S(1)}, u32[]{:S(2)}, u32[]{:S(2)}) collective-permute-start(bf16[1,1,1,128,1536]{4,3,2,1,0:T(8,128)(2,1)S(1)} %bitcast.217), channel_id=1, source_target_pairs={{0,8},{2,10},{4,12},{6,14},{8,16},{10,18},{12,20},{14,22},{16,24},... | collective-permute-start | bytes 1179656 | tf_op jit(solution)/shard_map/ppermute | solution.py:297
  347.6 16.2 %collective-permute-start.30 = (bf16[1,2,2,1,280,1536]{5,4,3,2,1,0:T(8,128)(2,1)}, bf16[1,2,2,1,280,1536]{5,4,3,2,1,0:T(8,128)(2,1)S(1)}, u32[]{:S(2)}, u32[]{:S(2)}) collective-permute-start(bf16[1,2,2,1,280,1536]{5,4,3,2,1,0:T(8,128)(2,1)} %constant_dynamic-slice_fusion.20), channel_id=1, source_target_pairs={{0,1},{1,0},{2,3},{3,2},{4,5},{5,4},{6,7},{7,6},{8,9},{9,8},{10,11... | collective-permute-start | bytes 10321928 | tf_op jit(solution)/shard_map/ppermute | solution.py:384
  356.7 41.0 %collective-permute-start.28 = (bf16[1,2,1,2,2,48,2304]{6,5,4,3,2,1,0:T(8,128)(2,1)S(1)}, bf16[1,2,1,2,2,48,2304]{6,5,4,3,2,1,0:T(8,128)(2,1)}, u32[]{:S(2)}, u32[]{:S(2)}) collective-permute-start(bf16[1,2,1,2,2,48,2304]{6,5,4,3,2,1,0:T(8,128)(2,1)S(1)} %slice.278), channel_id=1, source_target_pairs={{0,2},{2,0},{4,6},{6,4},{8,10},{10,8},{12,14},{14,12},{16,18},{18,... | collective-permute-start | bytes 5308424 | tf_op jit(solution)/shard_map/ppermute | solution.py:297
  358.4 29.9 %collective-permute-start.26 = (bf16[1,1,1,128,1536]{4,3,2,1,0:T(8,128)(2,1)S(1)}, bf16[1,1,1,128,1536]{4,3,2,1,0:T(8,128)(2,1)}, u32[]{:S(2)}, u32[]{:S(2)}) collective-permute-start(bf16[1,1,1,128,1536]{4,3,2,1,0:T(8,128)(2,1)S(1)} %get-tuple-element.163), channel_id=1, source_target_pairs={{0,16},{2,18},{4,20},{6,22},{8,24},{10,26},{12,28},{14,30},{16,0},... | collective-permute-start | bytes 1179656 | tf_op jit(solution)/shard_map/ppermute | solution.py:297
  360.2 28.1 %collective-permute-start.25 = (bf16[1,1,1,128,1536]{4,3,2,1,0:T(8,128)(2,1)S(1)}, bf16[1,1,1,128,1536]{4,3,2,1,0:T(8,128)(2,1)}, u32[]{:S(2)}, u32[]{:S(2)}) collective-permute-start(bf16[1,1,1,128,1536]{4,3,2,1,0:T(8,128)(2,1)S(1)} %get-tuple-element.161), channel_id=1, source_target_pairs={{0,24},{2,26},{4,28},{6,30},{8,0},{10,2},{12,4},{14,6},{16,8},{18,... | collective-permute-start | bytes 1179656 | tf_op jit(solution)/shard_map/ppermute | solution.py:297
  363.8 40.3 %collective-permute-start.29 = (bf16[1,1,2,2,2,48,2304]{6,5,4,3,2,1,0:T(8,128)(2,1)}, bf16[1,1,2,2,2,48,2304]{6,5,4,3,2,1,0:T(8,128)(2,1)}, u32[]{:S(2)}, u32[]{:S(2)}) collective-permute-start(bf16[1,1,2,2,2,48,2304]{6,5,4,3,2,1,0:T(8,128)(2,1)} %slice.280), channel_id=1, source_target_pairs={{0,4},{2,6},{4,0},{6,2},{8,12},{10,14},{12,8},{14,10},{16,20},{18,... | collective-permute-start | bytes 5308424 | tf_op jit(solution)/shard_map/ppermute | solution.py:297
  436.9 29.0 %collective-permute-start.35 = (bf16[4,2,2,1,48,1536]{5,4,3,2,1,0:T(8,128)(2,1)}, bf16[4,2,2,1,48,1536]{5,4,3,2,1,0:T(8,128)(2,1)}, u32[]{:S(2)}, u32[]{:S(2)}) collective-permute-start(bf16[4,2,2,1,48,1536]{5,4,3,2,1,0:T(8,128)(2,1)} %constant_dynamic-slice_fusion.18), channel_id=1, source_target_pairs={{0,1},{1,0},{2,3},{3,2},{4,5},{5,4},{6,7},{7,6},{8,9},{9,8},{10,11... | collective-permute-start | bytes 7077896 | tf_op jit(solution)/shard_map/ppermute | solution.py:384
  437.4 118.9 %reduce-scatter.5.cloned.1.call-start = ((), (), s32[]{:S(2)}) async-start(), calls=%async_computation.7 | async-start | bytes 2949120 | tf_op jit(solution)/shard_map/reduce_scatter | solution.py:651
  439.1 15.8 %collective-permute-start.34 = (bf16[4,1,1,128,512]{4,3,2,1,0:T(8,128)(2,1)S(1)}, bf16[4,1,1,128,512]{4,3,2,1,0:T(8,128)(2,1)S(1)}, u32[]{:S(2)}, u32[]{:S(2)}) collective-permute-start(bf16[4,1,1,128,512]{4,3,2,1,0:T(8,128)(2,1)S(1)} %get-tuple-element.157), channel_id=1, source_target_pairs={{0,6},{2,4},{4,2},{6,0},{8,14},{10,12},{12,10},{14,8},{16,22},{18,... | collective-permute-start | bytes 1572872 | tf_op jit(solution)/shard_map/ppermute | solution.py:297
  439.8 24.8 %collective-permute-start.33 = (bf16[4,1,1,128,512]{4,3,2,1,0:T(8,128)(2,1)S(1)}, bf16[4,1,1,128,512]{4,3,2,1,0:T(8,128)(2,1)S(1)}, u32[]{:S(2)}, u32[]{:S(2)}) collective-permute-start(bf16[4,1,1,128,512]{4,3,2,1,0:T(8,128)(2,1)S(1)} %get-tuple-element.158), channel_id=1, source_target_pairs={{0,4},{2,6},{4,0},{6,2},{8,12},{10,14},{12,8},{14,10},{16,20},{18,... | collective-permute-start | bytes 1572872 | tf_op jit(solution)/shard_map/ppermute | solution.py:297
  441.2 23.4 %collective-permute-start.32 = (bf16[4,1,1,128,512]{4,3,2,1,0:T(8,128)(2,1)S(1)}, bf16[4,1,1,128,512]{4,3,2,1,0:T(8,128)(2,1)S(1)}, u32[]{:S(2)}, u32[]{:S(2)}) collective-permute-start(bf16[4,1,1,128,512]{4,3,2,1,0:T(8,128)(2,1)S(1)} %get-tuple-element.156), channel_id=1, source_target_pairs={{0,2},{2,0},{4,6},{6,4},{8,10},{10,8},{12,14},{14,12},{16,18},{18,... | collective-permute-start | bytes 1572872 | tf_op jit(solution)/shard_map/ppermute | solution.py:297
  469.4 21.5 %collective-permute-start.39 = (bf16[1,1,1,2,2,48,2304]{6,5,4,3,2,1,0:T(8,128)(2,1)S(1)}, bf16[1,1,1,2,2,48,2304]{6,5,4,3,2,1,0:T(8,128)(2,1)}, u32[]{:S(2)}, u32[]{:S(2)}) collective-permute-start(bf16[1,1,1,2,2,48,2304]{6,5,4,3,2,1,0:T(8,128)(2,1)S(1)} %slice.303), channel_id=1, source_target_pairs={{0,4},{2,6},{4,0},{6,2},{8,12},{10,14},{12,8},{14,10},{16,20},{18,... | collective-permute-start | bytes 2654216 | tf_op jit(solution)/shard_map/ppermute | solution.py:297
  471.5 15.0 %collective-permute-start.37 = (bf16[1,1,1,128,512]{4,3,2,1,0:T(8,128)(2,1)S(1)}, bf16[1,1,1,128,512]{4,3,2,1,0:T(8,128)(2,1)S(1)}, u32[]{:S(2)}, u32[]{:S(2)}) collective-permute-start(bf16[1,1,1,128,512]{4,3,2,1,0:T(8,128)(2,1)S(1)} %get-tuple-element.181), channel_id=1, source_target_pairs={{0,16},{2,18},{4,20},{6,22},{8,24},{10,26},{12,28},{14,30},{16,0},... | collective-permute-start | bytes 393224 | tf_op jit(solution)/shard_map/ppermute | solution.py:297
  477.1 20.6 %collective-permute-start.40 = (bf16[1,1,1,2,2,48,2304]{6,5,4,3,2,1,0:T(8,128)(2,1)S(1)}, bf16[1,1,1,2,2,48,2304]{6,5,4,3,2,1,0:T(8,128)(2,1)S(1)}, u32[]{:S(2)}, u32[]{:S(2)}) collective-permute-start(bf16[1,1,1,2,2,48,2304]{6,5,4,3,2,1,0:T(8,128)(2,1)S(1)} %slice.305), channel_id=1, source_target_pairs={{0,2},{2,0},{4,6},{6,4},{8,10},{10,8},{12,14},{14,12},{16,18},{18,... | collective-permute-start | bytes 2654216 | tf_op jit(solution)/shard_map/ppermute | solution.py:297
  509.5 17.5 %collective-permute-start.43 = (bf16[4,1,1,1,48,1536]{5,4,3,2,1,0:T(8,128)(2,1)}, bf16[4,1,1,1,48,1536]{5,4,3,2,1,0:T(8,128)(2,1)}, u32[]{:S(2)}, u32[]{:S(2)}) collective-permute-start(bf16[4,1,1,1,48,1536]{5,4,3,2,1,0:T(8,128)(2,1)} %get-tuple-element.154), channel_id=1, source_target_pairs={{0,6},{2,4},{4,2},{6,0},{8,14},{10,12},{12,10},{14,8},{16,22},{18,... | collective-permute-start | bytes 1769480 | tf_op jit(solution)/shard_map/ppermute | solution.py:297
  510.8 26.1 %collective-permute-start.42 = (bf16[4,1,1,1,48,1536]{5,4,3,2,1,0:T(8,128)(2,1)}, bf16[4,1,1,1,48,1536]{5,4,3,2,1,0:T(8,128)(2,1)}, u32[]{:S(2)}, u32[]{:S(2)}) collective-permute-start(bf16[4,1,1,1,48,1536]{5,4,3,2,1,0:T(8,128)(2,1)} %get-tuple-element.155), channel_id=1, source_target_pairs={{0,4},{2,6},{4,0},{6,2},{8,12},{10,14},{12,8},{14,10},{16,20},{18,... | collective-permute-start | bytes 1769480 | tf_op jit(solution)/shard_map/ppermute | solution.py:297
  511.5 27.1 %collective-permute-start.41 = (bf16[4,1,1,1,48,1536]{5,4,3,2,1,0:T(8,128)(2,1)}, bf16[4,1,1,1,48,1536]{5,4,3,2,1,0:T(8,128)(2,1)}, u32[]{:S(2)}, u32[]{:S(2)}) collective-permute-start(bf16[4,1,1,1,48,1536]{5,4,3,2,1,0:T(8,128)(2,1)} %get-tuple-element.153), channel_id=1, source_target_pairs={{0,2},{2,0},{4,6},{6,4},{8,10},{10,8},{12,14},{14,12},{16,18},{18,... | collective-permute-start | bytes 1769480 | tf_op jit(solution)/shard_map/ppermute | solution.py:297
  515.9 53.1 %all-to-all-start.1 = ((bf16[4,2,48,2304]{3,2,1,0:T(8,128)(2,1)}), bf16[4,2,48,2304]{3,2,1,0:T(8,128)(2,1)}, u32[]{:S(2)}, u32[]{:S(2)}) async-start(bf16[4,2,48,2304]{3,2,1,0:T(8,128)(2,1)} %pad_maximum_fusion.7), calls=%async_computation.3 | async-start | bytes 3538944 | tf_op jit(solution)/shard_map/all_to_all | solution.py:678
  522.8 30.9 %collective-permute-start.45 = (bf16[1,2,1,1,280,768]{5,4,3,2,1,0:T(8,128)(2,1)S(1)}, bf16[1,2,1,1,280,768]{5,4,3,2,1,0:T(8,128)(2,1)S(1)}, u32[]{:S(2)}, u32[]{:S(2)}) collective-permute-start(bf16[1,2,1,1,280,768]{5,4,3,2,1,0:T(8,128)(2,1)S(1)} %constant_dynamic-slice_fusion.14), channel_id=1, source_target_pairs={{0,2},{2,0},{4,6},{6,4},{8,10},{10,8},{12,14},{14,12},{16,18},{18,... | collective-permute-start | bytes 2580488 | tf_op jit(solution)/shard_map/ppermute | solution.py:297
  523.4 31.8 %collective-permute-start.46 = (bf16[1,1,2,1,280,768]{5,4,3,2,1,0:T(8,128)(2,1)S(1)}, bf16[1,1,2,1,280,768]{5,4,3,2,1,0:T(8,128)(2,1)S(1)}, u32[]{:S(2)}, u32[]{:S(2)}) collective-permute-start(bf16[1,1,2,1,280,768]{5,4,3,2,1,0:T(8,128)(2,1)S(1)} %constant_dynamic-slice_fusion.13), channel_id=1, source_target_pairs={{0,4},{2,6},{4,0},{6,2},{8,12},{10,14},{12,8},{14,10},{16,20},{18,... | collective-permute-start | bytes 2580488 | tf_op jit(solution)/shard_map/ppermute | solution.py:297
  527.0 33.9 %collective-permute-start.44 = (bf16[4,2,2,1,48,768]{5,4,3,2,1,0:T(8,128)(2,1)S(1)}, bf16[4,2,2,1,48,768]{5,4,3,2,1,0:T(8,128)(2,1)}, u32[]{:S(2)}, u32[]{:S(2)}) collective-permute-start(bf16[4,2,2,1,48,768]{5,4,3,2,1,0:T(8,128)(2,1)S(1)} %fusion.23), channel_id=1, source_target_pairs={{0,1},{1,0},{2,3},{3,2},{4,5},{5,4},{6,7},{7,6},{8,9},{9,8},{10,11... | collective-permute-start | bytes 3538952 | tf_op jit(solution)/shard_map/ppermute | solution.py:384
  569.9 16.4 %collective-permute-start.55 = (bf16[4,1,1,1,48,768]{5,4,3,2,1,0:T(8,128)(2,1)}, bf16[4,1,1,1,48,768]{5,4,3,2,1,0:T(8,128)(2,1)}, u32[]{:S(2)}, u32[]{:S(2)}) collective-permute-start(bf16[4,1,1,1,48,768]{5,4,3,2,1,0:T(8,128)(2,1)} %get-tuple-element.165), channel_id=1, source_target_pairs={{0,6},{2,4},{4,2},{6,0},{8,14},{10,12},{12,10},{14,8},{16,22},{18,... | collective-permute-start | bytes 884744 | tf_op jit(solution)/shard_map/ppermute | solution.py:297
  571.2 18.1 %collective-permute-start.54 = (bf16[4,1,1,1,48,768]{5,4,3,2,1,0:T(8,128)(2,1)}, bf16[4,1,1,1,48,768]{5,4,3,2,1,0:T(8,128)(2,1)}, u32[]{:S(2)}, u32[]{:S(2)}) collective-permute-start(bf16[4,1,1,1,48,768]{5,4,3,2,1,0:T(8,128)(2,1)} %get-tuple-element.166), channel_id=1, source_target_pairs={{0,4},{2,6},{4,0},{6,2},{8,12},{10,14},{12,8},{14,10},{16,20},{18,... | collective-permute-start | bytes 884744 | tf_op jit(solution)/shard_map/ppermute | solution.py:297
  571.9 17.9 %collective-permute-start.53 = (bf16[4,1,1,1,48,768]{5,4,3,2,1,0:T(8,128)(2,1)}, bf16[4,1,1,1,48,768]{5,4,3,2,1,0:T(8,128)(2,1)}, u32[]{:S(2)}, u32[]{:S(2)}) collective-permute-start(bf16[4,1,1,1,48,768]{5,4,3,2,1,0:T(8,128)(2,1)} %get-tuple-element.164), channel_id=1, source_target_pairs={{0,2},{2,0},{4,6},{6,4},{8,10},{10,8},{12,14},{14,12},{16,18},{18,... | collective-permute-start | bytes 884744 | tf_op jit(solution)/shard_map/ppermute | solution.py:297
  574.2 18.3 %collective-permute-start.52 = (bf16[1,1,1,1,48,1536]{5,4,3,2,1,0:T(8,128)(2,1)}, bf16[1,1,1,1,48,1536]{5,4,3,2,1,0:T(8,128)(2,1)}, u32[]{:S(2)}, u32[]{:S(2)}) collective-permute-start(bf16[1,1,1,1,48,1536]{5,4,3,2,1,0:T(8,128)(2,1)} %get-tuple-element.174), channel_id=1, source_target_pairs={{0,8},{2,10},{4,12},{6,14},{8,16},{10,18},{12,20},{14,22},{16,24},... | collective-permute-start | bytes 442376 | tf_op jit(solution)/shard_map/ppermute | solution.py:297
  574.4 18.6 %collective-permute-start.51 = (bf16[1,1,1,1,48,1536]{5,4,3,2,1,0:T(8,128)(2,1)}, bf16[1,1,1,1,48,1536]{5,4,3,2,1,0:T(8,128)(2,1)}, u32[]{:S(2)}, u32[]{:S(2)}) collective-permute-start(bf16[1,1,1,1,48,1536]{5,4,3,2,1,0:T(8,128)(2,1)} %get-tuple-element.175), channel_id=1, source_target_pairs={{0,16},{2,18},{4,20},{6,22},{8,24},{10,26},{12,28},{14,30},{16,0},... | collective-permute-start | bytes 442376 | tf_op jit(solution)/shard_map/ppermute | solution.py:297
  (81 other events, 643.7 us)
Sparse Core Ops, SparseCore 0:
  11.5 98.2 all-gather.2
  112.7 88.2 all-gather.4
  437.5 33.1 reduce-scatter.2
  475.9 46.0 reduce-scatter.4
